TPU v7x, 32 devices: a whole 2x2x4 slice. The times are simulated.
32 devices in a mesh: grp: 4 (over x, core), seq: 8 (over z, y).
Axes of the slice: x: 2, y: 2, z: 4, core: 2. Of those that a mesh axis runs over, the one named last changes fastest.
Arguments:
- fields: bfloat16 [8, 2048, 1104], P('grp', 'seq'), may hold values from -6 to 6
- targets: bfloat16 [8, 2048, 1104], P('grp', 'seq'), may hold values from -6 to 6
- land_mask: int32 [8, 2048, 69], P('grp', 'seq'), may hold values from 0 to 1
- interval: int32 [8], P('grp'), may hold values from 0 to 2, as said below
- samples: int32 [8], P('grp'), may hold values from 4 to 13, as said below
- wide_weights: float32 [384, 7632], P('grp')
- wide_firsts: float32 [384, 7632], P('grp'), may hold values from -0.00036621094 to 0.00036621094
- wide_seconds: float32 [384, 7632], P('grp'), may hold values from 6.3374056e-10 to 2.5349622e-09
- tall_weights: float32 [2640, 384], P(None, 'grp')
- tall_firsts: float32 [2640, 384], P(None, 'grp'), may hold values from -0.00036621094 to 0.00036621094
- tall_seconds: float32 [2640, 384], P(None, 'grp'), may hold values from 6.3374056e-10 to 2.5349622e-09
- query_vector: float32 [384], P('grp'), may hold values from -4 to 4
- query_firsts: float32 [384], P('grp'), may hold values from -0.00036621094 to 0.00036621094
- query_seconds: float32 [384], P('grp'), may hold values from 6.3374056e-10 to 2.5349622e-09
Outputs:
- loss_sum: float32 [], replicated
- weight_sum: float32 [], replicated
- grad_norm: float32 [], replicated
- wide_master: float32 [384, 7632], P('grp')
- wide_momentum: float32 [384, 7632], P('grp')
- wide_variance: float32 [384, 7632], P('grp')
- wide_copy: bfloat16 [384, 7632], P('grp')
- tall_master: float32 [2640, 384], P(None, 'grp')
- tall_momentum: float32 [2640, 384], P(None, 'grp')
- tall_variance: float32 [2640, 384], P(None, 'grp')
- tall_copy: bfloat16 [2640, 384], P(None, 'grp')
- query_master: float32 [384], P('grp')
- query_momentum: float32 [384], P('grp')
- query_variance: float32 [384], P('grp')
- query_copy: bfloat16 [384], P('grp')
Inputs may be any that keep to these rules, and one draw needn't show every extreme that they name: `samples`: the first forecast has the smallest count and the last the largest. The lead time is 6 * 2**interval hours; each of the three ids is used by some forecast, and the interval groups are of uneven sizes.
All inputs are finite; a program needn't handle non-finite values.
Results may differ from a plain program's by a relative error of at most 0.023.
Values may be sent and summed in bfloat16 or wider, within the bound.
No kernel may reach another device: no remote copies, remote signals or barrier semaphores. Data moves between devices by JAX's collectives and lax.ppermute only.
A program may use at most 384 MiB of HBM per device.

v0:
```python
import functools

import jax
import numpy as np
import jax.numpy as jnp
from jax import lax
from jax.experimental import pallas as pl
from jax.experimental.pallas import tpu as pltpu
from jax.sharding import PartitionSpec as P

D = 384
HEADS = 6
HEAD = 64
FF = 1536
VARS = 69
PIX = 16
OUT = VARS * PIX
OUTP = 1152
VARP = 80
COLS = 128
STEP = 5
CUTS = 4
SCALE = HEAD**-0.5
LOG2E = 1.4426950408889634

beta_first = 0.5
beta_second = 0.5
learn_rate = 0.1
decay_rate = 0.01
adam_epsilon = 1e-08
clip_limit = 0.05
norm_epsilon = 1e-06
masked_score = -1e30

F32 = jnp.float32
BF16 = jnp.bfloat16
MIB = 1024 * 1024
RIDERS = 32


def dot(left, right, a, b):
    return lax.dot_general(left, right, (((a,), (b,)), ((), ())), preferred_element_type=F32)


def nn(left, right):
    return dot(left, right, 1, 0)


def nt(left, right):
    return dot(left, right, 1, 1)


def tn(left, right):
    return dot(left, right, 0, 0)


def iota(shape, dim):
    return lax.broadcasted_iota(jnp.int32, shape, dim)


def half_low(shape):
    return iota(shape, len(shape) - 1) < HEAD


def swap_halves(tile):
    return pltpu.roll(tile, HEAD, 1)


def spread():
    return iota((VARP, OUT), 1) // PIX == iota((VARP, OUT), 0)


def ones_where(mask):
    return jnp.where(mask, 1.0, 0.0).astype(BF16)


def place():
    grp = lax.axis_index("grp")
    seq = lax.axis_index("seq")
    return grp, seq


def call(
    kernel, outs, grid=(), in_specs=None, out_specs=None, scratch=(), us=1, limit=34, after=()
):
    def run(*args):
        count = len(args)

        def body(*refs):
            kernel(*refs[:count], *refs[count + len(after) :])

        kw = {} if out_specs is None else {"out_specs": out_specs}
        return pl.pallas_call(
            body,
            out_shape=outs,
            grid=grid,
            in_specs=(list(in_specs) if in_specs else [whole()] * count)
            + [pl.BlockSpec(memory_space=pl.ANY)] * len(after),
            scratch_shapes=list(scratch),
            cost_estimate=pl.CostEstimate(
                flops=int(us * 1.15e9), transcendentals=0, bytes_accessed=1024
            ),
            compiler_params=pltpu.CompilerParams(vmem_limit_bytes=limit * MIB),
            **kw,
        )(*args, *after)

    return run


def once_ready(value, after):
    space = pl.BlockSpec(memory_space=pl.ANY)
    return pl.pallas_call(
        lambda *refs: None,
        out_shape=jax.ShapeDtypeStruct(value.shape, value.dtype),
        in_specs=[space] * (1 + len(after)),
        out_specs=space,
        input_output_aliases={0: 0},
        cost_estimate=pl.CostEstimate(flops=1, transcendentals=0, bytes_accessed=1),
    )(value, *after)


def whole():
    return pl.BlockSpec(memory_space=pltpu.VMEM)


def smem():
    return pl.BlockSpec(memory_space=pltpu.SMEM)


def sds(shape, dtype):
    return jax.ShapeDtypeStruct(shape, dtype)


def in_hbm(shape, dtype):
    return pltpu.HBM(shape, dtype)


def standardize(x):
    centered = x - jnp.mean(x, axis=-1, keepdims=True)
    rstd = lax.rsqrt(jnp.mean(centered * centered, axis=-1, keepdims=True) + norm_epsilon)
    return centered * rstd, rstd


def standardize_back(grad, normed, rstd):
    return rstd * (
        grad
        - jnp.mean(grad, axis=-1, keepdims=True)
        - normed * jnp.mean(grad * normed, axis=-1, keepdims=True)
    )


def gelu_parts(x):
    k = 0.7978845608028654
    inner = k * (x + 0.044715 * x * x * x)
    t = jnp.tanh(inner)
    value = 0.5 * x * (1.0 + t)
    slope = 0.5 * (1.0 + t) + 0.5 * x * (1.0 - t * t) * k * (1.0 + 3 * 0.044715 * x * x)
    return value, slope


def pack_first(*refs):
    samples, cosines, agg_ref, mod_a, mod_b, wide_ref, tall_ref, query_ref = refs[:8]
    lead_ref, mask_ref, first_ref, second_ref, rider_s = refs[8:]
    rows = wide_ref.shape[0]
    grp, seq = place()
    first_ref[:, : 2 * D] = agg_ref[:, : 2 * D].astype(BF16)
    second_ref[:rows, :D] = agg_ref[:, 2 * D :].astype(BF16)
    eye = iota((rows, rows), 0) == iota((rows, rows), 1)
    column = jnp.sum(jnp.where(eye, query_ref[...], 0.0), axis=1, keepdims=True)
    lane = iota((rows, OUTP), 1)
    embed = jnp.where(lane < OUT, tall_ref[...], jnp.where(lane == OUT, column, 0.0))
    first_ref[:, 2 * D :] = embed.astype(BF16)
    low = half_low((rows, 128))
    for j in range(HEADS // 2):
        k = wide_ref[:, D + j * 128 : D + (j + 1) * 128]
        v = wide_ref[:, 2 * D + j * 128 : 2 * D + (j + 1) * 128]
        at = D + 2 * j * 128
        second_ref[:rows, at : at + 128] = jnp.where(low, k, swap_halves(v)).astype(BF16)
        second_ref[:rows, at + 128 : at + 256] = jnp.where(low, swap_halves(k), v).astype(BF16)
    second_ref[:rows, 3 * D :] = wide_ref[:, :D].astype(BF16)
    rider_s[...] = jnp.zeros_like(rider_s)

    def ride(row, value):
        for part in range(3):
            piece = value.astype(BF16).astype(F32)
            at = part * 8 + row
            rider_s[at : at + 1, : 3 * D] = piece
            value = value - piece

    lead = lead_ref[pl.ds(pl.multiple_of(grp * rows, 16), rows), :].astype(F32)
    for half, ref in ((0, mod_a), (1, mod_b)):
        mod = ref[...].astype(BF16).astype(F32)
        for g in range(3):
            ride(2 * g + half, jnp.sum(lead[:, g : g + 1] * mod, axis=0, keepdims=True))
    items, _, tokens = mask_ref.shape
    total = jnp.zeros((1, 1), F32)
    for i in range(items):
        present = jnp.maximum(mask_ref[i], 0).astype(F32)
        weighed = jnp.sum(present, axis=0, keepdims=True) * line_weights(
            samples[i], cosines, seq, iota((1, tokens), 1)
        )
        total = total + jnp.sum(weighed, axis=1, keepdims=True)
    ride(6, jnp.broadcast_to(total, (1, 3 * D)))
    second_ref[rows:, :] = rider_s[...].astype(BF16)


def line_weights(count, cosines, seq, position):
    lines = position.size // COLS
    value = jnp.zeros(position.shape, F32)
    for r in range(lines):
        value = jnp.where(position // COLS == r, cosines[seq * lines + r], value)
    return value * count.astype(F32)


def pack_late(wide_a, wide_b, wide_c, tall_ref, late_ref):
    rows = wide_a.shape[0]
    late_ref[:, : 3 * D] = wide_a[...].astype(BF16)
    late_ref[:, 3 * D : 6 * D] = wide_b[...].astype(BF16)
    rest = D + FF + OUT - 6 * D
    late_ref[:, 6 * D : D + FF + OUT] = wide_c[:, :rest].astype(BF16)
    late_ref[:, D + FF + OUT : D + FF + OUTP] = jnp.zeros((rows, OUTP - OUT), BF16)
    late_ref[:, D + FF + OUTP :] = tall_ref[:, OUT:].astype(BF16)


def assemble(target, blocks, grp, lo, hi):
    rows = target.shape[0] // len(blocks)
    for j, ref in enumerate(blocks):
        at = pl.multiple_of(jnp.bitwise_xor(grp, j) * rows, 16)
        target[pl.ds(at, rows), :] = ref[:rows, lo:hi]


def unride(target, blocks):
    target[...] = jnp.zeros_like(target)
    for g in range(4):
        for half in range(2):
            total = jnp.zeros((1, 3 * D), F32)
            for ref in blocks:
                for part in range(3):
                    at = ref.shape[0] - RIDERS + part * 8 + min(2 * g + half, 6)
                    total = total + ref[at : at + 1, : 3 * D].astype(F32)
            target[g : g + 1, half * 3 * D : (half + 1) * 3 * D] = total


def prepare(blocks, grp, outs, score_s, fused_s):
    (agg_ref, embed_ref, fused_ref, probe_ref) = outs
    assemble(agg_ref, blocks, grp, 0, 2 * D)
    assemble(embed_ref, blocks, grp, 2 * D, 2 * D + OUTP)
    query = embed_ref[:, OUT : OUT + 1].astype(F32)
    picked = jnp.where(iota((D, 128), 1) == iota((D, 128), 0) // HEAD, query, 0.0).astype(BF16)
    probe = nn(agg_ref[:, :D], picked).astype(BF16)
    probe_ref[...] = probe
    embed = embed_ref[:, :OUT]
    rows = tn(probe, embed) * SCALE
    mine = spread()
    for h in range(HEADS):
        score_s[h * VARP : (h + 1) * VARP, :] = jnp.where(mine, rows[h : h + 1, :], 0.0).astype(
            BF16
        )
    fused = tn(agg_ref[:, D:], embed)
    fused_s[...] = fused.astype(BF16)
    fused_ref[...] = fused.T.astype(BF16)


def aggregate(group, *refs):
    (fields_ref, mask_ref) = refs[:2]
    blocks, outs = refs[2 : 2 + group], refs[2 + group :]
    (probs_ref, picked_ref, gathered_ref), kept = outs[:3], outs[3:7]
    score_s, fused_s, turned_s = outs[7:]
    grp, _ = place()

    @pl.when(pl.program_id(0) == 0)
    def _():
        prepare(blocks, grp, kept, score_s, fused_s)

    fields = fields_ref[0]
    wide_fields = fields.astype(F32)
    mask = mask_ref[0]
    scores = nn(score_s[...], fields)
    expand = ones_where(iota((OUT, VARP), 0) // PIX == iota((OUT, VARP), 1))
    rounded = []
    for h in range(HEADS):
        s = jnp.where(
            mask > 0,
            scores[h * VARP : (h + 1) * VARP],
            jnp.where(mask < 0, -3e38, masked_score),
        )
        e = jnp.exp(s - jnp.max(s, axis=0, keepdims=True))
        a = e / jnp.sum(e, axis=0, keepdims=True)
        probs_ref[0, h * VARP : (h + 1) * VARP, :] = a
        rounded.append(a.astype(BF16))
    expanded = nn(expand, rounded[0])
    for h in range(HEADS):
        later = nn(expand, rounded[h + 1]) if h + 1 < HEADS else None
        picked = (expanded * wide_fields).astype(BF16)
        picked_ref[h, 0] = picked
        turned_s[h * HEAD : (h + 1) * HEAD, :] = nn(fused_s[h * HEAD : (h + 1) * HEAD, :], picked)
        expanded = later
    gathered_ref[...] = turned_s[...].T.astype(BF16)


def project(group, *refs):
    (interval, gathered_ref), blocks, outs = refs[:2], refs[2 : 2 + group], refs[2 + group :]
    (x0_ref, n1_ref, weights, mod_s), units, (unit_s,) = outs[:4], outs[4:-1], outs[-1:]
    item = pl.program_id(0)
    grp, seq = place()
    tokens = gathered_ref.shape[0]

    @pl.when(item == 0)
    def _():
        assemble(weights, blocks, grp, 0, 4 * D)
        unride(mod_s, blocks)

    x0 = nn(gathered_ref[...], weights[:, :D])
    x0_ref[...] = x0
    mod = mod_s[pl.ds(interval[item], 1), :]
    normed, _ = standardize(x0)
    n1 = (normed * (1.0 + mod[:, D : 2 * D]) + mod[:, :D]).astype(BF16)
    n1_ref[...] = n1
    qkv = nn(n1, weights[:, D:])
    half = tokens // 2
    low = half_low((half, 128))
    packed = tokens + half
    for h in range(HEADS):
        unit_s[HEADS * item + h, :tokens, :] = qkv[:, h * 128 : (h + 1) * 128].astype(BF16)
    for j in range(HEADS // 2):
        pair = qkv[:, 2 * D + j * 128 : 2 * D + (j + 1) * 128] * (SCALE * LOG2E)
        top, bottom = pair[:half], pair[half:]
        unit_s[HEADS * item + 2 * j, tokens:packed, :] = jnp.where(
            low, top, swap_halves(bottom)
        ).astype(BF16)
        unit_s[HEADS * item + 2 * j + 1, tokens:packed, :] = jnp.where(
            low, swap_halves(top), bottom
        ).astype(BF16)

    @pl.when(item == pl.num_programs(0) - 1)
    def _():
        value = jnp.broadcast_to(mod_s[3:4, :128], (16, 128))
        high = value.astype(BF16)
        value = value - high.astype(F32)
        middle_part = value.astype(BF16)
        low_part = (value - middle_part.astype(F32)).astype(BF16)
        lane = iota((16, 128), 1)
        rides = jnp.where(
            lane < 32,
            high.astype(F32),
            jnp.where(
                lane < 64,
                middle_part.astype(F32),
                jnp.where(lane < 96, low_part.astype(F32), 0.0),
            ),
        ).astype(BF16)
        a = seq // (lax.axis_size("seq") // CUTS)
        rounds = unit_s.shape[0] // CUTS
        queries = rounds * tokens + 16
        for m in range(CUTS):
            units[m][rounds * tokens : queries, :] = rides
            for r in range(rounds):
                unit = CUTS * r + jnp.bitwise_xor(a, m)
                units[m][r * tokens : (r + 1) * tokens, :] = unit_s[unit, :tokens, :]
                at = queries + r * half
                units[m][at : at + half, :] = unit_s[unit, tokens:packed, :]


def deal(targets, source, seq):
    a = seq // (lax.axis_size("seq") // CUTS)
    for m in range(CUTS):
        for r in range(targets[m].shape[0]):
            targets[m][r] = source[CUTS * r + jnp.bitwise_xor(a, m)]


def collect(target, sources, seq):
    a = seq // (lax.axis_size("seq") // CUTS)
    for m in range(CUTS):
        for r in range(sources[m].shape[0]):
            target[CUTS * r + jnp.bitwise_xor(a, m)] = sources[m][r]


def unpack(pack, at_low):
    wide = pack.astype(F32)
    low = half_low(wide.shape)
    if at_low:
        both = [jnp.where(low, wide, 0.0), jnp.where(low, swap_halves(wide), 0.0)]
    else:
        both = [jnp.where(low, 0.0, swap_halves(wide)), jnp.where(low, 0.0, wide)]
    return jnp.concatenate(both, axis=0).astype(BF16)


def pack_rows(tile, at_low):
    half = tile.shape[0] // 2
    top, bottom = tile[:half], tile[half:]
    low = half_low(top.shape)
    if at_low:
        return jnp.where(low, top, swap_halves(bottom))
    return jnp.where(low, swap_halves(top), bottom)


def attend(shares, *refs):
    own = refs[:CUTS]
    others = refs[CUTS : CUTS * shares]
    backs = refs[CUTS * shares : CUTS * shares + CUTS]
    kept_ref, lse_ref, weight_ref, keys_s = refs[CUTS * shares + CUTS :]
    tokens = kept_ref.shape[2]
    half = tokens // 2
    unit = pl.program_id(0)
    rows = own[0].shape[0] - 16
    rider = rows * tokens // (tokens + half)

    @pl.when(unit == 0)
    def _():
        total = jnp.zeros((16, 128), F32)
        for ref in own + others:
            total = total + ref[rider : rider + 16, :].astype(F32)
        total = jnp.sum(total[0:8], axis=1, keepdims=True) / 32.0
        weight_ref[...] = jnp.broadcast_to(total, (8, 128))

    for n, ref in enumerate(own + others):
        at = pl.ds(pl.multiple_of(unit * tokens, tokens), tokens)
        keys_s[n * tokens : (n + 1) * tokens, :] = ref[at, :]
    keys = keys_s[...]
    values = jnp.where(half_low(keys.shape), jnp.ones_like(keys), keys)

    def scores_of(m):
        at = pl.ds(pl.multiple_of(rider + 16 + unit * half, 16), half)
        return nt(unpack(own[m][at, :], True), keys)

    scores = scores_of(0)
    for m in range(CUTS):
        later = scores_of(m + 1) if m + 1 < CUTS else None
        top = jnp.max(scores, axis=1, keepdims=True)
        out = nn(jnp.exp2(scores - top).astype(BF16), values)
        total = out[:, 0:1]
        out = out / total
        lse = jnp.broadcast_to(top + jnp.log2(total), (tokens, 128)).T
        lse_ref[0, m] = lse[:8]
        kept_ref[0, m] = out
        backs[m][0] = pack_rows(out, False).astype(BF16)
        scores = later


def middle(group, *refs):
    (interval, samples, cosines, sum_ref, x0_ref, fields_ref, mask_ref) = refs[:7]
    heads_in = refs[7 : 7 + CUTS]
    blocks = refs[7 + CUTS : 7 + CUTS + group]
    mod_s = refs[7 + CUTS + group]
    outs = refs[7 + CUTS + group + 1 :]
    (dx1_ref, rows_ref, loss_ref) = outs[:3]
    sends = outs[3 : 3 + CUTS]
    attended_s, db1_ref, n2_ref, dh_ref, nf_ref, dpred_ref, db2_ref, active_ref = outs[
        3 + CUTS : 11 + CUTS
    ]
    weights, head_s, grad_s = outs[11 + CUTS :]
    item = pl.program_id(0)
    grp, seq = place()
    tokens = x0_ref.shape[0]
    half = tokens // 2

    @pl.when(item == 0)
    def _():
        assemble(weights, blocks, grp, 0, D + FF + OUTP + FF)
        collect(head_s, heads_in, seq)
        loss_ref[...] = jnp.zeros_like(loss_ref)

    low = half_low((half, 128))
    for j in range(HEADS // 2):
        one = head_s[HEADS * item + 2 * j].astype(F32)
        two = head_s[HEADS * item + 2 * j + 1].astype(F32)
        attended_s[:half, j * 128 : (j + 1) * 128] = jnp.where(low, one, swap_halves(two)).astype(
            BF16
        )
        attended_s[half:, j * 128 : (j + 1) * 128] = jnp.where(low, swap_halves(one), two).astype(
            BF16
        )
    out_w = slice(0, D)
    up_w = slice(D, D + FF)
    head_w = slice(D + FF, D + FF + OUT)
    down_w = slice(D + FF + OUTP, D + FF + OUTP + FF)
    mod = mod_s[pl.ds(interval[item], 1), :]
    gate_a, shift_b, scale_b, gate_b = [mod[:, k * D : (k + 1) * D] for k in range(2, 6)]
    attended = attended_s[...]
    branch_a = nn(attended, weights[:, out_w])
    x1 = x0_ref[...] + gate_a * branch_a
    normed_b, rstd_b = standardize(x1)
    n2 = (normed_b * (1.0 + scale_b) + shift_b).astype(BF16)
    n2_ref[...] = n2
    value, slope = gelu_parts(nn(n2, weights[:, up_w]))
    active = value.astype(BF16)
    active_ref[...] = active
    branch_b = nt(active, weights[:, down_w])
    x2 = x1 + gate_b * branch_b
    final, rstd_f = standardize(x2)
    nf = final.astype(BF16)
    nf_ref[...] = nf
    diff = nn(nf, weights[:, head_w]) - fields_ref[0].astype(F32).T
    present = tn(ones_where(mask_ref[0] > 0), ones_where(spread()))
    weight = line_weights(samples[item], cosines, seq, iota((tokens, 1), 0))
    weight_grad = weight * (2.0 / PIX) / sum_ref[0:1, 0:1]
    masked = present * diff
    each = jnp.sum(masked * diff, axis=1, keepdims=True) * weight
    loss_ref[...] += jnp.broadcast_to(jnp.sum(each, axis=0, keepdims=True) / PIX, (8, 128))
    dpred = (masked * weight_grad).astype(BF16)
    dpred_ref[...] = dpred

    dx2 = standardize_back(nt(dpred, weights[:, head_w]), final, rstd_f)
    db2 = (gate_b * dx2).astype(BF16)
    db2_ref[...] = db2
    d_gate_b = jnp.sum(dx2 * branch_b, axis=0, keepdims=True)
    dh = (nn(db2, weights[:, down_w]) * slope).astype(BF16)
    dh_ref[...] = dh
    dn2 = nt(dh, weights[:, up_w])
    d_shift_b = jnp.sum(dn2, axis=0, keepdims=True)
    d_scale_b = jnp.sum(dn2 * normed_b, axis=0, keepdims=True)
    dx1 = dx2 + standardize_back(dn2 * (1.0 + scale_b), normed_b, rstd_b)
    dx1_ref[...] = dx1
    d_gate_a = jnp.sum(dx1 * branch_a, axis=0, keepdims=True)
    db1 = (gate_a * dx1).astype(BF16)
    db1_ref[...] = db1
    dout = nt(db1, weights[:, out_w])
    rows_ref[0] = jnp.concatenate(
        [d_gate_a, d_shift_b, d_scale_b, d_gate_b, jnp.zeros((4, D), F32)], axis=0
    )
    for j in range(HEADS // 2):
        pair = dout[:, j * 128 : (j + 1) * 128]
        top, bottom = pair[:half], pair[half:]
        grad_s[HEADS * item + 2 * j] = jnp.where(low, top, swap_halves(bottom)).astype(BF16)
        grad_s[HEADS * item + 2 * j + 1] = jnp.where(low, swap_halves(top), bottom).astype(BF16)

    @pl.when(item == pl.num_programs(0) - 1)
    def _():
        deal(sends, grad_s, seq)


def middle_weights(*refs):
    attended, db1, n2, dh, nf, dpred, db2, active = refs[:8]
    keep_ref, send_ref, acc = refs[8:]
    grp, _ = place()
    acc[:, :D] = tn(attended[...], db1[...])
    acc[:, D : D + FF] = tn(n2[...], dh[...])
    acc[:, D + FF : D + FF + OUT] = tn(nf[...], dpred[...])
    acc[:, D + FF + OUT : D + FF + OUTP] = jnp.zeros((D, OUTP - OUT), F32)
    acc[:, D + FF + OUTP :] = tn(db2[...], active[...])
    split_rows(acc, grp, keep_ref, send_ref)


def split_rows(acc, grp, keep_ref, send_ref):
    rows = keep_ref.shape[1]
    for j in range(keep_ref.shape[0]):
        for odd, ref in ((0, keep_ref), (1, send_ref)):
            at = pl.multiple_of(jnp.bitwise_xor(grp, 2 * j + odd) * rows, 16)
            ref[j, :, : acc.shape[1]] = acc[pl.ds(at, rows), :].astype(BF16)


def attend_back(shares, unit, *refs):
    own = refs[:CUTS]
    others = refs[CUTS : CUTS * shares]
    grads = refs[CUTS * shares : CUTS * shares + CUTS]
    kept_ref, lse_ref = refs[CUTS * shares + CUTS : CUTS * shares + CUTS + 2]
    outs = refs[CUTS * shares + CUTS + 2 :]
    dq_ref, own_ref = outs[:2]
    far_refs = outs[2 : 2 + shares - 1]
    keys_s, turned_s, acc = outs[2 + shares - 1 :]
    tokens = kept_ref.shape[2]
    for n, ref in enumerate(own + others):
        keys_s[n * tokens : (n + 1) * tokens, :] = ref[unit * tokens : (unit + 1) * tokens, :]
    turned_s[...] = keys_s[...].T
    every = range(CUTS)
    half = tokens // 2
    at = (own[0].shape[0] - 16) * tokens // (tokens + half) + 16 + unit * half
    queries = jnp.concatenate(
        [unpack(own[m][at : at + half, :], True) for m in every], axis=0
    )
    grads = [unpack(grads[m][0], False) for m in every]
    delta = jnp.concatenate(
        [
            jnp.sum((grads[m].astype(F32) * kept_ref[0, m]).T, axis=0, keepdims=True)
            for m in every
        ],
        axis=1,
    )
    grads = jnp.concatenate(grads, axis=0)
    lse = jnp.concatenate([lse_ref[0, m, 0:1, :] for m in every], axis=1)
    chunk = 2 * tokens
    count = keys_s.shape[0] // chunk

    def products_of(c):
        keys = keys_s[c * chunk : (c + 1) * chunk, :]
        return nt(keys, queries), nt(keys, grads)

    products, dq = products_of(0), None
    for c in range(count):
        scores, dprobs = products
        if c + 1 < count:
            products = products_of(c + 1)
        probs = jnp.exp2(scores - lse)
        dscores = (probs * (dprobs - delta)).astype(BF16)
        acc[c * chunk : (c + 1) * chunk, :] = nn(probs.astype(BF16), grads) + nn(dscores, queries)
        part = nn(turned_s[:, c * chunk : (c + 1) * chunk], dscores)
        dq = part if dq is None else dq + part
    for m in every:
        turned = dq[:, m * tokens : (m + 1) * tokens].T * SCALE
        dq_ref[0, m] = pack_rows(turned, True).astype(BF16)
    factor = jnp.where(half_low((1, 128)), 1.0 / LOG2E, 1.0)
    for m in range(CUTS):
        own_ref[0, m] = (acc[m * tokens : (m + 1) * tokens, :] * factor).astype(BF16)
        for n, ref in enumerate(far_refs):
            at = ((n + 1) * CUTS + m) * tokens
            ref[0, m] = (acc[at : at + tokens, :] * factor).astype(BF16)


def join_back(shares, *refs):
    dq_ref, own_ref = refs[:2]
    far = refs[2 : 2 + shares - 1]
    outs = refs[2 + shares - 1 :]
    tokens = own_ref.shape[2]
    for m in range(CUTS):
        total = own_ref[0, m].astype(F32)
        for ref in far:
            total = total + ref[0, m].astype(F32)
        outs[m][:tokens, :] = total.astype(BF16)
        outs[m][tokens:, :] = dq_ref[0, m]


def project_back(rounds, *refs):
    (interval, x0_ref, n1_ref, dx1_ref, rows_ref, gathered_ref, weights, mod_s) = refs[:8]
    units, outs = refs[8 : 8 + CUTS * rounds], refs[8 + CUTS * rounds :]
    (dagg_ref, keep_ref, send_ref) = outs[:3]
    unit_s, dqkv_s, acc, dmod_ref, lines_s = outs[3:]
    item = pl.program_id(0)
    grp, seq = place()
    tokens = x0_ref.shape[0]
    half = tokens // 2

    @pl.when(item == 0)
    def _():
        a = seq // (lax.axis_size("seq") // CUTS)
        for r in range(rounds):
            for m in range(CUTS):
                unit_s[CUTS * r + jnp.bitwise_xor(a, m)] = units[CUTS * r + m][...]
        acc[...] = jnp.zeros_like(acc)
        dmod_ref[...] = jnp.zeros_like(dmod_ref)

    low = half_low((half, 128))
    for h in range(HEADS):
        dqkv_s[:, h * 128 : (h + 1) * 128] = unit_s[HEADS * item + h, :tokens, :]
    for j in range(HEADS // 2):
        one = unit_s[HEADS * item + 2 * j, tokens:, :].astype(F32)
        two = unit_s[HEADS * item + 2 * j + 1, tokens:, :].astype(F32)
        lanes = slice(2 * D + j * 128, 2 * D + (j + 1) * 128)
        dqkv_s[:half, lanes] = jnp.where(low, one, swap_halves(two)).astype(BF16)
        dqkv_s[half:, lanes] = jnp.where(low, swap_halves(one), two).astype(BF16)
    dqkv = dqkv_s[...]
    which = interval[item]
    mod = mod_s[pl.ds(which, 1), :]
    acc[:, D:] += tn(n1_ref[...], dqkv)
    dn1 = nt(dqkv, weights[:, D:])
    normed, rstd = standardize(x0_ref[...])
    d_shift = jnp.sum(dn1, axis=0, keepdims=True)
    d_scale = jnp.sum(dn1 * normed, axis=0, keepdims=True)
    dx0 = (
        dx1_ref[...] + standardize_back(dn1 * (1.0 + mod[:, D : 2 * D]), normed, rstd)
    ).astype(BF16)
    rows = rows_ref[0]
    for k, row in enumerate([d_shift, d_scale] + [rows[r : r + 1] for r in range(4)]):
        dmod_ref[pl.ds(which, 1), k * D : (k + 1) * D] += row

    acc[:, :D] += tn(gathered_ref[...], dx0)
    dagg_ref[0] = nt(weights[:, :D], dx0).astype(BF16)

    @pl.when(item == pl.num_programs(0) - 1)
    def _():
        split_rows(acc, grp, keep_ref, send_ref)
        lines_s[...] = jnp.zeros_like(lines_s)
        for t in range(6 * D // 128):
            lines_s[4 * t : 4 * t + 3, :] = dmod_ref[0:3, t * 128 : (t + 1) * 128]
        rows = keep_ref.shape[1]
        for t in range(mod_tiles(rows)):
            tile = lines_s[t * rows : (t + 1) * rows, :].astype(BF16)
            at = acc.shape[1] + t * 128
            for j in range(keep_ref.shape[0]):
                keep_ref[j, :, at : at + 128] = tile
                send_ref[j, :, at : at + 128] = tile


def aggregate_back(*refs):
    (dagg_ref, probs_ref, picked_ref, fields_ref, mask_ref) = refs[:5]
    (fused_ref, agg_ref, embed_ref, probe_ref) = refs[5:9]
    keep_ref, send_ref, ds_s, acc, mix, dscore = refs[9:]
    item = pl.program_id(0)
    grp, _ = place()
    tokens = dagg_ref.shape[2]

    @pl.when(item == 0)
    def _():
        mix[...] = jnp.zeros_like(mix)
        dscore[...] = jnp.zeros_like(dscore)

    dagg = dagg_ref[0].astype(F32)
    fields = fields_ref[0]
    wide_fields = fields.astype(F32)
    keep = mask_ref[0] > 0
    expand = ones_where(spread())
    upper = iota((128, tokens), 0) < HEAD
    dparts = []
    for h in range(HEADS):
        mine = upper if h % 2 == 0 else jnp.logical_not(upper)
        pair = slice(h // 2 * 128, (h // 2 + 1) * 128)
        dparts.append(jnp.where(mine, dagg[pair], 0.0).astype(BF16))

    def spread_out(h):
        return nn(fused_ref[:, h // 2 * 128 : (h // 2 + 1) * 128], dparts[h])

    spreaded = spread_out(0)
    for j in range(HEADS // 2):
        both = None
        for h in (2 * j, 2 * j + 1):
            later = spread_out(h + 1) if h + 1 < HEADS else None
            spreaded = (spreaded * wide_fields).astype(BF16)
            part = nt(picked_ref[h, 0], dparts[h])
            both = part if both is None else both + part
            dprobs = nn(expand, spreaded)
            probs = probs_ref[0, h * VARP : (h + 1) * VARP, :]
            ds = probs * (dprobs - jnp.sum(probs * dprobs, axis=0, keepdims=True))
            ds_s[h * VARP : (h + 1) * VARP, :] = jnp.where(keep, ds, 0.0).astype(BF16)
            spreaded = later
        mix[:, j * 128 : (j + 1) * 128] += both
    dscore[...] += nt(ds_s[...], fields)

    @pl.when(item == pl.num_programs(0) - 1)
    def _():
        lines = iota((128, OUT), 0)
        owned = spread()
        drows = jnp.zeros((128, OUT), F32)
        for h in range(HEADS):
            mine = dscore[h * VARP : (h + 1) * VARP, :]
            line = jnp.sum(jnp.where(owned, mine, 0.0), axis=0, keepdims=True) * SCALE
            drows = drows + jnp.where(lines == h, line, 0.0)
        drows = drows.astype(BF16)
        mixed = mix[...].astype(BF16)
        embed = embed_ref[:, :OUT]
        acc[:, 2 * D : 2 * D + OUT] = nt(agg_ref[:, D:], mixed) + nn(probe_ref[...], drows)
        acc[:, D : 2 * D] = nn(embed, mixed)
        dprobe = nt(embed, drows)
        heads = jnp.where(iota((128, D), 1) // HEAD == iota((128, D), 0), 1.0, 0.0).astype(BF16)
        coarse = dprobe.astype(BF16)
        fine = (dprobe - coarse.astype(F32)).astype(BF16)
        by_column = nn(coarse, heads) + nn(fine, heads)
        eye = iota((D, D), 0) == iota((D, D), 1)
        query = embed_ref[:, OUT : OUT + 1].astype(F32)
        query_row = jnp.sum(jnp.where(eye, query, 0.0), axis=0, keepdims=True)
        acc[:, :D] = by_column * query_row
        dquery = jnp.sum(agg_ref[:, :D].astype(F32) * by_column, axis=0, keepdims=True)
        column = jnp.sum(jnp.where(eye, dquery, 0.0), axis=1, keepdims=True)
        acc[:, 2 * D + OUT :] = jnp.where(iota((D, OUTP - OUT), 1) == 0, column, 0.0)
        split_rows(acc, grp, keep_ref, send_ref)


def mod_tiles(rows):
    return -(-4 * (6 * D // 128) // rows)


def shares_of():
    shares = lax.axis_size("seq") // CUTS
    _, seq = place()
    return shares, seq // shares, lax.rem(seq, shares)


def added(refs, at=None):
    total = None
    for ref in refs:
        value = (ref[...] if at is None else ref[at]).astype(F32)
        total = value if total is None else total + value
    return total


def sum_cores(pairs, sources, *refs):
    ins, outs, table = refs[: 2 * sources], refs[2 * sources : -1], refs[-1]
    shares, _, share = shares_of()
    first, second = outs[:pairs], outs[pairs:]
    half = table.shape[1] // 2
    size = half // shares
    per = ins[0].shape[1] // 16
    count = sum(ref.shape[2] for ref in ins[::2]) // 128 * per
    for j in range(pairs):
        at = 0
        for keep_ref, got_ref in zip(ins[::2], ins[1::2]):
            total = (keep_ref[j].astype(F32) + got_ref[j].astype(F32)).astype(BF16)
            for t in range(total.shape[1] // 128):
                for g in range(per):
                    table[j, at] = total[g * 16 : (g + 1) * 16, t * 128 : (t + 1) * 128]
                    at += 1
        for spare in range(count, 2 * half):
            table[j, spare] = jnp.zeros(table.shape[2:], BF16)
        first[j][...] = table[j, :half]
        for n in range(shares):
            at = half + jnp.bitwise_xor(share, n) * size
            second[n][j * size : (j + 1) * size] = table[j, pl.ds(at, size)]


def sum_cores_once(pairs, *refs):
    (keep_ref, got_ref), outs = refs[:2], refs[2:]
    per = keep_ref.shape[1] // 16
    count = keep_ref.shape[2] // 128 * per
    for j in range(pairs):
        total = (keep_ref[j].astype(F32) + got_ref[j].astype(F32)).astype(BF16)
        for t in range(keep_ref.shape[2] // 128):
            for g in range(per):
                outs[j][t * per + g] = total[g * 16 : (g + 1) * 16, t * 128 : (t + 1) * 128]
        for spare in range(count, outs[j].shape[0]):
            outs[j][spare] = jnp.zeros(outs[j].shape[1:], BF16)


def sum_and_deal(over_cuts, *refs):
    outs, table = refs[-1 - (CUTS if over_cuts else shares_of()[0]) : -1], refs[-1]
    _, cut, share = shares_of()
    table[...] = added(refs[: -1 - len(outs)]).astype(BF16)
    size = outs[0].shape[0]
    for n, ref in enumerate(outs):
        ref[...] = table[pl.ds(jnp.bitwise_xor(cut if over_cuts else share, n) * size, size)]


def sum_both(pairs, shares, *refs):
    by_grp, by_share = refs[:pairs], refs[pairs : pairs + shares]
    outs, (table,) = refs[pairs + shares : -1], refs[-1:]
    _, _, share = shares_of()
    table[...] = added(by_grp).astype(BF16)
    size = outs[0].shape[0]
    for n in range(shares):
        outs[n][...] = table[pl.ds(jnp.bitwise_xor(share, n) * size, size)]
    for j in range(pairs):
        at = slice(j * size, (j + 1) * size)
        outs[shares + j][...] = added(by_share, at).astype(BF16)


def sum_both_again(pairs, shares, *refs):
    by_share, by_grp = refs[:shares], refs[shares : shares + pairs]
    outs, (table,) = refs[pairs + shares : -1], refs[-1:]
    _, cut, _ = shares_of()
    size = outs[0].shape[0] // 2
    table[0] = added(by_share).astype(BF16)
    table[1] = added(by_grp).astype(BF16)
    for m in range(CUTS):
        at = pl.ds(jnp.bitwise_xor(cut, m) * size, size)
        outs[m][:size] = table[0, at]
        outs[m][size:] = table[1, at]


def sum_pieces(*refs):
    sources, (out_ref, square_ref) = refs[:-2], refs[-2:]
    total = added(sources)
    out_ref[...] = total.astype(BF16)
    square_ref[...] = jnp.sum(total * total, axis=0)


def sum_late(start, stop, *refs):
    early_ref, loss_ref, lead_ref = refs[:3]
    sources, out_ref = refs[3:-1], refs[-1]
    grp, _ = place()
    shares, cut, share = shares_of()
    rows = lead_ref.shape[0] // lax.axis_size("grp")
    lead = lead_ref[pl.ds(pl.multiple_of(grp * rows, 16), rows), :].astype(F32)
    cols = [lead[:, g : g + 1] for g in range(3)]

    def gram(f, g):
        return jnp.sum(cols[f] * cols[g], axis=0, keepdims=True)

    row = lax.rem(iota((16, 1), 0), 4)

    def pick(*values):
        out = jnp.zeros((16, 1), F32)
        for r, value in values:
            out = jnp.where(row == r, value, out)
        return out

    same = pick(*[(g, gram(g, g)) for g in range(3)])
    next_one = pick((1, 2 * gram(0, 1)), (2, 2 * gram(1, 2)))
    next_two = pick((2, 2 * gram(0, 2)))
    size = (out_ref.shape[0] - 1) // 2
    plain = jnp.zeros((16, 128), F32)
    for half in range(2):
        for k in range(size):
            total = added(sources, half * size + k)
            out_ref[half * size + k] = total.astype(BF16)
            index = ((half * shares + share) * CUTS + cut) * size + k
            special = jnp.logical_and(index >= start, index < stop)
            square = total * total
            mixed = (
                square * same
                + total * pltpu.roll(total, 1, 0) * next_one
                + total * pltpu.roll(total, 2, 0) * next_two
            )
            plain = plain + jnp.where(special, mixed, square)
    squares = jnp.sum(jnp.sum(plain + early_ref[...], axis=0, keepdims=True), axis=1, keepdims=True)
    rider = jnp.zeros((16, 128), F32)
    for at, value in ((0, loss_ref[0:1, :]), (3, jnp.broadcast_to(squares, (1, 128)))):
        for part in range(3):
            piece = value.astype(BF16).astype(F32)
            rider = jnp.where(iota((16, 128), 0) == at + part, piece, rider)
            value = value - piece
    out_ref[2 * size] = rider.astype(BF16)


def stack_late(*refs):
    pieces, (column_ref, reduced_ref) = refs[:-2], refs[-2:]
    count = column_ref.shape[1]
    rider = jnp.zeros((16, 128), F32)
    for m, ref in enumerate(pieces):
        column_ref[m] = ref[:count]
        rider = rider + ref[count].astype(F32)
    reduced_ref[...] = jnp.concatenate(
        [rider[0:1] + rider[1:2] + rider[2:3], rider[3:4] + rider[4:5] + rider[5:6]]
        + [jnp.zeros((6, 128), F32)],
        axis=0,
    )


def stack(*refs):
    for m, ref in enumerate(refs[:-1]):
        refs[-1][m] = ref[...]


def step_values(param, first, second, grad):
    first = beta_first * first + (1.0 - beta_first) * grad
    second = beta_second * second + (1.0 - beta_second) * grad * grad
    mean_hat = first * (1.0 / (1.0 - beta_first**STEP))
    var_hat = second * (1.0 / (1.0 - beta_second**STEP))
    param = param - learn_rate * (
        mean_hat / (jnp.sqrt(var_hat) + adam_epsilon) + decay_rate * param
    )
    return param, first, second, param.astype(BF16)


def optimize(shares, *refs):
    reduced_ref, sum_ref, lead_ref = refs[:3]
    early = refs[3 : 3 + shares]
    late = refs[3 + shares : 3 + 2 * shares]
    wide = refs[3 + 2 * shares : 6 + 2 * shares]
    tall = refs[6 + 2 * shares : 9 + 2 * shares]
    query = refs[9 + 2 * shares : 12 + 2 * shares]
    outs = refs[12 + 2 * shares :]
    scalars, wide_hbm, tall_hbm, query_out = outs[:3], outs[3:7], outs[7:11], outs[11:15]
    early_s, late_s, wide_out, tall_out, sems = outs[15], outs[16], outs[17:21], outs[21:25], outs[25]
    grp, _ = place()
    _, cut, share = shares_of()
    for table, stacks, halves in ((early_s, early, 1), (late_s, late, 2)):
        size = stacks[0].shape[1] // halves
        for n, ref in enumerate(stacks):
            for m in range(CUTS):
                for half in range(halves):
                    at = (half * shares + jnp.bitwise_xor(share, n)) * CUTS
                    at = (at + jnp.bitwise_xor(cut, m)) * size
                    table[pl.ds(at, size)] = ref[m, half * size : (half + 1) * size]
    norm = jnp.sqrt(reduced_ref[1:2, 0:1])
    for ref, value in zip(scalars, (reduced_ref[0:1, 0:1], sum_ref[0:1, 0:1], norm)):
        ref[...] = value
    factor = jnp.minimum(1.0, clip_limit / (norm + 1e-06))
    rows = wide[0].shape[0]
    per = rows // 16

    def tile(table, t):
        return jnp.concatenate([table[t * per + g] for g in range(per)], axis=0).astype(F32)

    def put(ins, targets, at, grad):
        new = step_values(*[r[at] for r in ins], grad * factor)
        for ref, value in zip(targets, new):
            ref[at] = value

    def at(t, width=128):
        return (slice(None), slice(t * 128, t * 128 + width))

    copies = []

    def flush(sources, targets, lo, hi):
        for source, target in zip(sources, targets):
            copy = pltpu.make_async_copy(
                source.at[:, lo:hi], target.at[:, lo:hi], sems.at[len(copies)]
            )
            copy.start()
            copies.append(copy)

    low = half_low((rows, 128))
    for t in range(6):
        put(wide, wide_out, at(t), tile(late_s, t))
    for t in range(3):
        put(wide, wide_out, at(6 + t), tile(late_s, 15 + t))
    flush(wide_out, wide_hbm, 0, 3 * D)
    lead = lead_ref[pl.ds(pl.multiple_of(grp * rows, 16), rows), :].astype(F32)
    lines = jnp.concatenate([tile(late_s, 27 + t) for t in range(mod_tiles(rows))], axis=0)
    for t in range(18):
        grad = lead[:, 0:1] * lines[4 * t : 4 * t + 1]
        for g in (1, 2):
            grad = grad + lead[:, g : g + 1] * lines[4 * t + g : 4 * t + g + 1]
        put(wide, wide_out, at(9 + t), grad)
    flush(wide_out, wide_hbm, 3 * D, 9 * D)
    qkv = 18
    for j in range(3):
        put(wide, wide_out, at(27 + j), tile(late_s, qkv + 6 + j))
        one, two = tile(late_s, qkv + 2 * j), tile(late_s, qkv + 2 * j + 1)
        put(wide, wide_out, at(30 + j), jnp.where(low, one, swap_halves(two)))
        put(wide, wide_out, at(33 + j), jnp.where(low, swap_halves(one), two))
    flush(wide_out, wide_hbm, 9 * D, 12 * D)
    for t in range(15 + 8):
        put(wide, wide_out, at(36 + t), tile(early_s, t))
    rest = OUT - 8 * 128
    put(wide, wide_out, at(59, rest), tile(early_s, 23)[:, :rest])
    flush(wide_out, wide_hbm, 12 * D, wide[0].shape[1])
    for t in range(8):
        put(tall, tall_out, at(t), tile(late_s, 6 + t))
    flush(tall_out, tall_hbm, 0, 8 * 128)
    last = tile(late_s, 14)
    lane = iota((rows, 128), 1)
    for t in range(FF // 128):
        turned = pltpu.roll(tile(early_s, 24 + t), rest, 1)
        put(tall, tall_out, at(8 + t), jnp.where(lane < rest, last, turned))
        if t == 0:
            eye = iota((rows, rows), 0) == iota((rows, rows), 1)
            grad = jnp.sum(jnp.where(eye, last[:, rest : rest + 1], 0.0), axis=0, keepdims=True)
            put(query, query_out, (slice(None), slice(None)), grad)
        last = turned
    put(tall, tall_out, at(8 + FF // 128, rest), last[:, :rest])
    flush(tall_out, tall_hbm, 8 * 128, tall[0].shape[1])
    for copy in copies:
        copy.wait()


def shift(value, axis, bit):
    size = lax.axis_size(axis)
    return lax.ppermute(value, axis, [(i, i ^ bit) for i in range(size)])


def gather_blocks(own, group):
    blocks = {0: own}
    for j in range(2, group, 2):
        blocks[j] = shift(own, "grp", j)
    for j in range(0, group, 2):
        blocks[j + 1] = shift(blocks[j], "grp", 1)
    return [blocks[j] for j in range(group)]


def granules(rows, cols, shares):
    unit = 2 * shares * CUTS
    return -(-(rows // 16) * (cols // 128) // unit) * unit


def piece_shape(count):
    return sds((count, 16, 128), BF16)


def reduce_cores(*sources, after=()):
    pairs, rows, _ = sources[0][0].shape
    shares = lax.axis_size("seq") // CUTS
    count = granules(rows, sum(keep.shape[2] for keep, _ in sources), shares)
    results = call(
        functools.partial(sum_cores, pairs, len(sources)),
        [piece_shape(count // 2)] * pairs + [piece_shape(count // 2 // shares * pairs)] * shares,
        scratch=[pltpu.VMEM((pairs, count, 16, 128), BF16)],
        after=after,
    )(*[x for source in sources for x in source])
    return results[:pairs], results[pairs:]


def reduce_cores_once(keep, got, after=()):
    pairs, rows, cols = keep.shape
    parts = lax.axis_size("seq")
    count = -(-(rows // 16) * (cols // 128) // parts) * parts
    halves = call(
        functools.partial(sum_cores_once, pairs), [piece_shape(count)] * pairs, after=after
    )(keep, got)
    return [halves[0]] + [shift(halves[j], "grp", 2 * j) for j in range(1, pairs)]


def reduce_and_deal(pieces, over, after=()):
    count = pieces[0].shape[0]
    number = CUTS if over else lax.axis_size("seq") // CUTS
    outs = call(
        functools.partial(sum_and_deal, over),
        [piece_shape(count // number)] * number,
        scratch=[pltpu.VMEM((count, 16, 128), BF16)],
        after=after,
    )(*pieces)
    if over:
        return over_cuts(outs[0], outs[1:])
    return [outs[0]] + [shift(outs[n], "seq", n) for n in range(1, number)]


def exchange_once(by_grp, by_share):
    return [by_grp[0]] + [shift(by_grp[j], "grp", 2 * j) for j in range(1, len(by_grp))], [
        by_share[0]
    ] + [shift(by_share[n], "seq", n) for n in range(1, len(by_share))]


def reduce_once(by_grp, by_share, after=()):
    pairs, shares = len(by_grp), len(by_share)
    size = by_grp[0].shape[0] // shares
    results = call(
        functools.partial(sum_both, pairs, shares),
        [piece_shape(size)] * (pairs + shares),
        scratch=[pltpu.VMEM(by_grp[0].shape, BF16)],
        after=after,
    )(*by_grp, *by_share)
    return results[:shares], results[shares:]


def exchange_again(by_share, by_grp):
    pairs, shares = len(by_grp), len(by_share)
    return [by_share[0]] + [shift(by_share[n], "seq", n) for n in range(1, shares)], [
        by_grp[0]
    ] + [shift(by_grp[j], "grp", 2 * j) for j in range(1, pairs)]


def reduce_twice(by_share, by_grp, after=()):
    pairs, shares = len(by_grp), len(by_share)
    size = by_grp[0].shape[0]
    return call(
        functools.partial(sum_both_again, pairs, shares),
        [piece_shape(2 * size // CUTS)] * CUTS,
        scratch=[pltpu.VMEM((2, size, 16, 128), BF16)],
        after=after,
    )(*by_share, *by_grp)


def over_cuts(first, others=None):
    shares = lax.axis_size("seq") // CUTS
    sent = [first] * (CUTS - 1) if others is None else others
    return [first] + [shift(sent[m - 1], "seq", m * shares) for m in range(1, CUTS)]


def gather_shares(pieces, after=()):
    shares = lax.axis_size("seq") // CUTS
    column = call(stack, sds((CUTS,) + pieces[0].shape, BF16), after=after)(*pieces)
    return [column] + [shift(column, "seq", n) for n in range(1, shares)]


def butterfly(value, axis, bit, stop):
    while bit < stop:
        value = value + shift(value, axis, bit)
        bit *= 2
    return value


def lead_table():
    half = D // 2
    hours = 6.0 * np.exp2(np.arange(3, dtype=np.float32))
    freqs = np.exp(-np.log(np.float32(1000.0)) * np.arange(half, dtype=np.float32) / half)
    angles = hours[None, :] * freqs.astype(np.float32)[:, None]
    waves = np.concatenate([np.sin(angles), np.cos(angles)], axis=0)
    table = np.zeros((D, 128), np.float32)
    table[:, :3] = waves / (1.0 + np.exp(-waves))
    return jnp.asarray(table).astype(BF16)


def cosine_table(count):
    line = np.arange(count, dtype=np.float32)
    return jnp.asarray(np.cos(np.pi * ((line + 0.5) / count - 0.5)).astype(np.float32))


def per_device(
    fields,
    targets,
    land_mask,
    interval,
    samples,
    wide_weights,
    wide_firsts,
    wide_seconds,
    tall_weights,
    tall_firsts,
    tall_seconds,
    query_vector,
    query_firsts,
    query_seconds,
):
    group = lax.axis_size("grp")
    parts = lax.axis_size("seq")
    shares = parts // CUTS
    rows, columns = wide_weights.shape
    items, tokens = fields.shape[:2]
    units = items * HEADS // CUTS
    every = items * tokens
    late_cols = D + FF + OUTP + FF

    query_row = query_vector.reshape(1, rows)
    tall = [x.T for x in (tall_weights, tall_firsts, tall_seconds)]
    lead = lead_table()
    cosines = cosine_table(tokens // COLS * parts)
    fields = fields.transpose(0, 2, 1)
    targets = targets.transpose(0, 2, 1)
    mask = jnp.pad(
        land_mask.transpose(0, 2, 1), ((0, 0), (0, VARP - VARS), (0, 0)), constant_values=-1
    )

    def columns_of(index):
        return pl.BlockSpec((rows, 3 * D), lambda i: (0, index))

    first_own, second_own = call(
        pack_first,
        [sds((rows, 2 * D + OUTP), BF16), sds((rows + RIDERS, 4 * D), BF16)],
        grid=(1,),
        in_specs=[smem(), smem()]
        + [columns_of(i) for i in (0, 1, 2, 3, 0)]
        + [pl.BlockSpec((1, rows), lambda i: (0, 0)), whole(), whole()],
        out_specs=[whole()] * 2,
        scratch=[pltpu.VMEM((RIDERS, 4 * D), F32)],
        us=3,
        limit=62,
    )(samples, cosines, *[wide_weights] * 4, tall[0], query_row, lead, mask)
    first = gather_blocks(first_own, group)
    second = gather_blocks(second_own, group)
    late_own = call(
        pack_late,
        sds((rows, late_cols), BF16),
        grid=(1,),
        in_specs=[columns_of(4), columns_of(5), columns_of(6), whole()],
        out_specs=whole(),
        us=2,
        limit=62,
        after=(first_own,),
    )(wide_weights, wide_weights, wide_weights, tall[0])
    late_blocks = gather_blocks(late_own, group)

    by_item = pl.BlockSpec((tokens, D), lambda i: (i, 0))

    def lane_block(height):
        return pl.BlockSpec((1, height, tokens), lambda i: (i, 0, 0))

    heads_spec = pl.BlockSpec((HEADS, 1, OUT, tokens), lambda i: (0, i, 0, 0))
    packed = units * (tokens + tokens // 2) + 16

    probs, picked, gathered, agg_weights, embed, fused_w, probe = call(
        functools.partial(aggregate, group),
        [
            in_hbm((items, HEADS * VARP, tokens), F32),
            in_hbm((HEADS, items, OUT, tokens), BF16),
            sds((every, D), BF16),
            in_hbm((D, 2 * D), BF16),
            in_hbm((D, OUTP), BF16),
            in_hbm((OUT, D), BF16),
            in_hbm((D, 128), BF16),
        ],
        grid=(items,),
        in_specs=[lane_block(OUT), lane_block(VARP)] + [whole()] * group,
        out_specs=[lane_block(HEADS * VARP), heads_spec, by_item] + [whole()] * 4,
        scratch=[
            pltpu.VMEM((HEADS * VARP, OUT), BF16),
            pltpu.VMEM((D, OUT), BF16),
            pltpu.VMEM((D, tokens), F32),
        ],
        us=10,
        limit=34,
    )(fields, mask, *first)
    results = call(
        functools.partial(project, group),
        [
            in_hbm((every, D), F32),
            in_hbm((every, D), BF16),
            in_hbm((D, 4 * D), BF16),
            in_hbm((8, 6 * D), F32),
        ]
        + [sds((packed, 128), BF16)] * CUTS,
        grid=(items,),
        in_specs=[smem(), by_item] + [whole()] * group,
        out_specs=[by_item, by_item] + [whole()] * (2 + CUTS),
        scratch=[pltpu.VMEM((items * HEADS, tokens + tokens // 2, 128), BF16)],
        us=4,
        limit=34,
    )(interval, gathered, *second)
    x0, n1, second_weights, mods = results[:4]
    dealt = results[4:]

    own = over_cuts(dealt[0], dealt[1:])
    keys_only = [x[: units * tokens + 16] for x in own]
    others = [shift(keys_only[m], "seq", n) for n in range(1, shares) for m in range(CUTS)]
    keys_total = parts * tokens

    half_in = pl.BlockSpec((1, tokens // 2, 128), lambda u: (u, 0, 0))
    kept_spec = pl.BlockSpec((1, CUTS, tokens, 128), lambda u: (u, 0, 0, 0))
    lse_spec = pl.BlockSpec((1, CUTS, 8, tokens), lambda u: (u, 0, 0, 0))
    pack_spec = pl.BlockSpec((1, CUTS, tokens // 2, 128), lambda u: (u, 0, 0, 0))
    half_out = sds((units, tokens // 2, 128), BF16)
    results = call(
        functools.partial(attend, shares),
        [half_out] * CUTS
        + [
            in_hbm((units, CUTS, tokens, 128), F32),
            in_hbm((units, CUTS, 8, tokens), F32),
            in_hbm((8, 128), F32),
        ],
        grid=(units,),
        in_specs=[whole()] * (CUTS * shares),
        out_specs=[half_in] * CUTS + [kept_spec, lse_spec, whole()],
        scratch=[pltpu.VMEM((keys_total, 128), BF16)],
        us=9,
        limit=60 if shares > 2 else 34,
    )(*own, *others)
    backs, (kept, lse, weight_sum) = results[:CUTS], results[CUTS:]
    heads_in = over_cuts(backs[0], backs[1:])

    saved = [D, D, D, FF, D, OUT, D, FF]
    results = call(
        functools.partial(middle, group),
        [in_hbm((every, D), F32), in_hbm((items, 8, D), F32), in_hbm((8, 128), F32)]
        + [half_out] * CUTS
        + [sds((every, width), BF16) for width in saved],
        grid=(items,),
        in_specs=[smem(), smem(), smem(), whole(), by_item, lane_block(OUT), lane_block(VARP)]
        + [whole()] * (CUTS + group + 1),
        out_specs=[by_item, pl.BlockSpec((1, 8, D), lambda i: (i, 0, 0))]
        + [whole()] * (1 + CUTS)
        + [pl.BlockSpec((tokens, width), lambda i: (i, 0)) for width in saved],
        scratch=[
            pltpu.VMEM((D, late_cols), BF16),
            pltpu.VMEM((items * HEADS, tokens // 2, 128), BF16),
            pltpu.VMEM((items * HEADS, tokens // 2, 128), BF16),
        ],
        us=11,
        limit=34,
    )(
        interval,
        samples,
        cosines,
        weight_sum,
        x0,
        targets,
        mask,
        *heads_in,
        *late_blocks,
        mods,
    )
    dx1, mod_rows, loss = results[:3]
    sends, operands = results[3 : 3 + CUTS], results[3 + CUTS :]
    early_keep, early_send = call(
        middle_weights,
        [sds((group // 2, rows, late_cols), BF16)] * 2,
        scratch=[pltpu.VMEM((D, late_cols), F32)],
        us=6,
        limit=34,
    )(*operands)
    grads_in = over_cuts(sends[0], sends[1:])

    def of_unit(u, *shape):
        return pl.BlockSpec((1,) + shape, lambda i: (u,) + (0,) * len(shape))

    def back_of(u, after):
        results = call(
            functools.partial(attend_back, shares, u),
            [sds((1, CUTS, tokens // 2, 128), BF16)]
            + [sds((1, CUTS, tokens, 128), BF16)] * shares,
            grid=(1,),
            in_specs=[whole()] * (CUTS * shares)
            + [of_unit(u, tokens // 2, 128)] * CUTS
            + [of_unit(u, CUTS, tokens, 128), of_unit(u, CUTS, 8, tokens)],
            out_specs=[whole()] * (1 + shares),
            scratch=[
                pltpu.VMEM((keys_total, 128), BF16),
                pltpu.VMEM((128, keys_total), BF16),
                pltpu.VMEM((keys_total, 128), F32),
            ],
            us=6,
            limit=60 if shares > 2 else 34,
            after=after,
        )(*own, *others, *grads_in, kept, lse)
        far = results[2:]
        if u == 2:
            far = [once_ready(far[0], units_in[0][1:]), *far[1:]]
        return results[:2], [shift(far[n], "seq", n + 1) for n in range(shares - 1)]

    def joined(near, far):
        dealt = call(
            functools.partial(join_back, shares),
            [sds((tokens + tokens // 2, 128), BF16)] * CUTS,
        )(*near, *far)
        return over_cuts(dealt[0], dealt[1:])

    early_got = shift(early_send, "grp", 1)
    partial_sums, units_in = [], []
    for u in range(units):
        after = (early_keep,) if u == 0 else (partial_sums[u - 1][0][0],)
        if u == 2:
            early_once = reduce_cores_once(early_keep, early_got, after=after)
            after += (early_once[0],)
        if u >= 2:
            units_in.append(joined(*partial_sums[u - 2]))
        partial_sums.append(back_of(u, after))
    units_in.append(joined(*partial_sums[-2]))
    units_in.append(joined(*partial_sums[-1]))
    early_twice = reduce_and_deal(early_once, False, after=(units_in[1][1],))

    second_cols = 4 * D + mod_tiles(rows) * 128
    dagg, second_keep, second_send = call(
        functools.partial(project_back, units),
        [
            sds((items, D, tokens), BF16),
            sds((group // 2, rows, second_cols), BF16),
            sds((group // 2, rows, second_cols), BF16),
        ],
        grid=(items,),
        in_specs=[
            smem(),
            by_item,
            by_item,
            by_item,
            pl.BlockSpec((1, 8, D), lambda i: (i, 0, 0)),
            by_item,
        ]
        + [whole()] * (2 + CUTS * units),
        out_specs=[pl.BlockSpec((1, D, tokens), lambda i: (i, 0, 0))] + [whole()] * 2,
        scratch=[
            pltpu.VMEM((items * HEADS, tokens + tokens // 2, 128), BF16),
            pltpu.VMEM((tokens, 3 * D), BF16),
            pltpu.VMEM((D, 4 * D), F32),
            pltpu.VMEM((8, 6 * D), F32),
            pltpu.VMEM((mod_tiles(rows) * rows, 128), F32),
        ],
        us=4,
        limit=34,
    )(
        interval,
        x0,
        n1,
        dx1,
        mod_rows,
        gathered,
        second_weights,
        mods,
        *[x for unit in units_in for x in unit],
    )
    second_got = shift(second_send, "grp", 1)
    early_pieces = reduce_and_deal(early_twice, True, after=(dagg,))
    late_keep, late_send = call(
        aggregate_back,
        [sds((group // 2, rows, 2 * D + OUTP), BF16)] * 2,
        grid=(items,),
        in_specs=[
            pl.BlockSpec((1, D, tokens), lambda i: (i, 0, 0)),
            lane_block(HEADS * VARP),
            heads_spec,
            lane_block(OUT),
            lane_block(VARP),
        ]
        + [whole()] * 4,
        out_specs=[whole()] * 2,
        scratch=[
            pltpu.VMEM((HEADS * VARP, tokens), BF16),
            pltpu.VMEM((D, 2 * D + OUTP), F32),
            pltpu.VMEM((OUT, D), F32),
            pltpu.VMEM((HEADS * VARP, OUT), F32),
        ],
        us=13,
        limit=34,
        after=(early_pieces[0],),
    )(dagg, probs, picked, fields, mask, fused_w, agg_weights, embed, probe)
    early_piece, early_squares = call(
        sum_pieces,
        [piece_shape(early_pieces[0].shape[0]), sds((16, 128), F32)],
        after=(late_keep,),
    )(*early_pieces)
    early_column = over_cuts(early_piece)
    late_first = reduce_cores(
        (late_keep, shift(late_send, "grp", 1)),
        (second_keep, second_got),
    )
    late_second = reduce_once(*exchange_once(*late_first))
    early_all = gather_shares(early_column, after=(late_second[0][0],))
    late_third = reduce_twice(*exchange_again(*late_second))
    late_pieces = over_cuts(late_third[0], late_third[1:])
    start = (rows // 16) * 27
    stop = (rows // 16) * (27 + mod_tiles(rows))
    count = late_pieces[0].shape[0]
    late_piece = call(
        functools.partial(sum_late, start, stop), piece_shape(count + 1)
    )(early_squares, loss, lead, *late_pieces)
    late_column, reduced = call(
        stack_late, [sds((CUTS, count, 16, 128), BF16), sds((8, 128), F32)]
    )(*over_cuts(late_piece))
    late_all = [late_column] + [shift(late_column, "seq", n) for n in range(1, shares)]
    reduced = butterfly(reduced, "grp", 1, group)
    reduced = butterfly(reduced, "seq", 1, shares)

    def like(x, dtype=F32):
        return sds(x.shape, dtype)

    results = call(
        functools.partial(optimize, shares),
        [sds((1, 1), F32)] * 3
        + [like(wide_weights)] * 3
        + [like(wide_weights, BF16)]
        + [like(tall[0])] * 3
        + [like(tall[0], BF16)]
        + [like(query_row)] * 3
        + [like(query_row, BF16)],
        out_specs=[whole()] * 3 + [pl.BlockSpec(memory_space=pl.ANY)] * 8 + [whole()] * 4,
        scratch=[
            pltpu.VMEM((parts * early_piece.shape[0], 16, 128), BF16),
            pltpu.VMEM((parts * count, 16, 128), BF16),
        ]
        + [pltpu.VMEM(wide_weights.shape, dtype) for dtype in (F32, F32, F32, BF16)]
        + [pltpu.VMEM(tall[0].shape, dtype) for dtype in (F32, F32, F32, BF16)]
        + [pltpu.SemaphoreType.DMA((24,))],
        us=10,
        limit=34,
    )(
        reduced,
        weight_sum,
        lead,
        *early_all,
        *late_all,
        wide_weights,
        wide_firsts,
        wide_seconds,
        *tall,
        query_row,
        query_firsts.reshape(1, rows),
        query_seconds.reshape(1, rows),
    )
    tall_out = tuple(r.T for r in results[7:11])
    query_out = tuple(r.reshape(rows) for r in results[11:15])
    return tuple(r.reshape(()) for r in results[:3]) + tuple(results[3:7]) + tall_out + query_out


def solution(mesh):
    placed = (
        P("grp", "seq", None),
        P("grp", "seq", None),
        P("grp", "seq", None),
        P("grp"),
        P("grp"),
        P("grp", None),
        P("grp", None),
        P("grp", None),
        P(None, "grp"),
        P(None, "grp"),
        P(None, "grp"),
        P("grp"),
        P("grp"),
        P("grp"),
    )
    return jax.shard_map(
        per_device,
        mesh=mesh,
        in_specs=placed,
        out_specs=(
            P(),
            P(),
            P(),
            P("grp", None),
            P("grp", None),
            P("grp", None),
            P("grp", None),
            P(None, "grp"),
            P(None, "grp"),
            P(None, "grp"),
            P(None, "grp"),
            P("grp"),
            P("grp"),
            P("grp"),
            P("grp"),
        ),
        check_vma=False,
    )
```

profile of v0, /device:TPU:0, one launch (start us, length us, event | category | flops | bytes accessed | tf_op | source)
XLA Modules:
  0.0 277.0 jit_solution(9895487116459851335)
XLA Ops:
  8.4 9.5 %collective-permute-done.1.refs_4_ = bf16[96,1920]{1,0:T(8,128)(2,1)S(1)} collective-permute-done((bf16[96,1920]{1,0:T(8,128)(2,1)}, bf16[96,1920]{1,0:T(8,128)(2,1)S(1)}, u32[]{:S(2)}, u32[]{:S(2)}) %collective-permute-start.1) | collective-permute-done | bytes 368672 | tf_op jit(solution)/shard_map/ppermute | solution.py:1026
  23.1 3.3 %collective-permute-done.4.refs_4_ = bf16[128,1536]{1,0:T(8,128)(2,1)} collective-permute-done((bf16[128,1536]{1,0:T(8,128)(2,1)}, bf16[128,1536]{1,0:T(8,128)(2,1)}, u32[]{:S(2)}, u32[]{:S(2)}) %collective-permute-start.4) | collective-permute-done | bytes 393248 | tf_op jit(solution)/shard_map/ppermute | solution.py:1026
  26.5 10.6 %shard_map.272 = (f32[2,480,256]{2,1,0:T(8,128)}, bf16[6,2,1104,256]{3,2,1,0:T(8,128)(2,1)}, bf16[512,384]{1,0:T(8,128)(2,1)S(1)}, bf16[384,768]{1,0:T(8,128)(2,...) custom-call(bf16[2,1104,256]{2,1,0:T(8,128)(2,1)S(1)} %bitcast.28, ...), custom_call_target="tpu_custom_call" | custom-call | flops 11500000256 | bytes 1024 | tf_op jit(solution)/shard_map/pallas_call | solution.py:93
  37.2 4.9 %shard_map.273 = (f32[512,384]{1,0:T(8,128)}, bf16[512,384]{1,0:T(8,128)(2,1)}, bf16[384,1536]{1,0:T(8,128)(2,1)}, f32[8,2304]{1,0:T(8,128)}, bf16[1168,128]{1,0...) custom-call(s32[2]{0:T(128)S(1)} %copy-done.23, ...), custom_call_target="tpu_custom_call" | custom-call | flops 4600000000 | bytes 1024 | tf_op jit(solution)/shard_map/pallas_call | solution.py:93
  48.7 9.3 %collective-permute-done.6.refs_1_ = bf16[1168,128]{1,0:T(8,128)(2,1)S(1)} collective-permute-done((bf16[1168,128]{1,0:T(8,128)(2,1)S(1)}, bf16[1168,128]{1,0:T(8,128)(2,1)S(1)}, u32[]{:S(2)}, u32[]{:S(2)}) %collective-permute-start.6) | collective-permute-done | bytes 299040 | tf_op jit(solution)/shard_map/ppermute | solution.py:1026
  59.8 8.2 %collective-permute-done.7.refs_2_ = bf16[1168,128]{1,0:T(8,128)(2,1)S(1)} collective-permute-done((bf16[1168,128]{1,0:T(8,128)(2,1)S(1)}, bf16[1168,128]{1,0:T(8,128)(2,1)S(1)}, u32[]{:S(2)}, u32[]{:S(2)}) %collective-permute-start.7) | collective-permute-done | bytes 299040 | tf_op jit(solution)/shard_map/ppermute | solution.py:1026
  76.0 9.0 %shard_map.274 = (bf16[3,128,128]{2,1,0:T(8,128)(2,1)S(1)}, bf16[3,128,128]{2,1,0:T(8,128)(2,1)S(1)}, bf16[3,128,128]{2,1,0:T(8,128)(2,1)S(1)}, bf16[3,128,128]{...) custom-call(bf16[1168,128]{1,0:T(8,128)(2,1)S(1)} %get-tuple-element.124.refs_0_, ...), custom_call_target="tpu_custom_call" | custom-call | flops 10350000128 | bytes 1024 | tf_op jit(solution)/shard_map/pallas_call | solution.py:93
  85.0 4.7 %collective-permute-start.13 = (bf16[3,128,128]{2,1,0:T(8,128)(2,1)S(1)}, bf16[3,128,128]{2,1,0:T(8,128)(2,1)S(1)}, u32[]{:S(2)}, u32[]{:S(2)}) collective-permute-start(bf16[3,128,128]{2,1,0:T(8,128)(2,1)S(1)} %get-tuple-element.131), channel_id=1, source_target_pairs={{0,2},{1,3},{2,0},{3,1},{4,6},{5,7},{6,4},{7,5},{8,10},{9,11},{10,... | collective-permute-start | bytes 294920 | tf_op jit(solution)/shard_map/ppermute | solution.py:1026
  93.3 5.5 %collective-permute-done.14.refs_9_ = bf16[3,128,128]{2,1,0:T(8,128)(2,1)S(1)} collective-permute-done((bf16[3,128,128]{2,1,0:T(8,128)(2,1)S(1)}, bf16[3,128,128]{2,1,0:T(8,128)(2,1)S(1)}, u32[]{:S(2)}, u32[]{:S(2)}) %collective-permute-start.14) | collective-permute-done | bytes 98336 | tf_op jit(solution)/shard_map/ppermute | solution.py:1026
  99.5 21.5 %shard_map.276 = (f32[512,384]{1,0:T(8,128)}, f32[2,8,384]{2,1,0:T(8,128)}, f32[8,128]{1,0:T(8,128)}, bf16[3,128,128]{2,1,0:T(8,128)(2,1)S(1)}, bf16[3,128,128]{...) custom-call(s32[2]{0:T(128)S(1)} %copy-done.23, ...), custom_call_target="tpu_custom_call" | custom-call | flops 12650000384 | bytes 1024 | tf_op jit(solution)/shard_map/pallas_call | solution.py:93
  129.1 7.2 %collective-permute-done.21.refs_10_ = bf16[3,128,128]{2,1,0:T(8,128)(2,1)S(1)} collective-permute-done((bf16[3,128,128]{2,1,0:T(8,128)(2,1)S(1)}, bf16[3,128,128]{2,1,0:T(8,128)(2,1)S(1)}, u32[]{:S(2)}, u32[]{:S(2)}) %collective-permute-start.21) | collective-permute-done | bytes 98336 | tf_op jit(solution)/shard_map/ppermute | solution.py:1026
  136.3 5.5 %shard_map.278 = (bf16[1,4,128,128]{3,2,1,0:T(8,128)(2,1)S(1)}, bf16[1,4,256,128]{3,2,1,0:T(8,128)(2,1)S(1)}, bf16[1,4,256,128]{3,2,1,0:T(8,128)(2,1)S(1)}) custom-call(bf16[1168,128]{1,0:T(8,128)(2,1)S(1)} %get-tuple-element.124.refs_0_, bf16[1168,128]{1,0:T(8,128)(2,1)S(1)} %collective-permute-done.6.refs_1_, ...), custom_call_target="tpu_custom_call" | custom-call | flops 6899999744 | bytes 1024 | tf_op jit(solution)/shard_map/pallas_call | solution.py:93
  143.4 5.9 %shard_map.279 = (bf16[1,4,128,128]{3,2,1,0:T(8,128)(2,1)S(1)}, bf16[1,4,256,128]{3,2,1,0:T(8,128)(2,1)S(1)}, bf16[1,4,256,128]{3,2,1,0:T(8,128)(2,1)S(1)}) custom-call(bf16[1168,128]{1,0:T(8,128)(2,1)S(1)} %get-tuple-element.124.refs_0_, bf16[1168,128]{1,0:T(8,128)(2,1)S(1)} %collective-permute-done.6.refs_1_, ...), custom_call_target="tpu_custom_call" | custom-call | flops 6899999744 | bytes 1024 | tf_op jit(solution)/shard_map/pallas_call | solution.py:93
  157.1 5.5 %shard_map.284 = (bf16[1,4,128,128]{3,2,1,0:T(8,128)(2,1)S(1)}, bf16[1,4,256,128]{3,2,1,0:T(8,128)(2,1)S(1)}, bf16[1,4,256,128]{3,2,1,0:T(8,128)(2,1)S(1)}) custom-call(bf16[1168,128]{1,0:T(8,128)(2,1)S(1)} %get-tuple-element.124.refs_0_, bf16[1168,128]{1,0:T(8,128)(2,1)S(1)} %collective-permute-done.6.refs_1_, ...), custom_call_target="tpu_custom_call" | custom-call | flops 6899999744 | bytes 1024 | tf_op jit(solution)/shard_map/pallas_call | solution.py:93
  173.1 3.3 %collective-permute-done.25.refs_2_.refs_13_ = bf16[384,128]{1,0:T(8,128)(2,1)S(1)} collective-permute-done((bf16[384,128]{1,0:T(8,128)(2,1)S(1)}, bf16[384,128]{1,0:T(8,128)(2,1)S(1)}, u32[]{:S(2)}, u32[]{:S(2)}) %collective-permute-start.25) | collective-permute-done | bytes 98336 | tf_op jit(solution)/shard_map/ppermute | solution.py:1026
  180.1 5.2 %collective-permute-done.35.refs_18_ = bf16[384,128]{1,0:T(8,128)(2,1)S(1)} collective-permute-done((bf16[384,128]{1,0:T(8,128)(2,1)S(1)}, bf16[384,128]{1,0:T(8,128)(2,1)S(1)}, u32[]{:S(2)}, u32[]{:S(2)}) %collective-permute-start.35) | collective-permute-done | bytes 98336 | tf_op jit(solution)/shard_map/ppermute | solution.py:1026
  185.4 4.0 %shard_map.287 = (bf16[2,384,256]{2,1,0:T(8,128)(2,1)S(1)}, bf16[2,96,1664]{2,1,0:T(8,128)(2,1)S(1)}, bf16[2,96,1664]{2,1,0:T(8,128)(2,1)S(1)}) custom-call(s32[2]{0:T(128)S(1)} %copy-done.24, f32[512,384]{1,0:T(8,128)S(1)} %copy-done.39, bf16[512,384]{1,0:T(8,128)(2,1)S(1)} %copy-done.44, f32[512,384]{1,0:T(8,128)S(1)} %copy-done.40, ...), custom_call_target="tpu_custom_call" | custom-call | flops 4600000000 | bytes 1024 | tf_op jit(solution)/shard_map/pallas_call | solution.py:93
  191.4 9.2 %shard_map.289 = (bf16[2,96,1920]{2,1,0:T(8,128)(2,1)S(1)}, bf16[2,96,1920]{2,1,0:T(8,128)(2,1)S(1)}) custom-call(bf16[2,384,256]{2,1,0:T(8,128)(2,1)S(1)} %get-tuple-element.180.refs_2_.refs_0_, f32[2,480,256]{2,1,0:T(8,128)S(1)} %copy-done.45, bf16[6,2,1104,256]{3,2,1,0:T(8,128)(2,1)S(1)} %bitcast.35, bf16[2,1104,256]{2,1,0:T(8,128)(2,1)S(1)} %bitcast.29, ...), custom_call_target="tpu_custom_call" | custom-call | flops 14949999616 | bytes 1024 | tf_op jit(solution)/shard_map/pallas_call | solution.py:93
  205.9 9.1 %collective-permute-done.42.refs_1_ = bf16[88,16,128]{2,1,0:T(8,128)(2,1)S(1)} collective-permute-done((bf16[88,16,128]{2,1,0:T(8,128)(2,1)S(1)}, bf16[88,16,128]{2,1,0:T(8,128)(2,1)S(1)}, u32[]{:S(2)}, u32[]{:S(2)}) %collective-permute-start.42) | collective-permute-done | bytes 360480 | tf_op jit(solution)/shard_map/ppermute | solution.py:1026
  228.1 3.6 %collective-permute-done.38.refs_2_ = bf16[27,16,128]{2,1,0:T(8,128)(2,1)S(1)} collective-permute-done((bf16[27,16,128]{2,1,0:T(8,128)(2,1)S(1)}, bf16[27,16,128]{2,1,0:T(8,128)(2,1)S(1)}, u32[]{:S(2)}, u32[]{:S(2)}) %collective-permute-start.38) | collective-permute-done | bytes 110624 | tf_op jit(solution)/shard_map/ppermute | solution.py:1026
  234.1 5.0 %collective-permute-start.56 = (bf16[27,16,128]{2,1,0:T(8,128)(2,1)S(1)}, bf16[27,16,128]{2,1,0:T(8,128)(2,1)S(1)}, u32[]{:S(2)}, u32[]{:S(2)}) collective-permute-start(bf16[27,16,128]{2,1,0:T(8,128)(2,1)S(1)} %get-tuple-element.210.refs_0_), channel_id=1, source_target_pairs={{0,4},{1,5},{2,6},{3,7},{4,0},{5,1},{6,2},{7,3},{8,12},{9,13},{10,... | collective-permute-start | bytes 331784 | tf_op jit(solution)/shard_map/ppermute | solution.py:1026
  243.5 4.3 %collective-permute-start.50 = (bf16[23,16,128]{2,1,0:T(8,128)(2,1)S(1)}, bf16[23,16,128]{2,1,0:T(8,128)(2,1)S(1)}, u32[]{:S(2)}, u32[]{:S(2)}) collective-permute-start(bf16[23,16,128]{2,1,0:T(8,128)(2,1)S(1)} %shard_map.294.refs_0_), channel_id=1, source_target_pairs={{0,4},{1,5},{2,6},{3,7},{4,0},{5,1},{6,2},{7,3},{8,12},{9,13},{10,... | collective-permute-start | bytes 282632 | tf_op jit(solution)/shard_map/ppermute | solution.py:1026
  262.8 6.6 %collective-permute-done.54 = f32[8,128]{1,0:T(8,128)S(1)} collective-permute-done((f32[8,128]{1,0:T(8,128)S(1)}, f32[8,128]{1,0:T(8,128)S(1)}, u32[]{:S(2)}, u32[]{:S(2)}) %collective-permute-start.54) | collective-permute-done | bytes 4128 | tf_op jit(solution)/shard_map/ppermute | solution.py:1026
  269.6 7.2 %shard_map.297 = (f32[1,1]{1,0:T(1,128)}, f32[1,1]{1,0:T(1,128)}, f32[1,1]{1,0:T(1,128)}, f32[96,7632]{1,0:T(8,128)}, f32[96,7632]{1,0:T(8,128)}, /*index=5*/f32...) custom-call(f32[8,128]{1,0:T(8,128)S(1)} %add.13.refs_0_, ...), custom_call_target="tpu_custom_call" | custom-call | flops 11500000256 | bytes 1024 | tf_op jit(solution)/shard_map/pallas_call | solution.py:93
  (249 shorter events, 107.1 us)
Async XLA Ops:
  8.3 18.1 %collective-permute-start.4 = (bf16[128,1536]{1,0:T(8,128)(2,1)}, bf16[128,1536]{1,0:T(8,128)(2,1)}, u32[]{:S(2)}, u32[]{:S(2)}) collective-permute-start(bf16[128,1536]{1,0:T(8,128)(2,1)} %get-tuple-element.123.refs_2_), channel_id=1, source_target_pairs={{0,16},{8,24},{16,0},{24,8},{1,17},{9,25},{17,1},{25,9},{2,18},{10... | collective-permute-start | bytes 1179656 | tf_op jit(solution)/shard_map/ppermute | solution.py:1026
  8.4 18.1 %collective-permute-start = (bf16[96,1920]{1,0:T(8,128)(2,1)}, bf16[96,1920]{1,0:T(8,128)(2,1)}, u32[]{:S(2)}, u32[]{:S(2)}) collective-permute-start(bf16[96,1920]{1,0:T(8,128)(2,1)} %get-tuple-element.121.refs_2_.refs_4_), channel_id=1, source_target_pairs={{0,8},{8,0},{16,24},{24,16},{1,9},{9,1},{17,25},{25,17},{2,10},{10... | collective-permute-start | bytes 1105928 | tf_op jit(solution)/shard_map/ppermute | solution.py:1026
  17.9 19.2 %collective-permute-start.3 = (bf16[128,1536]{1,0:T(8,128)(2,1)}, bf16[128,1536]{1,0:T(8,128)(2,1)}, u32[]{:S(2)}, u32[]{:S(2)}) collective-permute-start(bf16[128,1536]{1,0:T(8,128)(2,1)} %get-tuple-element.123.refs_2_), channel_id=1, source_target_pairs={{0,8},{8,0},{16,24},{24,16},{1,9},{9,1},{17,25},{25,17},{2,10},{10... | collective-permute-start | bytes 1179656 | tf_op jit(solution)/shard_map/ppermute | solution.py:1026
  21.1 49.2 %collective-permute-start.17 = (bf16[96,4608]{1,0:T(8,128)(2,1)}, bf16[96,4608]{1,0:T(8,128)(2,1)S(1)}, u32[]{:S(2)}, u32[]{:S(2)}) collective-permute-start(bf16[96,4608]{1,0:T(8,128)(2,1)} %shard_map.275.refs_11_), channel_id=1, source_target_pairs={{0,16},{8,24},{16,0},{24,8},{1,17},{9,25},{17,1},{25,9},{2,18},{10... | collective-permute-start | bytes 2654216 | tf_op jit(solution)/shard_map/ppermute | solution.py:1026
  42.1 16.0 %collective-permute-start.6 = (bf16[1168,128]{1,0:T(8,128)(2,1)S(1)}, bf16[1168,128]{1,0:T(8,128)(2,1)S(1)}, u32[]{:S(2)}, u32[]{:S(2)}) collective-permute-start(bf16[1168,128]{1,0:T(8,128)(2,1)S(1)} %get-tuple-element.125), channel_id=1, source_target_pairs={{0,2},{1,3},{2,0},{3,1},{4,6},{5,7},{6,4},{7,5},{8,10},{9,11},{10,... | collective-permute-start | bytes 897032 | tf_op jit(solution)/shard_map/ppermute | solution.py:1026
  44.3 23.7 %collective-permute-start.7 = (bf16[1168,128]{1,0:T(8,128)(2,1)S(1)}, bf16[1168,128]{1,0:T(8,128)(2,1)S(1)}, u32[]{:S(2)}, u32[]{:S(2)}) collective-permute-start(bf16[1168,128]{1,0:T(8,128)(2,1)S(1)} %get-tuple-element.126), channel_id=1, source_target_pairs={{0,4},{1,5},{2,6},{3,7},{4,0},{5,1},{6,2},{7,3},{8,12},{9,13},{10,... | collective-permute-start | bytes 897032 | tf_op jit(solution)/shard_map/ppermute | solution.py:1026
  46.9 22.7 %collective-permute-start.8 = (bf16[1168,128]{1,0:T(8,128)(2,1)S(1)}, bf16[1168,128]{1,0:T(8,128)(2,1)S(1)}, u32[]{:S(2)}, u32[]{:S(2)}) collective-permute-start(bf16[1168,128]{1,0:T(8,128)(2,1)S(1)} %get-tuple-element.127), channel_id=1, source_target_pairs={{0,6},{1,7},{2,4},{3,5},{4,2},{5,3},{6,0},{7,1},{8,14},{9,15},{10,... | collective-permute-start | bytes 897032 | tf_op jit(solution)/shard_map/ppermute | solution.py:1026
  46.9 23.4 %collective-permute-start.9 = (bf16[784,128]{1,0:T(8,128)(2,1)S(1)}, bf16[784,128]{1,0:T(8,128)(2,1)S(1)}, u32[]{:S(2)}, u32[]{:S(2)}) collective-permute-start(bf16[784,128]{1,0:T(8,128)(2,1)S(1)} %slice.12), channel_id=1, source_target_pairs={{0,1},{1,0},{2,3},{3,2},{4,5},{5,4},{6,7},{7,6},{8,9},{9,8},{10,11... | collective-permute-start | bytes 602120 | tf_op jit(solution)/shard_map/ppermute | solution.py:1026
  70.3 21.9 %collective-permute-start.16 = (bf16[96,4608]{1,0:T(8,128)(2,1)S(1)}, bf16[96,4608]{1,0:T(8,128)(2,1)S(1)}, u32[]{:S(2)}, u32[]{:S(2)}) collective-permute-start(bf16[96,4608]{1,0:T(8,128)(2,1)S(1)} %copy-done.2), channel_id=1, source_target_pairs={{0,8},{8,0},{16,24},{24,16},{1,9},{9,1},{17,25},{25,17},{2,10},{10... | collective-permute-start | bytes 2654216 | tf_op jit(solution)/shard_map/ppermute | solution.py:1026
  70.3 28.5 %collective-permute-start.18 = (bf16[96,4608]{1,0:T(8,128)(2,1)S(1)}, bf16[96,4608]{1,0:T(8,128)(2,1)S(1)}, u32[]{:S(2)}, u32[]{:S(2)}) collective-permute-start(bf16[96,4608]{1,0:T(8,128)(2,1)S(1)} %collective-permute-done.17.refs_13_), channel_id=1, source_target_pairs={{0,8},{8,0},{16,24},{24,16},{1,9},{9,1},{17,25},{25,17},{2,10},{10... | collective-permute-start | bytes 2654216 | tf_op jit(solution)/shard_map/ppermute | solution.py:1026
  123.8 30.6 %collective-permute-start.19 = (bf16[2,96,4608]{2,1,0:T(8,128)(2,1)S(1)}, bf16[2,96,4608]{2,1,0:T(8,128)(2,1)S(1)}, u32[]{:S(2)}, u32[]{:S(2)}) collective-permute-start(bf16[2,96,4608]{2,1,0:T(8,128)(2,1)S(1)} %get-tuple-element.144), channel_id=1, source_target_pairs={{0,8},{8,0},{16,24},{24,16},{1,9},{9,1},{17,25},{25,17},{2,10},{10... | collective-permute-start | bytes 5308424 | tf_op jit(solution)/shard_map/ppermute | solution.py:1026
  149.3 17.6 %collective-permute-start.24 = (bf16[1,4,256,128]{3,2,1,0:T(8,128)(2,1)S(1)}, bf16[1,4,256,128]{3,2,1,0:T(8,128)(2,1)S(1)}, u32[]{:S(2)}, u32[]{:S(2)}) collective-permute-start(bf16[1,4,256,128]{3,2,1,0:T(8,128)(2,1)S(1)} %get-tuple-element.156), channel_id=1, source_target_pairs={{0,1},{1,0},{2,3},{3,2},{4,5},{5,4},{6,7},{7,6},{8,9},{9,8},{10,11... | collective-permute-start | bytes 786440 | tf_op jit(solution)/shard_map/ppermute | solution.py:1026
  150.0 14.7 %collective-permute-start.28 = (bf16[384,128]{1,0:T(8,128)(2,1)S(1)}, bf16[384,128]{1,0:T(8,128)(2,1)S(1)}, u32[]{:S(2)}, u32[]{:S(2)}) collective-permute-start(bf16[384,128]{1,0:T(8,128)(2,1)S(1)} %get-tuple-element.167), channel_id=1, source_target_pairs={{0,2},{1,3},{2,0},{3,1},{4,6},{5,7},{6,4},{7,5},{8,10},{9,11},{10,... | collective-permute-start | bytes 294920 | tf_op jit(solution)/shard_map/ppermute | solution.py:1026
  151.9 12.7 %collective-permute-start.29 = (bf16[384,128]{1,0:T(8,128)(2,1)S(1)}, bf16[384,128]{1,0:T(8,128)(2,1)S(1)}, u32[]{:S(2)}, u32[]{:S(2)}) collective-permute-start(bf16[384,128]{1,0:T(8,128)(2,1)S(1)} %get-tuple-element.168), channel_id=1, source_target_pairs={{0,4},{1,5},{2,6},{3,7},{4,0},{5,1},{6,2},{7,3},{8,12},{9,13},{10,... | collective-permute-start | bytes 294920 | tf_op jit(solution)/shard_map/ppermute | solution.py:1026
  155.5 20.9 %collective-permute-start.23 = (bf16[216,16,128]{2,1,0:T(8,128)(2,1)}, bf16[216,16,128]{2,1,0:T(8,128)(2,1)S(1)}, u32[]{:S(2)}, u32[]{:S(2)}) collective-permute-start(bf16[216,16,128]{2,1,0:T(8,128)(2,1)} %get-tuple-element.154), channel_id=1, source_target_pairs={{0,16},{8,24},{16,0},{24,8},{1,17},{9,25},{17,1},{25,9},{2,18},{10... | collective-permute-start | bytes 2654216 | tf_op jit(solution)/shard_map/ppermute | solution.py:1026
  222.4 16.7 %collective-permute-start.46 = (bf16[22,16,128]{2,1,0:T(8,128)(2,1)S(1)}, bf16[22,16,128]{2,1,0:T(8,128)(2,1)S(1)}, u32[]{:S(2)}, u32[]{:S(2)}) collective-permute-start(bf16[22,16,128]{2,1,0:T(8,128)(2,1)S(1)} %get-tuple-element.206), channel_id=1, source_target_pairs={{0,2},{1,3},{2,0},{3,1},{4,6},{5,7},{6,4},{7,5},{8,10},{9,11},{10,... | collective-permute-start | bytes 270344 | tf_op jit(solution)/shard_map/ppermute | solution.py:1026
  223.7 17.6 %collective-permute-start.47 = (bf16[22,16,128]{2,1,0:T(8,128)(2,1)S(1)}, bf16[22,16,128]{2,1,0:T(8,128)(2,1)S(1)}, u32[]{:S(2)}, u32[]{:S(2)}) collective-permute-start(bf16[22,16,128]{2,1,0:T(8,128)(2,1)S(1)} %get-tuple-element.207), channel_id=1, source_target_pairs={{0,4},{1,5},{2,6},{3,7},{4,0},{5,1},{6,2},{7,3},{8,12},{9,13},{10,... | collective-permute-start | bytes 270344 | tf_op jit(solution)/shard_map/ppermute | solution.py:1026
  225.8 15.4 %collective-permute-start.48 = (bf16[22,16,128]{2,1,0:T(8,128)(2,1)S(1)}, bf16[22,16,128]{2,1,0:T(8,128)(2,1)S(1)}, u32[]{:S(2)}, u32[]{:S(2)}) collective-permute-start(bf16[22,16,128]{2,1,0:T(8,128)(2,1)S(1)} %get-tuple-element.208), channel_id=1, source_target_pairs={{0,6},{1,7},{2,4},{3,5},{4,2},{5,3},{6,0},{7,1},{8,14},{9,15},{10,... | collective-permute-start | bytes 270344 | tf_op jit(solution)/shard_map/ppermute | solution.py:1026
  231.7 16.1 %collective-permute-start.57 = (bf16[27,16,128]{2,1,0:T(8,128)(2,1)S(1)}, bf16[27,16,128]{2,1,0:T(8,128)(2,1)S(1)}, u32[]{:S(2)}, u32[]{:S(2)}) collective-permute-start(bf16[27,16,128]{2,1,0:T(8,128)(2,1)S(1)} %get-tuple-element.210.refs_0_), channel_id=1, source_target_pairs={{0,6},{1,7},{2,4},{3,5},{4,2},{5,3},{6,0},{7,1},{8,14},{9,15},{10,... | collective-permute-start | bytes 331784 | tf_op jit(solution)/shard_map/ppermute | solution.py:1026
  234.1 19.0 %collective-permute-start.56 = (bf16[27,16,128]{2,1,0:T(8,128)(2,1)S(1)}, bf16[27,16,128]{2,1,0:T(8,128)(2,1)S(1)}, u32[]{:S(2)}, u32[]{:S(2)}) collective-permute-start(bf16[27,16,128]{2,1,0:T(8,128)(2,1)S(1)} %get-tuple-element.210.refs_0_), channel_id=1, source_target_pairs={{0,4},{1,5},{2,6},{3,7},{4,0},{5,1},{6,2},{7,3},{8,12},{9,13},{10,... | collective-permute-start | bytes 331784 | tf_op jit(solution)/shard_map/ppermute | solution.py:1026
  239.1 14.0 %collective-permute-start.55 = (bf16[27,16,128]{2,1,0:T(8,128)(2,1)S(1)}, bf16[27,16,128]{2,1,0:T(8,128)(2,1)S(1)}, u32[]{:S(2)}, u32[]{:S(2)}) collective-permute-start(bf16[27,16,128]{2,1,0:T(8,128)(2,1)S(1)} %get-tuple-element.210.refs_0_), channel_id=1, source_target_pairs={{0,2},{1,3},{2,0},{3,1},{4,6},{5,7},{6,4},{7,5},{8,10},{9,11},{10,... | collective-permute-start | bytes 331784 | tf_op jit(solution)/shard_map/ppermute | solution.py:1026
  241.7 12.9 %collective-permute-start.51 = (bf16[23,16,128]{2,1,0:T(8,128)(2,1)S(1)}, bf16[23,16,128]{2,1,0:T(8,128)(2,1)S(1)}, u32[]{:S(2)}, u32[]{:S(2)}) collective-permute-start(bf16[23,16,128]{2,1,0:T(8,128)(2,1)S(1)} %shard_map.294.refs_0_), channel_id=1, source_target_pairs={{0,6},{1,7},{2,4},{3,5},{4,2},{5,3},{6,0},{7,1},{8,14},{9,15},{10,... | collective-permute-start | bytes 282632 | tf_op jit(solution)/shard_map/ppermute | solution.py:1026
  253.3 16.2 %collective-permute-start.58 = (bf16[4,27,16,128]{3,2,1,0:T(8,128)(2,1)S(1)}, bf16[4,27,16,128]{3,2,1,0:T(8,128)(2,1)S(1)}, u32[]{:S(2)}, u32[]{:S(2)}) collective-permute-start(bf16[4,27,16,128]{3,2,1,0:T(8,128)(2,1)S(1)} %shard_map.296.refs_3_), channel_id=1, source_target_pairs={{0,1},{1,0},{2,3},{3,2},{4,5},{5,4},{6,7},{7,6},{8,9},{9,8},{10,11... | collective-permute-start | bytes 1327112 | tf_op jit(solution)/shard_map/ppermute | solution.py:1026
  255.9 13.5 %collective-permute-start.59 = (bf16[4,22,16,128]{3,2,1,0:T(8,128)(2,1)S(1)}, bf16[4,22,16,128]{3,2,1,0:T(8,128)(2,1)S(1)}, u32[]{:S(2)}, u32[]{:S(2)}) collective-permute-start(bf16[4,22,16,128]{3,2,1,0:T(8,128)(2,1)S(1)} %get-tuple-element.211.refs_5_), channel_id=1, source_target_pairs={{0,1},{1,0},{2,3},{3,2},{4,5},{5,4},{6,7},{7,6},{8,9},{9,8},{10,11... | collective-permute-start | bytes 1081352 | tf_op jit(solution)/shard_map/ppermute | solution.py:1026
  (94 other events, 965.9 us)
where the time goes:
time: 279 us; the launch traced here: 277 us
  Pallas kernels  95.6 us (34%)
  waiting for transfers between devices  92.7 us (33%)
  starting transfers between devices  79.1 us (28%)
  local copies, waits for them, and re-layouts  7.84 us (3%)
    pallas_call x26, Pallas kernels, run(): pl.pallas_call(body, out_shape=outs, grid=grid, in_specs=(list(in_specs)...  95.6 us
    ppermute x60, waiting for transfers between devices, shift(): return lax.ppermute(value, axis, [(i, i ^ bit) for i in range(size)])  92.7 us
    ppermute x60, starting transfers between devices, shift(): return lax.ppermute(value, axis, [(i, i ^ bit) for i in range(size)])  79.1 us
    unnamed x117, local copies, waits for them, and re-layouts  7.11 us
  transfers between devices with their start and end apart: 60, of which 24 were waited for; matrix products, arithmetic and copies ran while one was open for 0% of the time, Pallas kernels for 18%

commit v1 on v0

--- a/solution.py
+++ b/solution.py
@@ -84,39 +84,27 @@
     kernel, outs, grid=(), in_specs=None, out_specs=None, scratch=(), us=1, limit=34, after=()
 ):
     def run(*args):
-        count = len(args)
-
-        def body(*refs):
-            kernel(*refs[:count], *refs[count + len(after) :])
-
+        if after:
+            args = (once_ready(args[0], after), *args[1:])
         kw = {} if out_specs is None else {"out_specs": out_specs}
         return pl.pallas_call(
-            body,
+            kernel,
             out_shape=outs,
             grid=grid,
-            in_specs=(list(in_specs) if in_specs else [whole()] * count)
-            + [pl.BlockSpec(memory_space=pl.ANY)] * len(after),
+            in_specs=list(in_specs) if in_specs else [whole()] * len(args),
             scratch_shapes=list(scratch),
             cost_estimate=pl.CostEstimate(
                 flops=int(us * 1.15e9), transcendentals=0, bytes_accessed=1024
             ),
             compiler_params=pltpu.CompilerParams(vmem_limit_bytes=limit * MIB),
             **kw,
-        )(*args, *after)
+        )(*args)
 
     return run
 
 
 def once_ready(value, after):
-    space = pl.BlockSpec(memory_space=pl.ANY)
-    return pl.pallas_call(
-        lambda *refs: None,
-        out_shape=jax.ShapeDtypeStruct(value.shape, value.dtype),
-        in_specs=[space] * (1 + len(after)),
-        out_specs=space,
-        input_output_aliases={0: 0},
-        cost_estimate=pl.CostEstimate(flops=1, transcendentals=0, bytes_accessed=1),
-    )(value, *after)
+    return lax.optimization_barrier((value, *after))[0]
 
 
 def whole():
@@ -1026,10 +1014,12 @@
     return lax.ppermute(value, axis, [(i, i ^ bit) for i in range(size)])
 
 
-def gather_blocks(own, group):
+def gather_blocks(own, group, behind=None):
     blocks = {0: own}
     for j in range(2, group, 2):
         blocks[j] = shift(own, "grp", j)
+    if behind is not None:
+        blocks = behind(blocks)
     for j in range(0, group, 2):
         blocks[j + 1] = shift(blocks[j], "grp", 1)
     return [blocks[j] for j in range(group)]
@@ -1203,19 +1193,6 @@
         limit=62,
     )(samples, cosines, *[wide_weights] * 4, tall[0], query_row, lead, mask)
     first = gather_blocks(first_own, group)
-    second = gather_blocks(second_own, group)
-    late_own = call(
-        pack_late,
-        sds((rows, late_cols), BF16),
-        grid=(1,),
-        in_specs=[columns_of(4), columns_of(5), columns_of(6), whole()],
-        out_specs=whole(),
-        us=2,
-        limit=62,
-        after=(first_own,),
-    )(wide_weights, wide_weights, wide_weights, tall[0])
-    late_blocks = gather_blocks(late_own, group)
-
     by_item = pl.BlockSpec((tokens, D), lambda i: (i, 0))
 
     def lane_block(height):
@@ -1246,6 +1223,23 @@
         us=10,
         limit=34,
     )(fields, mask, *first)
+    second = gather_blocks(
+        second_own,
+        group,
+        lambda blocks: {j: once_ready(block, (gathered,)) for j, block in blocks.items()},
+    )
+    late_own = call(
+        pack_late,
+        sds((rows, late_cols), BF16),
+        grid=(1,),
+        in_specs=[columns_of(4), columns_of(5), columns_of(6), whole()],
+        out_specs=whole(),
+        us=2,
+        limit=62,
+        after=(gathered,),
+    )(wide_weights, wide_weights, wide_weights, tall[0])
+    late_blocks = gather_blocks(late_own, group)
+
     results = call(
         functools.partial(project, group),
         [
@@ -1261,6 +1255,7 @@
         scratch=[pltpu.VMEM((items * HEADS, tokens + tokens // 2, 128), BF16)],
         us=4,
         limit=34,
+        after=(late_own,),
     )(interval, gathered, *second)
     x0, n1, second_weights, mods = results[:4]
     dealt = results[4:]

time: 279 us -> 272 us (0.975)
  waiting for transfers between devices: 92.7 us -> 86.2 us
  starting transfers between devices: 79.1 us -> 82.2 us
    ppermute x60, waiting for transfers between devices: 92.7 us -> 86.2 us  [shift(): return lax.ppermute(value, axis, [(i, i ^ bit) for i in range(size)])]
    ppermute x60, starting transfers between devices: 79.1 us -> 82.2 us  [shift(): return lax.ppermute(value, axis, [(i, i ^ bit) for i in range(size)])]
    unnamed x117 -> x81, local copies, waits for them, and re-layouts: 7.11 us -> 5.27 us
    pallas_call x27 -> x26, Pallas kernels: 95.6 us -> 93.8 us  [run(): pl.pallas_call(kernel, out_shape=outs, grid=grid, in_specs=list(in_specs)...]
where the time goes in v1:
time: 272 us; the launch traced here: 270 us
  Pallas kernels  93.8 us (34%)
  waiting for transfers between devices  86.2 us (32%)
  starting transfers between devices  82.2 us (30%)
  local copies, waits for them, and re-layouts  6 us (2%)
    pallas_call x26, Pallas kernels, run(): pl.pallas_call(kernel, out_shape=outs, grid=grid, in_specs=list(in_specs)...  93.8 us
    ppermute x60, waiting for transfers between devices, shift(): return lax.ppermute(value, axis, [(i, i ^ bit) for i in range(size)])  86.2 us
    ppermute x60, starting transfers between devices, shift(): return lax.ppermute(value, axis, [(i, i ^ bit) for i in range(size)])  82.2 us
  transfers between devices with their start and end apart: 60, of which 24 were waited for; matrix products, arithmetic and copies ran while one was open for 0% of the time, Pallas kernels for 18%

profile of v1, /device:TPU:0, one launch (start us, length us, event | category | flops | bytes accessed | tf_op | source)
XLA Modules:
  0.0 269.7 jit_solution(15367573830744110618)
XLA Ops:
  2.3 3.2 %shard_map.271 = (bf16[96,1920]{1,0:T(8,128)(2,1)}, bf16[128,1536]{1,0:T(8,128)(2,1)}) custom-call(s32[2]{0:T(128)} %refs_1_.2, f32[16]{0:T(128)} %constant.7.clone.refs_1_.refs_2_, f32[96,7632]{1,0:T(8,128)} %refs_7_.1, f32[96,7632]{1,0:T(8,128)} %refs_7_.1, f32[96,7632]{1,0:T(8,128)} %refs_7_.1, f32[96,7632]{1,0:T(8,128)} %refs_7_.1, f32[96,2640]{1,0:T(8,128)} %bitcast.22, ...), custom_call_target="tpu_custom_call" | custom-call | flops 3449999872 | bytes 1024 | tf_op jit(solution)/shard_map/pallas_call | solution.py:90
  8.4 8.8 %collective-permute-done.1.refs_4_ = bf16[96,1920]{1,0:T(8,128)(2,1)S(1)} collective-permute-done((bf16[96,1920]{1,0:T(8,128)(2,1)}, bf16[96,1920]{1,0:T(8,128)(2,1)S(1)}, u32[]{:S(2)}, u32[]{:S(2)}) %collective-permute-start.1) | collective-permute-done | bytes 368672 | tf_op jit(solution)/shard_map/ppermute | solution.py:1014
  19.9 9.5 %shard_map.272 = (f32[2,480,256]{2,1,0:T(8,128)}, bf16[6,2,1104,256]{3,2,1,0:T(8,128)(2,1)}, bf16[512,384]{1,0:T(8,128)(2,1)S(1)}, bf16[384,768]{1,0:T(8,128)(2,...) custom-call(bf16[2,1104,256]{2,1,0:T(8,128)(2,1)S(1)} %bitcast.28, ...), custom_call_target="tpu_custom_call" | custom-call | flops 11500000256 | bytes 1024 | tf_op jit(solution)/shard_map/pallas_call | solution.py:90
  36.1 4.8 %shard_map.274 = (f32[512,384]{1,0:T(8,128)}, bf16[512,384]{1,0:T(8,128)(2,1)}, bf16[384,1536]{1,0:T(8,128)(2,1)}, f32[8,2304]{1,0:T(8,128)}, bf16[1168,128]{1,0...) custom-call(s32[2]{0:T(128)S(1)} %copy-done.16, ...), custom_call_target="tpu_custom_call" | custom-call | flops 4600000000 | bytes 1024 | tf_op jit(solution)/shard_map/pallas_call | solution.py:90
  46.9 8.5 %collective-permute-done.6.refs_1_ = bf16[1168,128]{1,0:T(8,128)(2,1)S(1)} collective-permute-done((bf16[1168,128]{1,0:T(8,128)(2,1)S(1)}, bf16[1168,128]{1,0:T(8,128)(2,1)S(1)}, u32[]{:S(2)}, u32[]{:S(2)}) %collective-permute-start.6) | collective-permute-done | bytes 299040 | tf_op jit(solution)/shard_map/ppermute | solution.py:1014
  57.0 9.2 %collective-permute-done.7.refs_2_ = bf16[1168,128]{1,0:T(8,128)(2,1)S(1)} collective-permute-done((bf16[1168,128]{1,0:T(8,128)(2,1)S(1)}, bf16[1168,128]{1,0:T(8,128)(2,1)S(1)}, u32[]{:S(2)}, u32[]{:S(2)}) %collective-permute-start.7) | collective-permute-done | bytes 299040 | tf_op jit(solution)/shard_map/ppermute | solution.py:1014
  69.0 3.0 %collective-permute-done.11.refs_6_ = bf16[784,128]{1,0:T(8,128)(2,1)S(1)} collective-permute-done((bf16[784,128]{1,0:T(8,128)(2,1)S(1)}, bf16[784,128]{1,0:T(8,128)(2,1)S(1)}, u32[]{:S(2)}, u32[]{:S(2)}) %collective-permute-start.11) | collective-permute-done | bytes 200736 | tf_op jit(solution)/shard_map/ppermute | solution.py:1014
  74.2 9.0 %shard_map.275 = (bf16[3,128,128]{2,1,0:T(8,128)(2,1)S(1)}, bf16[3,128,128]{2,1,0:T(8,128)(2,1)S(1)}, bf16[3,128,128]{2,1,0:T(8,128)(2,1)S(1)}, bf16[3,128,128]{...) custom-call(bf16[1168,128]{1,0:T(8,128)(2,1)S(1)} %get-tuple-element.194.refs_0_, ...), custom_call_target="tpu_custom_call" | custom-call | flops 10350000128 | bytes 1024 | tf_op jit(solution)/shard_map/pallas_call | solution.py:90
  83.2 3.5 %collective-permute-start.13 = (bf16[3,128,128]{2,1,0:T(8,128)(2,1)S(1)}, bf16[3,128,128]{2,1,0:T(8,128)(2,1)S(1)}, u32[]{:S(2)}, u32[]{:S(2)}) collective-permute-start(bf16[3,128,128]{2,1,0:T(8,128)(2,1)S(1)} %get-tuple-element.149), channel_id=1, source_target_pairs={{0,2},{1,3},{2,0},{3,1},{4,6},{5,7},{6,4},{7,5},{8,10},{9,11},{10,... | collective-permute-start | bytes 294920 | tf_op jit(solution)/shard_map/ppermute | solution.py:1014
  89.5 5.3 %collective-permute-done.14.refs_9_ = bf16[3,128,128]{2,1,0:T(8,128)(2,1)S(1)} collective-permute-done((bf16[3,128,128]{2,1,0:T(8,128)(2,1)S(1)}, bf16[3,128,128]{2,1,0:T(8,128)(2,1)S(1)}, u32[]{:S(2)}, u32[]{:S(2)}) %collective-permute-start.14) | collective-permute-done | bytes 98336 | tf_op jit(solution)/shard_map/ppermute | solution.py:1014
  95.6 21.5 %shard_map.276 = (f32[512,384]{1,0:T(8,128)}, f32[2,8,384]{2,1,0:T(8,128)}, f32[8,128]{1,0:T(8,128)}, bf16[3,128,128]{2,1,0:T(8,128)(2,1)S(1)}, bf16[3,128,128]{...) custom-call(s32[2]{0:T(128)S(1)} %copy-done.16, ...), custom_call_target="tpu_custom_call" | custom-call | flops 12650000384 | bytes 1024 | tf_op jit(solution)/shard_map/pallas_call | solution.py:90
  125.1 7.2 %collective-permute-done.20.refs_10_ = bf16[3,128,128]{2,1,0:T(8,128)(2,1)S(1)} collective-permute-done((bf16[3,128,128]{2,1,0:T(8,128)(2,1)S(1)}, bf16[3,128,128]{2,1,0:T(8,128)(2,1)S(1)}, u32[]{:S(2)}, u32[]{:S(2)}) %collective-permute-start.20) | collective-permute-done | bytes 98336 | tf_op jit(solution)/shard_map/ppermute | solution.py:1014
  132.4 5.5 %shard_map.278 = (bf16[1,4,128,128]{3,2,1,0:T(8,128)(2,1)S(1)}, bf16[1,4,256,128]{3,2,1,0:T(8,128)(2,1)S(1)}, bf16[1,4,256,128]{3,2,1,0:T(8,128)(2,1)S(1)}) custom-call(bf16[1168,128]{1,0:T(8,128)(2,1)S(1)} %get-tuple-element.194.refs_0_, bf16[1168,128]{1,0:T(8,128)(2,1)S(1)} %collective-permute-done.6.refs_1_, ...), custom_call_target="tpu_custom_call" | custom-call | flops 6899999744 | bytes 1024 | tf_op jit(solution)/shard_map/pallas_call | solution.py:90
  139.4 5.9 %shard_map.279 = (bf16[1,4,128,128]{3,2,1,0:T(8,128)(2,1)S(1)}, bf16[1,4,256,128]{3,2,1,0:T(8,128)(2,1)S(1)}, bf16[1,4,256,128]{3,2,1,0:T(8,128)(2,1)S(1)}) custom-call(bf16[1168,128]{1,0:T(8,128)(2,1)S(1)} %get-tuple-element.194.refs_0_, bf16[1168,128]{1,0:T(8,128)(2,1)S(1)} %collective-permute-done.6.refs_1_, ...), custom_call_target="tpu_custom_call" | custom-call | flops 6899999744 | bytes 1024 | tf_op jit(solution)/shard_map/pallas_call | solution.py:90
  151.5 5.5 %shard_map.284 = (bf16[1,4,128,128]{3,2,1,0:T(8,128)(2,1)S(1)}, bf16[1,4,256,128]{3,2,1,0:T(8,128)(2,1)S(1)}, bf16[1,4,256,128]{3,2,1,0:T(8,128)(2,1)S(1)}) custom-call(bf16[1168,128]{1,0:T(8,128)(2,1)S(1)} %get-tuple-element.194.refs_0_, bf16[1168,128]{1,0:T(8,128)(2,1)S(1)} %collective-permute-done.6.refs_1_, ...), custom_call_target="tpu_custom_call" | custom-call | flops 6899999744 | bytes 1024 | tf_op jit(solution)/shard_map/pallas_call | solution.py:90
  167.4 3.3 %collective-permute-done.25.refs_1_ = bf16[216,16,128]{2,1,0:T(8,128)(2,1)S(1)} collective-permute-done((bf16[216,16,128]{2,1,0:T(8,128)(2,1)S(1)}, bf16[216,16,128]{2,1,0:T(8,128)(2,1)S(1)}, u32[]{:S(2)}, u32[]{:S(2)}) %collective-permute-start.25) | collective-permute-done | bytes 884768 | tf_op jit(solution)/shard_map/ppermute | solution.py:1014
  178.2 4.0 %shard_map.286 = (bf16[2,384,256]{2,1,0:T(8,128)(2,1)S(1)}, bf16[2,96,1664]{2,1,0:T(8,128)(2,1)S(1)}, bf16[2,96,1664]{2,1,0:T(8,128)(2,1)S(1)}) custom-call(s32[2]{0:T(128)S(1)} %copy-done.16, f32[512,384]{1,0:T(8,128)S(1)} %copy-done.20, bf16[512,384]{1,0:T(8,128)(2,1)S(1)} %copy-done.26, f32[512,384]{1,0:T(8,128)S(1)} %copy-done.21, ...), custom_call_target="tpu_custom_call" | custom-call | flops 4600000000 | bytes 1024 | tf_op jit(solution)/shard_map/pallas_call | solution.py:90
  184.1 9.2 %shard_map.288 = (bf16[2,96,1920]{2,1,0:T(8,128)(2,1)S(1)}, bf16[2,96,1920]{2,1,0:T(8,128)(2,1)S(1)}) custom-call(bf16[2,384,256]{2,1,0:T(8,128)(2,1)S(1)} %get-tuple-element.207.refs_0_, f32[2,480,256]{2,1,0:T(8,128)S(1)} %copy-done.27, bf16[6,2,1104,256]{3,2,1,0:T(8,128)(2,1)S(1)} %bitcast.35, bf16[2,1104,256]{2,1,0:T(8,128)(2,1)S(1)} %bitcast.29, ...), custom_call_target="tpu_custom_call" | custom-call | flops 14949999616 | bytes 1024 | tf_op jit(solution)/shard_map/pallas_call | solution.py:90
  198.6 9.1 %collective-permute-done.42.refs_1_ = bf16[88,16,128]{2,1,0:T(8,128)(2,1)S(1)} collective-permute-done((bf16[88,16,128]{2,1,0:T(8,128)(2,1)S(1)}, bf16[88,16,128]{2,1,0:T(8,128)(2,1)S(1)}, u32[]{:S(2)}, u32[]{:S(2)}) %collective-permute-start.42) | collective-permute-done | bytes 360480 | tf_op jit(solution)/shard_map/ppermute | solution.py:1014
  220.8 3.4 %collective-permute-done.38.refs_2_ = bf16[27,16,128]{2,1,0:T(8,128)(2,1)S(1)} collective-permute-done((bf16[27,16,128]{2,1,0:T(8,128)(2,1)S(1)}, bf16[27,16,128]{2,1,0:T(8,128)(2,1)S(1)}, u32[]{:S(2)}, u32[]{:S(2)}) %collective-permute-start.38) | collective-permute-done | bytes 110624 | tf_op jit(solution)/shard_map/ppermute | solution.py:1014
  224.3 5.0 %collective-permute-start.57 = (bf16[27,16,128]{2,1,0:T(8,128)(2,1)S(1)}, bf16[27,16,128]{2,1,0:T(8,128)(2,1)S(1)}, u32[]{:S(2)}, u32[]{:S(2)}) collective-permute-start(bf16[27,16,128]{2,1,0:T(8,128)(2,1)S(1)} %get-tuple-element.238.refs_0_), channel_id=1, source_target_pairs={{0,6},{1,7},{2,4},{3,5},{4,2},{5,3},{6,0},{7,1},{8,14},{9,15},{10,... | collective-permute-start | bytes 331784 | tf_op jit(solution)/shard_map/ppermute | solution.py:1014
  234.3 7.1 %collective-permute-start.50 = (bf16[23,16,128]{2,1,0:T(8,128)(2,1)S(1)}, bf16[23,16,128]{2,1,0:T(8,128)(2,1)S(1)}, u32[]{:S(2)}, u32[]{:S(2)}) collective-permute-start(bf16[23,16,128]{2,1,0:T(8,128)(2,1)S(1)} %shard_map.293.refs_0_), channel_id=1, source_target_pairs={{0,4},{1,5},{2,6},{3,7},{4,0},{5,1},{6,2},{7,3},{8,12},{9,13},{10,... | collective-permute-start | bytes 282632 | tf_op jit(solution)/shard_map/ppermute | solution.py:1014
  255.4 6.7 %collective-permute-done.54 = f32[8,128]{1,0:T(8,128)S(1)} collective-permute-done((f32[8,128]{1,0:T(8,128)S(1)}, f32[8,128]{1,0:T(8,128)S(1)}, u32[]{:S(2)}, u32[]{:S(2)}) %collective-permute-start.54) | collective-permute-done | bytes 4128 | tf_op jit(solution)/shard_map/ppermute | solution.py:1014
  262.2 7.3 %shard_map.296 = (f32[1,1]{1,0:T(1,128)}, f32[1,1]{1,0:T(1,128)}, f32[1,1]{1,0:T(1,128)}, f32[96,7632]{1,0:T(8,128)}, f32[96,7632]{1,0:T(8,128)}, /*index=5*/f32...) custom-call(f32[8,128]{1,0:T(8,128)S(1)} %add.13.refs_0_, ...), custom_call_target="tpu_custom_call" | custom-call | flops 11500000256 | bytes 1024 | tf_op jit(solution)/shard_map/pallas_call | solution.py:90
  (212 shorter events, 102.6 us)
Async XLA Ops:
  17.2 13.0 %collective-permute-start.4 = (bf16[128,1536]{1,0:T(8,128)(2,1)}, bf16[128,1536]{1,0:T(8,128)(2,1)}, u32[]{:S(2)}, u32[]{:S(2)}) collective-permute-start(bf16[128,1536]{1,0:T(8,128)(2,1)} %get-tuple-element.140.refs_2_), channel_id=1, source_target_pairs={{0,16},{8,24},{16,0},{24,8},{1,17},{9,25},{17,1},{25,9},{2,18},{10... | collective-permute-start | bytes 1179656 | tf_op jit(solution)/shard_map/ppermute | solution.py:1014
  33.4 35.1 %collective-permute-start.17 = (bf16[96,4608]{1,0:T(8,128)(2,1)}, bf16[96,4608]{1,0:T(8,128)(2,1)S(1)}, u32[]{:S(2)}, u32[]{:S(2)}) collective-permute-start(bf16[96,4608]{1,0:T(8,128)(2,1)} %shard_map.273.refs_11_), channel_id=1, source_target_pairs={{0,16},{8,24},{16,0},{24,8},{1,17},{9,25},{17,1},{25,9},{2,18},{10... | collective-permute-start | bytes 2654216 | tf_op jit(solution)/shard_map/ppermute | solution.py:1014
  40.9 14.6 %collective-permute-start.6 = (bf16[1168,128]{1,0:T(8,128)(2,1)S(1)}, bf16[1168,128]{1,0:T(8,128)(2,1)S(1)}, u32[]{:S(2)}, u32[]{:S(2)}) collective-permute-start(bf16[1168,128]{1,0:T(8,128)(2,1)S(1)} %get-tuple-element.143), channel_id=1, source_target_pairs={{0,2},{1,3},{2,0},{3,1},{4,6},{5,7},{6,4},{7,5},{8,10},{9,11},{10,... | collective-permute-start | bytes 897032 | tf_op jit(solution)/shard_map/ppermute | solution.py:1014
  42.5 23.7 %collective-permute-start.7 = (bf16[1168,128]{1,0:T(8,128)(2,1)S(1)}, bf16[1168,128]{1,0:T(8,128)(2,1)S(1)}, u32[]{:S(2)}, u32[]{:S(2)}) collective-permute-start(bf16[1168,128]{1,0:T(8,128)(2,1)S(1)} %get-tuple-element.144), channel_id=1, source_target_pairs={{0,4},{1,5},{2,6},{3,7},{4,0},{5,1},{6,2},{7,3},{8,12},{9,13},{10,... | collective-permute-start | bytes 897032 | tf_op jit(solution)/shard_map/ppermute | solution.py:1014
  45.1 22.8 %collective-permute-start.8 = (bf16[1168,128]{1,0:T(8,128)(2,1)S(1)}, bf16[1168,128]{1,0:T(8,128)(2,1)S(1)}, u32[]{:S(2)}, u32[]{:S(2)}) collective-permute-start(bf16[1168,128]{1,0:T(8,128)(2,1)S(1)} %get-tuple-element.145), channel_id=1, source_target_pairs={{0,6},{1,7},{2,4},{3,5},{4,2},{5,3},{6,0},{7,1},{8,14},{9,15},{10,... | collective-permute-start | bytes 897032 | tf_op jit(solution)/shard_map/ppermute | solution.py:1014
  45.3 23.1 %collective-permute-start.9 = (bf16[784,128]{1,0:T(8,128)(2,1)S(1)}, bf16[784,128]{1,0:T(8,128)(2,1)S(1)}, u32[]{:S(2)}, u32[]{:S(2)}) collective-permute-start(bf16[784,128]{1,0:T(8,128)(2,1)S(1)} %slice.12), channel_id=1, source_target_pairs={{0,1},{1,0},{2,3},{3,2},{4,5},{5,4},{6,7},{7,6},{8,9},{9,8},{10,11... | collective-permute-start | bytes 602120 | tf_op jit(solution)/shard_map/ppermute | solution.py:1014
  55.5 13.6 %collective-permute-start.10 = (bf16[784,128]{1,0:T(8,128)(2,1)S(1)}, bf16[784,128]{1,0:T(8,128)(2,1)S(1)}, u32[]{:S(2)}, u32[]{:S(2)}) collective-permute-start(bf16[784,128]{1,0:T(8,128)(2,1)S(1)} %slice.16), channel_id=1, source_target_pairs={{0,1},{1,0},{2,3},{3,2},{4,5},{5,4},{6,7},{7,6},{8,9},{9,8},{10,11... | collective-permute-start | bytes 602120 | tf_op jit(solution)/shard_map/ppermute | solution.py:1014
  68.5 20.7 %collective-permute-start.16 = (bf16[96,4608]{1,0:T(8,128)(2,1)S(1)}, bf16[96,4608]{1,0:T(8,128)(2,1)S(1)}, u32[]{:S(2)}, u32[]{:S(2)}) collective-permute-start(bf16[96,4608]{1,0:T(8,128)(2,1)S(1)} %copy-done.2), channel_id=1, source_target_pairs={{0,8},{8,0},{16,24},{24,16},{1,9},{9,1},{17,25},{25,17},{2,10},{10... | collective-permute-start | bytes 2654216 | tf_op jit(solution)/shard_map/ppermute | solution.py:1014
  68.5 26.4 %collective-permute-start.18 = (bf16[96,4608]{1,0:T(8,128)(2,1)S(1)}, bf16[96,4608]{1,0:T(8,128)(2,1)S(1)}, u32[]{:S(2)}, u32[]{:S(2)}) collective-permute-start(bf16[96,4608]{1,0:T(8,128)(2,1)S(1)} %collective-permute-done.17.refs_13_), channel_id=1, source_target_pairs={{0,8},{8,0},{16,24},{24,16},{1,9},{9,1},{17,25},{25,17},{2,10},{10... | collective-permute-start | bytes 2654216 | tf_op jit(solution)/shard_map/ppermute | solution.py:1014
  119.9 30.6 %collective-permute-start.22 = (bf16[2,96,4608]{2,1,0:T(8,128)(2,1)S(1)}, bf16[2,96,4608]{2,1,0:T(8,128)(2,1)S(1)}, u32[]{:S(2)}, u32[]{:S(2)}) collective-permute-start(bf16[2,96,4608]{2,1,0:T(8,128)(2,1)S(1)} %get-tuple-element.173), channel_id=1, source_target_pairs={{0,8},{8,0},{16,24},{24,16},{1,9},{9,1},{17,25},{25,17},{2,10},{10... | collective-permute-start | bytes 5308424 | tf_op jit(solution)/shard_map/ppermute | solution.py:1014
  145.3 13.5 %collective-permute-start.23 = (bf16[1,4,256,128]{3,2,1,0:T(8,128)(2,1)S(1)}, bf16[1,4,256,128]{3,2,1,0:T(8,128)(2,1)S(1)}, u32[]{:S(2)}, u32[]{:S(2)}) collective-permute-start(bf16[1,4,256,128]{3,2,1,0:T(8,128)(2,1)S(1)} %get-tuple-element.176), channel_id=1, source_target_pairs={{0,1},{1,0},{2,3},{3,2},{4,5},{5,4},{6,7},{7,6},{8,9},{9,8},{10,11... | collective-permute-start | bytes 786440 | tf_op jit(solution)/shard_map/ppermute | solution.py:1014
  150.9 19.8 %collective-permute-start.25 = (bf16[216,16,128]{2,1,0:T(8,128)(2,1)S(1)}, bf16[216,16,128]{2,1,0:T(8,128)(2,1)S(1)}, u32[]{:S(2)}, u32[]{:S(2)}) collective-permute-start(bf16[216,16,128]{2,1,0:T(8,128)(2,1)S(1)} %get-tuple-element.179), channel_id=1, source_target_pairs={{0,16},{8,24},{16,0},{24,8},{1,17},{9,25},{17,1},{25,9},{2,18},{10... | collective-permute-start | bytes 2654216 | tf_op jit(solution)/shard_map/ppermute | solution.py:1014
  160.5 13.2 %collective-permute-start.30 = (bf16[384,128]{1,0:T(8,128)(2,1)S(1)}, bf16[384,128]{1,0:T(8,128)(2,1)S(1)}, u32[]{:S(2)}, u32[]{:S(2)}) collective-permute-start(bf16[384,128]{1,0:T(8,128)(2,1)S(1)} %get-tuple-element.192), channel_id=1, source_target_pairs={{0,4},{1,5},{2,6},{3,7},{4,0},{5,1},{6,2},{7,3},{8,12},{9,13},{10,... | collective-permute-start | bytes 294920 | tf_op jit(solution)/shard_map/ppermute | solution.py:1014
  161.5 13.8 %collective-permute-start.31 = (bf16[384,128]{1,0:T(8,128)(2,1)S(1)}, bf16[384,128]{1,0:T(8,128)(2,1)S(1)}, u32[]{:S(2)}, u32[]{:S(2)}) collective-permute-start(bf16[384,128]{1,0:T(8,128)(2,1)S(1)} %get-tuple-element.193), channel_id=1, source_target_pairs={{0,6},{1,7},{2,4},{3,5},{4,2},{5,3},{6,0},{7,1},{8,14},{9,15},{10,... | collective-permute-start | bytes 294920 | tf_op jit(solution)/shard_map/ppermute | solution.py:1014
  215.2 16.5 %collective-permute-start.46 = (bf16[22,16,128]{2,1,0:T(8,128)(2,1)S(1)}, bf16[22,16,128]{2,1,0:T(8,128)(2,1)S(1)}, u32[]{:S(2)}, u32[]{:S(2)}) collective-permute-start(bf16[22,16,128]{2,1,0:T(8,128)(2,1)S(1)} %get-tuple-element.233), channel_id=1, source_target_pairs={{0,2},{1,3},{2,0},{3,1},{4,6},{5,7},{6,4},{7,5},{8,10},{9,11},{10,... | collective-permute-start | bytes 270344 | tf_op jit(solution)/shard_map/ppermute | solution.py:1014
  216.3 17.5 %collective-permute-start.47 = (bf16[22,16,128]{2,1,0:T(8,128)(2,1)S(1)}, bf16[22,16,128]{2,1,0:T(8,128)(2,1)S(1)}, u32[]{:S(2)}, u32[]{:S(2)}) collective-permute-start(bf16[22,16,128]{2,1,0:T(8,128)(2,1)S(1)} %get-tuple-element.234), channel_id=1, source_target_pairs={{0,4},{1,5},{2,6},{3,7},{4,0},{5,1},{6,2},{7,3},{8,12},{9,13},{10,... | collective-permute-start | bytes 270344 | tf_op jit(solution)/shard_map/ppermute | solution.py:1014
  218.1 15.7 %collective-permute-start.48 = (bf16[22,16,128]{2,1,0:T(8,128)(2,1)S(1)}, bf16[22,16,128]{2,1,0:T(8,128)(2,1)S(1)}, u32[]{:S(2)}, u32[]{:S(2)}) collective-permute-start(bf16[22,16,128]{2,1,0:T(8,128)(2,1)S(1)} %get-tuple-element.235), channel_id=1, source_target_pairs={{0,6},{1,7},{2,4},{3,5},{4,2},{5,3},{6,0},{7,1},{8,14},{9,15},{10,... | collective-permute-start | bytes 270344 | tf_op jit(solution)/shard_map/ppermute | solution.py:1014
  224.3 17.1 %collective-permute-start.57 = (bf16[27,16,128]{2,1,0:T(8,128)(2,1)S(1)}, bf16[27,16,128]{2,1,0:T(8,128)(2,1)S(1)}, u32[]{:S(2)}, u32[]{:S(2)}) collective-permute-start(bf16[27,16,128]{2,1,0:T(8,128)(2,1)S(1)} %get-tuple-element.238.refs_0_), channel_id=1, source_target_pairs={{0,6},{1,7},{2,4},{3,5},{4,2},{5,3},{6,0},{7,1},{8,14},{9,15},{10,... | collective-permute-start | bytes 331784 | tf_op jit(solution)/shard_map/ppermute | solution.py:1014
  229.2 16.6 %collective-permute-start.56 = (bf16[27,16,128]{2,1,0:T(8,128)(2,1)S(1)}, bf16[27,16,128]{2,1,0:T(8,128)(2,1)S(1)}, u32[]{:S(2)}, u32[]{:S(2)}) collective-permute-start(bf16[27,16,128]{2,1,0:T(8,128)(2,1)S(1)} %get-tuple-element.238.refs_0_), channel_id=1, source_target_pairs={{0,4},{1,5},{2,6},{3,7},{4,0},{5,1},{6,2},{7,3},{8,12},{9,13},{10,... | collective-permute-start | bytes 331784 | tf_op jit(solution)/shard_map/ppermute | solution.py:1014
  231.7 14.1 %collective-permute-start.55 = (bf16[27,16,128]{2,1,0:T(8,128)(2,1)S(1)}, bf16[27,16,128]{2,1,0:T(8,128)(2,1)S(1)}, u32[]{:S(2)}, u32[]{:S(2)}) collective-permute-start(bf16[27,16,128]{2,1,0:T(8,128)(2,1)S(1)} %get-tuple-element.238.refs_0_), channel_id=1, source_target_pairs={{0,2},{1,3},{2,0},{3,1},{4,6},{5,7},{6,4},{7,5},{8,10},{9,11},{10,... | collective-permute-start | bytes 331784 | tf_op jit(solution)/shard_map/ppermute | solution.py:1014
  234.2 13.2 %collective-permute-start.51 = (bf16[23,16,128]{2,1,0:T(8,128)(2,1)S(1)}, bf16[23,16,128]{2,1,0:T(8,128)(2,1)S(1)}, u32[]{:S(2)}, u32[]{:S(2)}) collective-permute-start(bf16[23,16,128]{2,1,0:T(8,128)(2,1)S(1)} %shard_map.293.refs_0_), channel_id=1, source_target_pairs={{0,6},{1,7},{2,4},{3,5},{4,2},{5,3},{6,0},{7,1},{8,14},{9,15},{10,... | collective-permute-start | bytes 282632 | tf_op jit(solution)/shard_map/ppermute | solution.py:1014
  234.3 14.2 %collective-permute-start.50 = (bf16[23,16,128]{2,1,0:T(8,128)(2,1)S(1)}, bf16[23,16,128]{2,1,0:T(8,128)(2,1)S(1)}, u32[]{:S(2)}, u32[]{:S(2)}) collective-permute-start(bf16[23,16,128]{2,1,0:T(8,128)(2,1)S(1)} %shard_map.293.refs_0_), channel_id=1, source_target_pairs={{0,4},{1,5},{2,6},{3,7},{4,0},{5,1},{6,2},{7,3},{8,12},{9,13},{10,... | collective-permute-start | bytes 282632 | tf_op jit(solution)/shard_map/ppermute | solution.py:1014
  245.9 16.2 %collective-permute-start.58 = (bf16[4,27,16,128]{3,2,1,0:T(8,128)(2,1)S(1)}, bf16[4,27,16,128]{3,2,1,0:T(8,128)(2,1)S(1)}, u32[]{:S(2)}, u32[]{:S(2)}) collective-permute-start(bf16[4,27,16,128]{3,2,1,0:T(8,128)(2,1)S(1)} %shard_map.295.refs_3_), channel_id=1, source_target_pairs={{0,1},{1,0},{2,3},{3,2},{4,5},{5,4},{6,7},{7,6},{8,9},{9,8},{10,11... | collective-permute-start | bytes 1327112 | tf_op jit(solution)/shard_map/ppermute | solution.py:1014
  248.5 13.6 %collective-permute-start.59 = (bf16[4,22,16,128]{3,2,1,0:T(8,128)(2,1)S(1)}, bf16[4,22,16,128]{3,2,1,0:T(8,128)(2,1)S(1)}, u32[]{:S(2)}, u32[]{:S(2)}) collective-permute-start(bf16[4,22,16,128]{3,2,1,0:T(8,128)(2,1)S(1)} %get-tuple-element.239.refs_5_), channel_id=1, source_target_pairs={{0,1},{1,0},{2,3},{3,2},{4,5},{5,4},{6,7},{7,6},{8,9},{9,8},{10,11... | collective-permute-start | bytes 1081352 | tf_op jit(solution)/shard_map/ppermute | solution.py:1014
  (76 other events, 802.1 us)

commit v2 on v1

--- a/solution.py
+++ b/solution.py
@@ -1113,9 +1113,12 @@
     return [first] + [shift(sent[m - 1], "seq", m * shares) for m in range(1, CUTS)]
 
 
-def gather_shares(pieces, after=()):
+def stacked(pieces):
+    return call(stack, sds((CUTS,) + pieces[0].shape, BF16))(*pieces)
+
+
+def over_shares(column):
     shares = lax.axis_size("seq") // CUTS
-    column = call(stack, sds((CUTS,) + pieces[0].shape, BF16), after=after)(*pieces)
     return [column] + [shift(column, "seq", n) for n in range(1, shares)]
 
 
@@ -1449,23 +1452,26 @@
     )(*early_pieces)
     early_column = over_cuts(early_piece)
     late_first = reduce_cores(
-        (late_keep, shift(late_send, "grp", 1)),
+        (late_keep, shift(once_ready(late_send, (early_piece,)), "grp", 1)),
         (second_keep, second_got),
     )
     late_second = reduce_once(*exchange_once(*late_first))
-    early_all = gather_shares(early_column, after=(late_second[0][0],))
-    late_third = reduce_twice(*exchange_again(*late_second))
+    early_column = stacked(early_column)
+    late_second = [[once_ready(x, (early_column,)) for x in side] for side in late_second]
+    late_twice = exchange_again(*late_second)
+    early_all = over_shares(once_ready(early_column, (late_twice[0][1], late_twice[1][1])))
+    late_third = reduce_twice(*late_twice)
     late_pieces = over_cuts(late_third[0], late_third[1:])
     start = (rows // 16) * 27
     stop = (rows // 16) * (27 + mod_tiles(rows))
     count = late_pieces[0].shape[0]
     late_piece = call(
-        functools.partial(sum_late, start, stop), piece_shape(count + 1)
+        functools.partial(sum_late, start, stop), piece_shape(count + 1), after=early_all[1:]
     )(early_squares, loss, lead, *late_pieces)
     late_column, reduced = call(
         stack_late, [sds((CUTS, count, 16, 128), BF16), sds((8, 128), F32)]
     )(*over_cuts(late_piece))
-    late_all = [late_column] + [shift(late_column, "seq", n) for n in range(1, shares)]
+    late_all = over_shares(late_column)
     reduced = butterfly(reduced, "grp", 1, group)
     reduced = butterfly(reduced, "seq", 1, shares)
 

time: 272 us -> 262 us (0.963)
  starting transfers between devices: 82.2 us -> 73.8 us
    ppermute x60, starting transfers between devices: 82.2 us -> 73.8 us  [shift(): return lax.ppermute(value, axis, [(i, i ^ bit) for i in range(size)])]
  transfers between devices with their start and end apart: 60 -> 60, of which waited for: 24 -> 25; matrix products, arithmetic and copies ran while one was open for 0% -> 0% of each run, Pallas kernels for 18% -> 22%
where the time goes in v2:
time: 262 us; the launch traced here: 260 us
  Pallas kernels  93.8 us (36%)
  waiting for transfers between devices  85.3 us (33%)
  starting transfers between devices  73.8 us (28%)
  local copies, waits for them, and re-layouts  5.21 us (2%)
    pallas_call x26, Pallas kernels, run(): pl.pallas_call(kernel, out_shape=outs, grid=grid, in_specs=list(in_specs)...  93.8 us
    ppermute x60, waiting for transfers between devices, shift(): return lax.ppermute(value, axis, [(i, i ^ bit) for i in range(size)])  85.3 us
    ppermute x60, starting transfers between devices, shift(): return lax.ppermute(value, axis, [(i, i ^ bit) for i in range(size)])  73.8 us
  transfers between devices with their start and end apart: 60, of which 25 were waited for; matrix products, arithmetic and copies ran while one was open for 0% of the time, Pallas kernels for 22%

profile of v2, /device:TPU:0, one launch (start us, length us, event | category | flops | bytes accessed | tf_op | source)
XLA Modules:
  0.0 259.6 jit_solution(5142495102443397549)
XLA Ops:
  2.3 3.2 %shard_map.271 = (bf16[96,1920]{1,0:T(8,128)(2,1)}, bf16[128,1536]{1,0:T(8,128)(2,1)}) custom-call(s32[2]{0:T(128)} %refs_1_.2, f32[16]{0:T(128)} %constant.7.clone.refs_1_.refs_2_, f32[96,7632]{1,0:T(8,128)} %refs_7_.1, f32[96,7632]{1,0:T(8,128)} %refs_7_.1, f32[96,7632]{1,0:T(8,128)} %refs_7_.1, f32[96,7632]{1,0:T(8,128)} %refs_7_.1, f32[96,2640]{1,0:T(8,128)} %bitcast.22, ...), custom_call_target="tpu_custom_call" | custom-call | flops 3449999872 | bytes 1024 | tf_op jit(solution)/shard_map/pallas_call | solution.py:90
  8.4 8.8 %collective-permute-done.1.refs_4_ = bf16[96,1920]{1,0:T(8,128)(2,1)S(1)} collective-permute-done((bf16[96,1920]{1,0:T(8,128)(2,1)}, bf16[96,1920]{1,0:T(8,128)(2,1)S(1)}, u32[]{:S(2)}, u32[]{:S(2)}) %collective-permute-start.1) | collective-permute-done | bytes 368672 | tf_op jit(solution)/shard_map/ppermute | solution.py:1014
  19.9 9.5 %shard_map.272 = (f32[2,480,256]{2,1,0:T(8,128)}, bf16[6,2,1104,256]{3,2,1,0:T(8,128)(2,1)}, bf16[512,384]{1,0:T(8,128)(2,1)S(1)}, bf16[384,768]{1,0:T(8,128)(2,...) custom-call(bf16[2,1104,256]{2,1,0:T(8,128)(2,1)S(1)} %bitcast.28, ...), custom_call_target="tpu_custom_call" | custom-call | flops 11500000256 | bytes 1024 | tf_op jit(solution)/shard_map/pallas_call | solution.py:90
  36.1 4.8 %shard_map.274 = (f32[512,384]{1,0:T(8,128)}, bf16[512,384]{1,0:T(8,128)(2,1)}, bf16[384,1536]{1,0:T(8,128)(2,1)}, f32[8,2304]{1,0:T(8,128)}, bf16[1168,128]{1,0...) custom-call(s32[2]{0:T(128)S(1)} %copy-done.16, ...), custom_call_target="tpu_custom_call" | custom-call | flops 4600000000 | bytes 1024 | tf_op jit(solution)/shard_map/pallas_call | solution.py:90
  46.9 8.5 %collective-permute-done.6.refs_1_ = bf16[1168,128]{1,0:T(8,128)(2,1)S(1)} collective-permute-done((bf16[1168,128]{1,0:T(8,128)(2,1)S(1)}, bf16[1168,128]{1,0:T(8,128)(2,1)S(1)}, u32[]{:S(2)}, u32[]{:S(2)}) %collective-permute-start.6) | collective-permute-done | bytes 299040 | tf_op jit(solution)/shard_map/ppermute | solution.py:1014
  57.0 9.2 %collective-permute-done.7.refs_2_ = bf16[1168,128]{1,0:T(8,128)(2,1)S(1)} collective-permute-done((bf16[1168,128]{1,0:T(8,128)(2,1)S(1)}, bf16[1168,128]{1,0:T(8,128)(2,1)S(1)}, u32[]{:S(2)}, u32[]{:S(2)}) %collective-permute-start.7) | collective-permute-done | bytes 299040 | tf_op jit(solution)/shard_map/ppermute | solution.py:1014
  69.0 3.0 %collective-permute-done.11.refs_6_ = bf16[784,128]{1,0:T(8,128)(2,1)S(1)} collective-permute-done((bf16[784,128]{1,0:T(8,128)(2,1)S(1)}, bf16[784,128]{1,0:T(8,128)(2,1)S(1)}, u32[]{:S(2)}, u32[]{:S(2)}) %collective-permute-start.11) | collective-permute-done | bytes 200736 | tf_op jit(solution)/shard_map/ppermute | solution.py:1014
  74.2 9.0 %shard_map.275 = (bf16[3,128,128]{2,1,0:T(8,128)(2,1)S(1)}, bf16[3,128,128]{2,1,0:T(8,128)(2,1)S(1)}, bf16[3,128,128]{2,1,0:T(8,128)(2,1)S(1)}, bf16[3,128,128]{...) custom-call(bf16[1168,128]{1,0:T(8,128)(2,1)S(1)} %get-tuple-element.200.refs_0_, ...), custom_call_target="tpu_custom_call" | custom-call | flops 10350000128 | bytes 1024 | tf_op jit(solution)/shard_map/pallas_call | solution.py:90
  83.2 3.5 %collective-permute-start.13 = (bf16[3,128,128]{2,1,0:T(8,128)(2,1)S(1)}, bf16[3,128,128]{2,1,0:T(8,128)(2,1)S(1)}, u32[]{:S(2)}, u32[]{:S(2)}) collective-permute-start(bf16[3,128,128]{2,1,0:T(8,128)(2,1)S(1)} %get-tuple-element.155), channel_id=1, source_target_pairs={{0,2},{1,3},{2,0},{3,1},{4,6},{5,7},{6,4},{7,5},{8,10},{9,11},{10,... | collective-permute-start | bytes 294920 | tf_op jit(solution)/shard_map/ppermute | solution.py:1014
  89.5 5.3 %collective-permute-done.14.refs_9_ = bf16[3,128,128]{2,1,0:T(8,128)(2,1)S(1)} collective-permute-done((bf16[3,128,128]{2,1,0:T(8,128)(2,1)S(1)}, bf16[3,128,128]{2,1,0:T(8,128)(2,1)S(1)}, u32[]{:S(2)}, u32[]{:S(2)}) %collective-permute-start.14) | collective-permute-done | bytes 98336 | tf_op jit(solution)/shard_map/ppermute | solution.py:1014
  95.6 21.5 %shard_map.276 = (f32[512,384]{1,0:T(8,128)}, f32[2,8,384]{2,1,0:T(8,128)}, f32[8,128]{1,0:T(8,128)}, bf16[3,128,128]{2,1,0:T(8,128)(2,1)S(1)}, bf16[3,128,128]{...) custom-call(s32[2]{0:T(128)S(1)} %copy-done.16, ...), custom_call_target="tpu_custom_call" | custom-call | flops 12650000384 | bytes 1024 | tf_op jit(solution)/shard_map/pallas_call | solution.py:90
  125.1 7.2 %collective-permute-done.20.refs_10_ = bf16[3,128,128]{2,1,0:T(8,128)(2,1)S(1)} collective-permute-done((bf16[3,128,128]{2,1,0:T(8,128)(2,1)S(1)}, bf16[3,128,128]{2,1,0:T(8,128)(2,1)S(1)}, u32[]{:S(2)}, u32[]{:S(2)}) %collective-permute-start.20) | collective-permute-done | bytes 98336 | tf_op jit(solution)/shard_map/ppermute | solution.py:1014
  132.4 5.5 %shard_map.278 = (bf16[1,4,128,128]{3,2,1,0:T(8,128)(2,1)S(1)}, bf16[1,4,256,128]{3,2,1,0:T(8,128)(2,1)S(1)}, bf16[1,4,256,128]{3,2,1,0:T(8,128)(2,1)S(1)}) custom-call(bf16[1168,128]{1,0:T(8,128)(2,1)S(1)} %get-tuple-element.200.refs_0_, bf16[1168,128]{1,0:T(8,128)(2,1)S(1)} %collective-permute-done.6.refs_1_, ...), custom_call_target="tpu_custom_call" | custom-call | flops 6899999744 | bytes 1024 | tf_op jit(solution)/shard_map/pallas_call | solution.py:90
  139.4 5.9 %shard_map.279 = (bf16[1,4,128,128]{3,2,1,0:T(8,128)(2,1)S(1)}, bf16[1,4,256,128]{3,2,1,0:T(8,128)(2,1)S(1)}, bf16[1,4,256,128]{3,2,1,0:T(8,128)(2,1)S(1)}) custom-call(bf16[1168,128]{1,0:T(8,128)(2,1)S(1)} %get-tuple-element.200.refs_0_, bf16[1168,128]{1,0:T(8,128)(2,1)S(1)} %collective-permute-done.6.refs_1_, ...), custom_call_target="tpu_custom_call" | custom-call | flops 6899999744 | bytes 1024 | tf_op jit(solution)/shard_map/pallas_call | solution.py:90
  151.5 5.5 %shard_map.284 = (bf16[1,4,128,128]{3,2,1,0:T(8,128)(2,1)S(1)}, bf16[1,4,256,128]{3,2,1,0:T(8,128)(2,1)S(1)}, bf16[1,4,256,128]{3,2,1,0:T(8,128)(2,1)S(1)}) custom-call(bf16[1168,128]{1,0:T(8,128)(2,1)S(1)} %get-tuple-element.200.refs_0_, bf16[1168,128]{1,0:T(8,128)(2,1)S(1)} %collective-permute-done.6.refs_1_, ...), custom_call_target="tpu_custom_call" | custom-call | flops 6899999744 | bytes 1024 | tf_op jit(solution)/shard_map/pallas_call | solution.py:90
  167.4 3.3 %collective-permute-done.25.refs_1_ = bf16[216,16,128]{2,1,0:T(8,128)(2,1)S(1)} collective-permute-done((bf16[216,16,128]{2,1,0:T(8,128)(2,1)S(1)}, bf16[216,16,128]{2,1,0:T(8,128)(2,1)S(1)}, u32[]{:S(2)}, u32[]{:S(2)}) %collective-permute-start.25) | collective-permute-done | bytes 884768 | tf_op jit(solution)/shard_map/ppermute | solution.py:1014
  178.2 4.0 %shard_map.286 = (bf16[2,384,256]{2,1,0:T(8,128)(2,1)S(1)}, bf16[2,96,1664]{2,1,0:T(8,128)(2,1)S(1)}, bf16[2,96,1664]{2,1,0:T(8,128)(2,1)S(1)}) custom-call(s32[2]{0:T(128)S(1)} %copy-done.16, f32[512,384]{1,0:T(8,128)S(1)} %copy-done.20, bf16[512,384]{1,0:T(8,128)(2,1)S(1)} %copy-done.26, f32[512,384]{1,0:T(8,128)S(1)} %copy-done.21, ...), custom_call_target="tpu_custom_call" | custom-call | flops 4600000000 | bytes 1024 | tf_op jit(solution)/shard_map/pallas_call | solution.py:90
  187.8 9.2 %shard_map.288 = (bf16[2,96,1920]{2,1,0:T(8,128)(2,1)S(1)}, bf16[2,96,1920]{2,1,0:T(8,128)(2,1)S(1)}) custom-call(bf16[2,384,256]{2,1,0:T(8,128)(2,1)S(1)} %get-tuple-element.213.refs_0_, f32[2,480,256]{2,1,0:T(8,128)S(1)} %copy-done.27, bf16[6,2,1104,256]{3,2,1,0:T(8,128)(2,1)S(1)} %bitcast.35, bf16[2,1104,256]{2,1,0:T(8,128)(2,1)S(1)} %bitcast.29, ...), custom_call_target="tpu_custom_call" | custom-call | flops 14949999616 | bytes 1024 | tf_op jit(solution)/shard_map/pallas_call | solution.py:90
  204.3 3.2 %collective-permute-start.40 = (bf16[27,16,128]{2,1,0:T(8,128)(2,1)S(1)}, bf16[27,16,128]{2,1,0:T(8,128)(2,1)S(1)}, u32[]{:S(2)}, u32[]{:S(2)}) collective-permute-start(bf16[27,16,128]{2,1,0:T(8,128)(2,1)S(1)} %get-tuple-element.226.refs_0_), channel_id=1, source_target_pairs={{0,2},{1,3},{2,0},{3,1},{4,6},{5,7},{6,4},{7,5},{8,10},{9,11},{10,... | collective-permute-start | bytes 331784 | tf_op jit(solution)/shard_map/ppermute | solution.py:1014
  207.5 3.5 %collective-permute-done.42.refs_3_ = bf16[27,16,128]{2,1,0:T(8,128)(2,1)S(1)} collective-permute-done((bf16[27,16,128]{2,1,0:T(8,128)(2,1)S(1)}, bf16[27,16,128]{2,1,0:T(8,128)(2,1)S(1)}, u32[]{:S(2)}, u32[]{:S(2)}) %collective-permute-start.42) | collective-permute-done | bytes 110624 | tf_op jit(solution)/shard_map/ppermute | solution.py:1014
  211.0 3.2 %collective-permute-done.41.refs_2_ = bf16[27,16,128]{2,1,0:T(8,128)(2,1)S(1)} collective-permute-done((bf16[27,16,128]{2,1,0:T(8,128)(2,1)S(1)}, bf16[27,16,128]{2,1,0:T(8,128)(2,1)S(1)}, u32[]{:S(2)}, u32[]{:S(2)}) %collective-permute-start.41) | collective-permute-done | bytes 110624 | tf_op jit(solution)/shard_map/ppermute | solution.py:1014
  216.8 4.3 %collective-permute-done.48.refs_3_ = bf16[44,16,128]{2,1,0:T(8,128)(2,1)S(1)} collective-permute-done((bf16[44,16,128]{2,1,0:T(8,128)(2,1)S(1)}, bf16[44,16,128]{2,1,0:T(8,128)(2,1)S(1)}, u32[]{:S(2)}, u32[]{:S(2)}) %collective-permute-start.48) | collective-permute-done | bytes 180256 | tf_op jit(solution)/shard_map/ppermute | solution.py:1014
  227.7 5.6 %collective-permute-done.49.refs_4_ = bf16[4,27,16,128]{3,2,1,0:T(8,128)(2,1)S(1)} collective-permute-done((bf16[4,27,16,128]{3,2,1,0:T(8,128)(2,1)S(1)}, bf16[4,27,16,128]{3,2,1,0:T(8,128)(2,1)S(1)}, u32[]{:S(2)}, u32[]{:S(2)}) %collective-permute-start.49) | collective-permute-done | bytes 442400 | tf_op jit(solution)/shard_map/ppermute | solution.py:1014
  252.2 7.3 %shard_map.296 = (f32[1,1]{1,0:T(1,128)}, f32[1,1]{1,0:T(1,128)}, f32[1,1]{1,0:T(1,128)}, f32[96,7632]{1,0:T(8,128)}, f32[96,7632]{1,0:T(8,128)}, /*index=5*/f32...) custom-call(f32[8,128]{1,0:T(8,128)S(1)} %add.13.refs_0_, ...), custom_call_target="tpu_custom_call" | custom-call | flops 11500000256 | bytes 1024 | tf_op jit(solution)/shard_map/pallas_call | solution.py:90
  (212 shorter events, 104.2 us)
Async XLA Ops:
  5.4 11.7 %collective-permute-start.1 = (bf16[96,1920]{1,0:T(8,128)(2,1)}, bf16[96,1920]{1,0:T(8,128)(2,1)S(1)}, u32[]{:S(2)}, u32[]{:S(2)}) collective-permute-start(bf16[96,1920]{1,0:T(8,128)(2,1)} %get-tuple-element.141.refs_2_), channel_id=1, source_target_pairs={{0,16},{8,24},{16,0},{24,8},{1,17},{9,25},{17,1},{25,9},{2,18},{10... | collective-permute-start | bytes 1105928 | tf_op jit(solution)/shard_map/ppermute | solution.py:1014
  17.2 13.0 %collective-permute-start.4 = (bf16[128,1536]{1,0:T(8,128)(2,1)}, bf16[128,1536]{1,0:T(8,128)(2,1)}, u32[]{:S(2)}, u32[]{:S(2)}) collective-permute-start(bf16[128,1536]{1,0:T(8,128)(2,1)} %get-tuple-element.146.refs_2_), channel_id=1, source_target_pairs={{0,16},{8,24},{16,0},{24,8},{1,17},{9,25},{17,1},{25,9},{2,18},{10... | collective-permute-start | bytes 1179656 | tf_op jit(solution)/shard_map/ppermute | solution.py:1014
  33.4 35.1 %collective-permute-start.17 = (bf16[96,4608]{1,0:T(8,128)(2,1)}, bf16[96,4608]{1,0:T(8,128)(2,1)S(1)}, u32[]{:S(2)}, u32[]{:S(2)}) collective-permute-start(bf16[96,4608]{1,0:T(8,128)(2,1)} %shard_map.273.refs_11_), channel_id=1, source_target_pairs={{0,16},{8,24},{16,0},{24,8},{1,17},{9,25},{17,1},{25,9},{2,18},{10... | collective-permute-start | bytes 2654216 | tf_op jit(solution)/shard_map/ppermute | solution.py:1014
  40.9 14.6 %collective-permute-start.6 = (bf16[1168,128]{1,0:T(8,128)(2,1)S(1)}, bf16[1168,128]{1,0:T(8,128)(2,1)S(1)}, u32[]{:S(2)}, u32[]{:S(2)}) collective-permute-start(bf16[1168,128]{1,0:T(8,128)(2,1)S(1)} %get-tuple-element.149), channel_id=1, source_target_pairs={{0,2},{1,3},{2,0},{3,1},{4,6},{5,7},{6,4},{7,5},{8,10},{9,11},{10,... | collective-permute-start | bytes 897032 | tf_op jit(solution)/shard_map/ppermute | solution.py:1014
  42.5 23.7 %collective-permute-start.7 = (bf16[1168,128]{1,0:T(8,128)(2,1)S(1)}, bf16[1168,128]{1,0:T(8,128)(2,1)S(1)}, u32[]{:S(2)}, u32[]{:S(2)}) collective-permute-start(bf16[1168,128]{1,0:T(8,128)(2,1)S(1)} %get-tuple-element.150), channel_id=1, source_target_pairs={{0,4},{1,5},{2,6},{3,7},{4,0},{5,1},{6,2},{7,3},{8,12},{9,13},{10,... | collective-permute-start | bytes 897032 | tf_op jit(solution)/shard_map/ppermute | solution.py:1014
  45.1 22.8 %collective-permute-start.8 = (bf16[1168,128]{1,0:T(8,128)(2,1)S(1)}, bf16[1168,128]{1,0:T(8,128)(2,1)S(1)}, u32[]{:S(2)}, u32[]{:S(2)}) collective-permute-start(bf16[1168,128]{1,0:T(8,128)(2,1)S(1)} %get-tuple-element.151), channel_id=1, source_target_pairs={{0,6},{1,7},{2,4},{3,5},{4,2},{5,3},{6,0},{7,1},{8,14},{9,15},{10,... | collective-permute-start | bytes 897032 | tf_op jit(solution)/shard_map/ppermute | solution.py:1014
  45.3 23.1 %collective-permute-start.9 = (bf16[784,128]{1,0:T(8,128)(2,1)S(1)}, bf16[784,128]{1,0:T(8,128)(2,1)S(1)}, u32[]{:S(2)}, u32[]{:S(2)}) collective-permute-start(bf16[784,128]{1,0:T(8,128)(2,1)S(1)} %slice.12), channel_id=1, source_target_pairs={{0,1},{1,0},{2,3},{3,2},{4,5},{5,4},{6,7},{7,6},{8,9},{9,8},{10,11... | collective-permute-start | bytes 602120 | tf_op jit(solution)/shard_map/ppermute | solution.py:1014
  55.5 13.6 %collective-permute-start.10 = (bf16[784,128]{1,0:T(8,128)(2,1)S(1)}, bf16[784,128]{1,0:T(8,128)(2,1)S(1)}, u32[]{:S(2)}, u32[]{:S(2)}) collective-permute-start(bf16[784,128]{1,0:T(8,128)(2,1)S(1)} %slice.16), channel_id=1, source_target_pairs={{0,1},{1,0},{2,3},{3,2},{4,5},{5,4},{6,7},{7,6},{8,9},{9,8},{10,11... | collective-permute-start | bytes 602120 | tf_op jit(solution)/shard_map/ppermute | solution.py:1014
  68.5 20.7 %collective-permute-start.16 = (bf16[96,4608]{1,0:T(8,128)(2,1)S(1)}, bf16[96,4608]{1,0:T(8,128)(2,1)S(1)}, u32[]{:S(2)}, u32[]{:S(2)}) collective-permute-start(bf16[96,4608]{1,0:T(8,128)(2,1)S(1)} %copy-done.2), channel_id=1, source_target_pairs={{0,8},{8,0},{16,24},{24,16},{1,9},{9,1},{17,25},{25,17},{2,10},{10... | collective-permute-start | bytes 2654216 | tf_op jit(solution)/shard_map/ppermute | solution.py:1014
  68.5 26.4 %collective-permute-start.18 = (bf16[96,4608]{1,0:T(8,128)(2,1)S(1)}, bf16[96,4608]{1,0:T(8,128)(2,1)S(1)}, u32[]{:S(2)}, u32[]{:S(2)}) collective-permute-start(bf16[96,4608]{1,0:T(8,128)(2,1)S(1)} %collective-permute-done.17.refs_13_), channel_id=1, source_target_pairs={{0,8},{8,0},{16,24},{24,16},{1,9},{9,1},{17,25},{25,17},{2,10},{10... | collective-permute-start | bytes 2654216 | tf_op jit(solution)/shard_map/ppermute | solution.py:1014
  119.9 30.6 %collective-permute-start.22 = (bf16[2,96,4608]{2,1,0:T(8,128)(2,1)S(1)}, bf16[2,96,4608]{2,1,0:T(8,128)(2,1)S(1)}, u32[]{:S(2)}, u32[]{:S(2)}) collective-permute-start(bf16[2,96,4608]{2,1,0:T(8,128)(2,1)S(1)} %get-tuple-element.179), channel_id=1, source_target_pairs={{0,8},{8,0},{16,24},{24,16},{1,9},{9,1},{17,25},{25,17},{2,10},{10... | collective-permute-start | bytes 5308424 | tf_op jit(solution)/shard_map/ppermute | solution.py:1014
  145.3 13.5 %collective-permute-start.23 = (bf16[1,4,256,128]{3,2,1,0:T(8,128)(2,1)S(1)}, bf16[1,4,256,128]{3,2,1,0:T(8,128)(2,1)S(1)}, u32[]{:S(2)}, u32[]{:S(2)}) collective-permute-start(bf16[1,4,256,128]{3,2,1,0:T(8,128)(2,1)S(1)} %get-tuple-element.182), channel_id=1, source_target_pairs={{0,1},{1,0},{2,3},{3,2},{4,5},{5,4},{6,7},{7,6},{8,9},{9,8},{10,11... | collective-permute-start | bytes 786440 | tf_op jit(solution)/shard_map/ppermute | solution.py:1014
  146.0 11.0 %collective-permute-start.27 = (bf16[384,128]{1,0:T(8,128)(2,1)S(1)}, bf16[384,128]{1,0:T(8,128)(2,1)S(1)}, u32[]{:S(2)}, u32[]{:S(2)}) collective-permute-start(bf16[384,128]{1,0:T(8,128)(2,1)S(1)} %get-tuple-element.194), channel_id=1, source_target_pairs={{0,2},{1,3},{2,0},{3,1},{4,6},{5,7},{6,4},{7,5},{8,10},{9,11},{10,... | collective-permute-start | bytes 294920 | tf_op jit(solution)/shard_map/ppermute | solution.py:1014
  150.9 19.8 %collective-permute-start.25 = (bf16[216,16,128]{2,1,0:T(8,128)(2,1)S(1)}, bf16[216,16,128]{2,1,0:T(8,128)(2,1)S(1)}, u32[]{:S(2)}, u32[]{:S(2)}) collective-permute-start(bf16[216,16,128]{2,1,0:T(8,128)(2,1)S(1)} %get-tuple-element.185), channel_id=1, source_target_pairs={{0,16},{8,24},{16,0},{24,8},{1,17},{9,25},{17,1},{25,9},{2,18},{10... | collective-permute-start | bytes 2654216 | tf_op jit(solution)/shard_map/ppermute | solution.py:1014
  160.5 13.2 %collective-permute-start.30 = (bf16[384,128]{1,0:T(8,128)(2,1)S(1)}, bf16[384,128]{1,0:T(8,128)(2,1)S(1)}, u32[]{:S(2)}, u32[]{:S(2)}) collective-permute-start(bf16[384,128]{1,0:T(8,128)(2,1)S(1)} %get-tuple-element.198), channel_id=1, source_target_pairs={{0,4},{1,5},{2,6},{3,7},{4,0},{5,1},{6,2},{7,3},{8,12},{9,13},{10,... | collective-permute-start | bytes 294920 | tf_op jit(solution)/shard_map/ppermute | solution.py:1014
  161.5 13.8 %collective-permute-start.31 = (bf16[384,128]{1,0:T(8,128)(2,1)S(1)}, bf16[384,128]{1,0:T(8,128)(2,1)S(1)}, u32[]{:S(2)}, u32[]{:S(2)}) collective-permute-start(bf16[384,128]{1,0:T(8,128)(2,1)S(1)} %get-tuple-element.199), channel_id=1, source_target_pairs={{0,6},{1,7},{2,4},{3,5},{4,2},{5,3},{6,0},{7,1},{8,14},{9,15},{10,... | collective-permute-start | bytes 294920 | tf_op jit(solution)/shard_map/ppermute | solution.py:1014
  164.5 10.8 %collective-permute-start.33 = (bf16[384,128]{1,0:T(8,128)(2,1)S(1)}, bf16[384,128]{1,0:T(8,128)(2,1)S(1)}, u32[]{:S(2)}, u32[]{:S(2)}) collective-permute-start(bf16[384,128]{1,0:T(8,128)(2,1)S(1)} %get-tuple-element.206), channel_id=1, source_target_pairs={{0,2},{1,3},{2,0},{3,1},{4,6},{5,7},{6,4},{7,5},{8,10},{9,11},{10,... | collective-permute-start | bytes 294920 | tf_op jit(solution)/shard_map/ppermute | solution.py:1014
  166.3 11.8 %collective-permute-start.34 = (bf16[384,128]{1,0:T(8,128)(2,1)S(1)}, bf16[384,128]{1,0:T(8,128)(2,1)S(1)}, u32[]{:S(2)}, u32[]{:S(2)}) collective-permute-start(bf16[384,128]{1,0:T(8,128)(2,1)S(1)} %get-tuple-element.207), channel_id=1, source_target_pairs={{0,4},{1,5},{2,6},{3,7},{4,0},{5,1},{6,2},{7,3},{8,12},{9,13},{10,... | collective-permute-start | bytes 294920 | tf_op jit(solution)/shard_map/ppermute | solution.py:1014
  183.3 13.7 %collective-permute-start.37 = (bf16[27,16,128]{2,1,0:T(8,128)(2,1)S(1)}, bf16[27,16,128]{2,1,0:T(8,128)(2,1)S(1)}, u32[]{:S(2)}, u32[]{:S(2)}) collective-permute-start(bf16[27,16,128]{2,1,0:T(8,128)(2,1)S(1)} %get-tuple-element.222), channel_id=1, source_target_pairs={{0,2},{1,3},{2,0},{3,1},{4,6},{5,7},{6,4},{7,5},{8,10},{9,11},{10,... | collective-permute-start | bytes 331784 | tf_op jit(solution)/shard_map/ppermute | solution.py:1014
  184.1 12.9 %collective-permute-start.38 = (bf16[27,16,128]{2,1,0:T(8,128)(2,1)S(1)}, bf16[27,16,128]{2,1,0:T(8,128)(2,1)S(1)}, u32[]{:S(2)}, u32[]{:S(2)}) collective-permute-start(bf16[27,16,128]{2,1,0:T(8,128)(2,1)S(1)} %get-tuple-element.223), channel_id=1, source_target_pairs={{0,4},{1,5},{2,6},{3,7},{4,0},{5,1},{6,2},{7,3},{8,12},{9,13},{10,... | collective-permute-start | bytes 331784 | tf_op jit(solution)/shard_map/ppermute | solution.py:1014
  185.3 11.7 %collective-permute-start.39 = (bf16[27,16,128]{2,1,0:T(8,128)(2,1)S(1)}, bf16[27,16,128]{2,1,0:T(8,128)(2,1)S(1)}, u32[]{:S(2)}, u32[]{:S(2)}) collective-permute-start(bf16[27,16,128]{2,1,0:T(8,128)(2,1)S(1)} %get-tuple-element.224), channel_id=1, source_target_pairs={{0,6},{1,7},{2,4},{3,5},{4,2},{5,3},{6,0},{7,1},{8,14},{9,15},{10,... | collective-permute-start | bytes 331784 | tf_op jit(solution)/shard_map/ppermute | solution.py:1014
  201.0 13.2 %collective-permute-start.45 = (bf16[88,16,128]{2,1,0:T(8,128)(2,1)S(1)}, bf16[88,16,128]{2,1,0:T(8,128)(2,1)S(1)}, u32[]{:S(2)}, u32[]{:S(2)}) collective-permute-start(bf16[88,16,128]{2,1,0:T(8,128)(2,1)S(1)} %get-tuple-element.232), channel_id=1, source_target_pairs={{0,16},{8,24},{16,0},{24,8},{1,17},{9,25},{17,1},{25,9},{2,18},{10... | collective-permute-start | bytes 1081352 | tf_op jit(solution)/shard_map/ppermute | solution.py:1014
  201.6 12.6 %collective-permute-start.46 = (bf16[88,16,128]{2,1,0:T(8,128)(2,1)S(1)}, bf16[88,16,128]{2,1,0:T(8,128)(2,1)S(1)}, u32[]{:S(2)}, u32[]{:S(2)}) collective-permute-start(bf16[88,16,128]{2,1,0:T(8,128)(2,1)S(1)} %get-tuple-element.234), channel_id=1, source_target_pairs={{0,1},{1,0},{2,3},{3,2},{4,5},{5,4},{6,7},{7,6},{8,9},{9,8},{10,11... | collective-permute-start | bytes 1081352 | tf_op jit(solution)/shard_map/ppermute | solution.py:1014
  222.3 10.9 %collective-permute-start.49 = (bf16[4,27,16,128]{3,2,1,0:T(8,128)(2,1)S(1)}, bf16[4,27,16,128]{3,2,1,0:T(8,128)(2,1)S(1)}, u32[]{:S(2)}, u32[]{:S(2)}) collective-permute-start(bf16[4,27,16,128]{3,2,1,0:T(8,128)(2,1)S(1)} %shard_map.290.refs_3_), channel_id=1, source_target_pairs={{0,1},{1,0},{2,3},{3,2},{4,5},{5,4},{6,7},{7,6},{8,9},{9,8},{10,11... | collective-permute-start | bytes 1327112 | tf_op jit(solution)/shard_map/ppermute | solution.py:1014
  (76 other events, 817.8 us)

commit v3 on v2

--- a/solution.py
+++ b/solution.py
@@ -146,18 +146,22 @@
     return value, slope
 
 
-def pack_first(*refs):
-    samples, cosines, agg_ref, mod_a, mod_b, wide_ref, tall_ref, query_ref = refs[:8]
-    lead_ref, mask_ref, first_ref, second_ref, rider_s = refs[8:]
-    rows = wide_ref.shape[0]
-    grp, seq = place()
+def pack_first(agg_ref, tall_ref, query_ref, first_ref):
+    rows = agg_ref.shape[0]
     first_ref[:, : 2 * D] = agg_ref[:, : 2 * D].astype(BF16)
-    second_ref[:rows, :D] = agg_ref[:, 2 * D :].astype(BF16)
     eye = iota((rows, rows), 0) == iota((rows, rows), 1)
     column = jnp.sum(jnp.where(eye, query_ref[...], 0.0), axis=1, keepdims=True)
     lane = iota((rows, OUTP), 1)
     embed = jnp.where(lane < OUT, tall_ref[...], jnp.where(lane == OUT, column, 0.0))
     first_ref[:, 2 * D :] = embed.astype(BF16)
+
+
+def pack_second(*refs):
+    samples, cosines, agg_ref, mod_a, mod_b, wide_ref, lead_ref, mask_ref = refs[:8]
+    second_ref, rider_s = refs[8:]
+    rows = wide_ref.shape[0]
+    grp, seq = place()
+    second_ref[:rows, :D] = agg_ref[:, 2 * D :].astype(BF16)
     low = half_low((rows, 128))
     for j in range(HEADS // 2):
         k = wide_ref[:, D + j * 128 : D + (j + 1) * 128]
@@ -1183,19 +1187,32 @@
     def columns_of(index):
         return pl.BlockSpec((rows, 3 * D), lambda i: (0, index))
 
-    first_own, second_own = call(
+    first_own = call(
         pack_first,
-        [sds((rows, 2 * D + OUTP), BF16), sds((rows + RIDERS, 4 * D), BF16)],
+        sds((rows, 2 * D + OUTP), BF16),
         grid=(1,),
-        in_specs=[smem(), smem()]
-        + [columns_of(i) for i in (0, 1, 2, 3, 0)]
-        + [pl.BlockSpec((1, rows), lambda i: (0, 0)), whole(), whole()],
-        out_specs=[whole()] * 2,
+        in_specs=[columns_of(0), columns_of(0), pl.BlockSpec((1, rows), lambda i: (0, 0))],
+        out_specs=whole(),
+        us=2,
+        limit=62,
+    )(wide_weights, tall[0], query_row)
+    second_own = call(
+        pack_second,
+        sds((rows + RIDERS, 4 * D), BF16),
+        grid=(1,),
+        in_specs=[smem(), smem()] + [columns_of(i) for i in range(4)] + [whole(), whole()],
+        out_specs=whole(),
         scratch=[pltpu.VMEM((RIDERS, 4 * D), F32)],
         us=3,
         limit=62,
-    )(samples, cosines, *[wide_weights] * 4, tall[0], query_row, lead, mask)
-    first = gather_blocks(first_own, group)
+        after=(first_own,),
+    )(samples, cosines, *[wide_weights] * 4, lead, mask)
+    first = gather_blocks(
+        first_own,
+        group,
+        lambda blocks: {j: once_ready(block, (second_own,)) for j, block in blocks.items()},
+    )
+
     by_item = pl.BlockSpec((tokens, D), lambda i: (i, 0))
 
     def lane_block(height):
@@ -1367,13 +1384,10 @@
         )(*near, *far)
         return over_cuts(dealt[0], dealt[1:])
 
-    early_got = shift(early_send, "grp", 1)
+    early_once = reduce_cores_once(early_keep, shift(early_send, "grp", 1))
     partial_sums, units_in = [], []
     for u in range(units):
-        after = (early_keep,) if u == 0 else (partial_sums[u - 1][0][0],)
-        if u == 2:
-            early_once = reduce_cores_once(early_keep, early_got, after=after)
-            after += (early_once[0],)
+        after = (early_once[0],) if u == 0 else (partial_sums[u - 1][0][0],)
         if u >= 2:
             units_in.append(joined(*partial_sums[u - 2]))
         partial_sums.append(back_of(u, after))

time: 262 us -> 259 us (0.989)
  waiting for transfers between devices: 85.3 us -> 81 us
    ppermute x60, waiting for transfers between devices: 85.3 us -> 81 us  [shift(): return lax.ppermute(value, axis, [(i, i ^ bit) for i in range(size)])]
    pallas_call x26 -> x27, Pallas kernels: 93.8 us -> 95.5 us  [run(): pl.pallas_call(kernel, out_shape=outs, grid=grid, in_specs=list(in_specs)...]
    unnamed x81 -> x89, local copies, waits for them, and re-layouts: 4.47 us -> 5.29 us
  transfers between devices with their start and end apart: 60 -> 60, of which waited for: 25 -> 25; matrix products, arithmetic and copies ran while one was open for 0% -> 0% of each run, Pallas kernels for 22% -> 21%
where the time goes in v3:
time: 259 us; the launch traced here: 257 us
  Pallas kernels  95.5 us (37%)
  waiting for transfers between devices  81 us (31%)
  starting transfers between devices  73.2 us (28%)
  local copies, waits for them, and re-layouts  6.02 us (2%)
    pallas_call x27, Pallas kernels, run(): pl.pallas_call(kernel, out_shape=outs, grid=grid, in_specs=list(in_specs)...  95.5 us
    ppermute x60, waiting for transfers between devices, shift(): return lax.ppermute(value, axis, [(i, i ^ bit) for i in range(size)])  81 us
    ppermute x60, starting transfers between devices, shift(): return lax.ppermute(value, axis, [(i, i ^ bit) for i in range(size)])  73.2 us
    unnamed x89, local copies, waits for them, and re-layouts  5.29 us
  transfers between devices with their start and end apart: 60, of which 25 were waited for; matrix products, arithmetic and copies ran while one was open for 0% of the time, Pallas kernels for 21%

profile of v3, /device:TPU:0, one launch (start us, length us, event | category | flops | bytes accessed | tf_op | source)
XLA Modules:
  0.0 257.2 jit_solution(819829774125024074)
XLA Ops:
  2.7 2.9 %collective-permute-start.1 = (bf16[96,1920]{1,0:T(8,128)(2,1)}, bf16[96,1920]{1,0:T(8,128)(2,1)S(1)}, u32[]{:S(2)}, u32[]{:S(2)}) collective-permute-start(bf16[96,1920]{1,0:T(8,128)(2,1)} %shard_map.271.refs_2_), channel_id=1, source_target_pairs={{0,16},{8,24},{16,0},{24,8},{1,17},{9,25},{17,1},{25,9},{2,18},{10... | collective-permute-start | bytes 1105928 | tf_op jit(solution)/shard_map/ppermute | solution.py:1018
  9.2 5.2 %collective-permute-done.1.refs_4_ = bf16[96,1920]{1,0:T(8,128)(2,1)S(1)} collective-permute-done((bf16[96,1920]{1,0:T(8,128)(2,1)}, bf16[96,1920]{1,0:T(8,128)(2,1)S(1)}, u32[]{:S(2)}, u32[]{:S(2)}) %collective-permute-start.1) | collective-permute-done | bytes 368672 | tf_op jit(solution)/shard_map/ppermute | solution.py:1018
  18.9 9.4 %shard_map.273 = (f32[2,480,256]{2,1,0:T(8,128)}, bf16[6,2,1104,256]{3,2,1,0:T(8,128)(2,1)}, bf16[512,384]{1,0:T(8,128)(2,1)S(1)}, bf16[384,768]{1,0:T(8,128)(2,...) custom-call(bf16[2,1104,256]{2,1,0:T(8,128)(2,1)S(1)} %bitcast.26, ...), custom_call_target="tpu_custom_call" | custom-call | flops 11500000256 | bytes 1024 | tf_op jit(solution)/shard_map/pallas_call | solution.py:90
  34.3 4.8 %shard_map.275 = (f32[512,384]{1,0:T(8,128)}, bf16[512,384]{1,0:T(8,128)(2,1)}, bf16[384,1536]{1,0:T(8,128)(2,1)}, f32[8,2304]{1,0:T(8,128)}, bf16[1168,128]{1,0...) custom-call(s32[2]{0:T(128)S(1)} %copy-done.16, ...), custom_call_target="tpu_custom_call" | custom-call | flops 4600000000 | bytes 1024 | tf_op jit(solution)/shard_map/pallas_call | solution.py:90
  45.1 8.5 %collective-permute-done.6.refs_1_ = bf16[1168,128]{1,0:T(8,128)(2,1)S(1)} collective-permute-done((bf16[1168,128]{1,0:T(8,128)(2,1)S(1)}, bf16[1168,128]{1,0:T(8,128)(2,1)S(1)}, u32[]{:S(2)}, u32[]{:S(2)}) %collective-permute-start.6) | collective-permute-done | bytes 299040 | tf_op jit(solution)/shard_map/ppermute | solution.py:1018
  55.3 9.2 %collective-permute-done.7.refs_2_ = bf16[1168,128]{1,0:T(8,128)(2,1)S(1)} collective-permute-done((bf16[1168,128]{1,0:T(8,128)(2,1)S(1)}, bf16[1168,128]{1,0:T(8,128)(2,1)S(1)}, u32[]{:S(2)}, u32[]{:S(2)}) %collective-permute-start.7) | collective-permute-done | bytes 299040 | tf_op jit(solution)/shard_map/ppermute | solution.py:1018
  67.2 3.0 %collective-permute-done.11.refs_6_ = bf16[784,128]{1,0:T(8,128)(2,1)S(1)} collective-permute-done((bf16[784,128]{1,0:T(8,128)(2,1)S(1)}, bf16[784,128]{1,0:T(8,128)(2,1)S(1)}, u32[]{:S(2)}, u32[]{:S(2)}) %collective-permute-start.11) | collective-permute-done | bytes 200736 | tf_op jit(solution)/shard_map/ppermute | solution.py:1018
  72.4 9.0 %shard_map.276 = (bf16[3,128,128]{2,1,0:T(8,128)(2,1)S(1)}, bf16[3,128,128]{2,1,0:T(8,128)(2,1)S(1)}, bf16[3,128,128]{2,1,0:T(8,128)(2,1)S(1)}, bf16[3,128,128]{...) custom-call(bf16[1168,128]{1,0:T(8,128)(2,1)S(1)} %get-tuple-element.200.refs_0_, ...), custom_call_target="tpu_custom_call" | custom-call | flops 10350000128 | bytes 1024 | tf_op jit(solution)/shard_map/pallas_call | solution.py:90
  81.4 3.5 %collective-permute-start.13 = (bf16[3,128,128]{2,1,0:T(8,128)(2,1)S(1)}, bf16[3,128,128]{2,1,0:T(8,128)(2,1)S(1)}, u32[]{:S(2)}, u32[]{:S(2)}) collective-permute-start(bf16[3,128,128]{2,1,0:T(8,128)(2,1)S(1)} %get-tuple-element.156), channel_id=1, source_target_pairs={{0,2},{1,3},{2,0},{3,1},{4,6},{5,7},{6,4},{7,5},{8,10},{9,11},{10,... | collective-permute-start | bytes 294920 | tf_op jit(solution)/shard_map/ppermute | solution.py:1018
  87.7 5.4 %collective-permute-done.14.refs_9_ = bf16[3,128,128]{2,1,0:T(8,128)(2,1)S(1)} collective-permute-done((bf16[3,128,128]{2,1,0:T(8,128)(2,1)S(1)}, bf16[3,128,128]{2,1,0:T(8,128)(2,1)S(1)}, u32[]{:S(2)}, u32[]{:S(2)}) %collective-permute-start.14) | collective-permute-done | bytes 98336 | tf_op jit(solution)/shard_map/ppermute | solution.py:1018
  93.8 21.5 %shard_map.277 = (f32[512,384]{1,0:T(8,128)}, f32[2,8,384]{2,1,0:T(8,128)}, f32[8,128]{1,0:T(8,128)}, bf16[3,128,128]{2,1,0:T(8,128)(2,1)S(1)}, bf16[3,128,128]{...) custom-call(s32[2]{0:T(128)S(1)} %copy-done.16, ...), custom_call_target="tpu_custom_call" | custom-call | flops 12650000384 | bytes 1024 | tf_op jit(solution)/shard_map/pallas_call | solution.py:90
  123.3 7.2 %collective-permute-done.21.refs_10_ = bf16[3,128,128]{2,1,0:T(8,128)(2,1)S(1)} collective-permute-done((bf16[3,128,128]{2,1,0:T(8,128)(2,1)S(1)}, bf16[3,128,128]{2,1,0:T(8,128)(2,1)S(1)}, u32[]{:S(2)}, u32[]{:S(2)}) %collective-permute-start.21) | collective-permute-done | bytes 98336 | tf_op jit(solution)/shard_map/ppermute | solution.py:1018
  130.6 5.5 %shard_map.280 = (bf16[1,4,128,128]{3,2,1,0:T(8,128)(2,1)S(1)}, bf16[1,4,256,128]{3,2,1,0:T(8,128)(2,1)S(1)}, bf16[1,4,256,128]{3,2,1,0:T(8,128)(2,1)S(1)}) custom-call(bf16[1168,128]{1,0:T(8,128)(2,1)S(1)} %get-tuple-element.200.refs_0_, bf16[1168,128]{1,0:T(8,128)(2,1)S(1)} %collective-permute-done.6.refs_1_, ...), custom_call_target="tpu_custom_call" | custom-call | flops 6899999744 | bytes 1024 | tf_op jit(solution)/shard_map/pallas_call | solution.py:90
  137.7 5.9 %shard_map.281 = (bf16[1,4,128,128]{3,2,1,0:T(8,128)(2,1)S(1)}, bf16[1,4,256,128]{3,2,1,0:T(8,128)(2,1)S(1)}, bf16[1,4,256,128]{3,2,1,0:T(8,128)(2,1)S(1)}) custom-call(bf16[1168,128]{1,0:T(8,128)(2,1)S(1)} %get-tuple-element.200.refs_0_, bf16[1168,128]{1,0:T(8,128)(2,1)S(1)} %collective-permute-done.6.refs_1_, ...), custom_call_target="tpu_custom_call" | custom-call | flops 6899999744 | bytes 1024 | tf_op jit(solution)/shard_map/pallas_call | solution.py:90
  150.0 5.5 %shard_map.285 = (bf16[1,4,128,128]{3,2,1,0:T(8,128)(2,1)S(1)}, bf16[1,4,256,128]{3,2,1,0:T(8,128)(2,1)S(1)}, bf16[1,4,256,128]{3,2,1,0:T(8,128)(2,1)S(1)}) custom-call(bf16[1168,128]{1,0:T(8,128)(2,1)S(1)} %get-tuple-element.200.refs_0_, bf16[1168,128]{1,0:T(8,128)(2,1)S(1)} %collective-permute-done.6.refs_1_, ...), custom_call_target="tpu_custom_call" | custom-call | flops 6899999744 | bytes 1024 | tf_op jit(solution)/shard_map/pallas_call | solution.py:90
  171.4 6.0 %collective-permute-done.34.refs_18_ = bf16[384,128]{1,0:T(8,128)(2,1)S(1)} collective-permute-done((bf16[384,128]{1,0:T(8,128)(2,1)S(1)}, bf16[384,128]{1,0:T(8,128)(2,1)S(1)}, u32[]{:S(2)}, u32[]{:S(2)}) %collective-permute-start.34) | collective-permute-done | bytes 98336 | tf_op jit(solution)/shard_map/ppermute | solution.py:1018
  177.5 4.0 %shard_map.287 = (bf16[2,384,256]{2,1,0:T(8,128)(2,1)S(1)}, bf16[2,96,1664]{2,1,0:T(8,128)(2,1)S(1)}, bf16[2,96,1664]{2,1,0:T(8,128)(2,1)S(1)}) custom-call(s32[2]{0:T(128)S(1)} %copy-done.16, f32[512,384]{1,0:T(8,128)S(1)} %copy-done.23, bf16[512,384]{1,0:T(8,128)(2,1)S(1)} %copy-done.29, f32[512,384]{1,0:T(8,128)S(1)} %copy-done.24, ...), custom_call_target="tpu_custom_call" | custom-call | flops 4600000000 | bytes 1024 | tf_op jit(solution)/shard_map/pallas_call | solution.py:90
  186.3 9.2 %shard_map.289 = (bf16[2,96,1920]{2,1,0:T(8,128)(2,1)S(1)}, bf16[2,96,1920]{2,1,0:T(8,128)(2,1)S(1)}) custom-call(bf16[2,384,256]{2,1,0:T(8,128)(2,1)S(1)} %get-tuple-element.213.refs_0_, f32[2,480,256]{2,1,0:T(8,128)S(1)} %copy-done.30, bf16[6,2,1104,256]{3,2,1,0:T(8,128)(2,1)S(1)} %bitcast.35, bf16[2,1104,256]{2,1,0:T(8,128)(2,1)S(1)} %bitcast.27, ...), custom_call_target="tpu_custom_call" | custom-call | flops 14949999616 | bytes 1024 | tf_op jit(solution)/shard_map/pallas_call | solution.py:90
  205.3 3.4 %collective-permute-done.42.refs_3_ = bf16[27,16,128]{2,1,0:T(8,128)(2,1)S(1)} collective-permute-done((bf16[27,16,128]{2,1,0:T(8,128)(2,1)S(1)}, bf16[27,16,128]{2,1,0:T(8,128)(2,1)S(1)}, u32[]{:S(2)}, u32[]{:S(2)}) %collective-permute-start.42) | collective-permute-done | bytes 110624 | tf_op jit(solution)/shard_map/ppermute | solution.py:1018
  208.7 4.2 %collective-permute-done.41.refs_2_ = bf16[27,16,128]{2,1,0:T(8,128)(2,1)S(1)} collective-permute-done((bf16[27,16,128]{2,1,0:T(8,128)(2,1)S(1)}, bf16[27,16,128]{2,1,0:T(8,128)(2,1)S(1)}, u32[]{:S(2)}, u32[]{:S(2)}) %collective-permute-start.41) | collective-permute-done | bytes 110624 | tf_op jit(solution)/shard_map/ppermute | solution.py:1018
  216.2 3.0 %collective-permute-done.48.refs_3_ = bf16[44,16,128]{2,1,0:T(8,128)(2,1)S(1)} collective-permute-done((bf16[44,16,128]{2,1,0:T(8,128)(2,1)S(1)}, bf16[44,16,128]{2,1,0:T(8,128)(2,1)S(1)}, u32[]{:S(2)}, u32[]{:S(2)}) %collective-permute-start.48) | collective-permute-done | bytes 180256 | tf_op jit(solution)/shard_map/ppermute | solution.py:1018
  221.9 3.0 %collective-permute-start.51 = (bf16[22,16,128]{2,1,0:T(8,128)(2,1)S(1)}, bf16[22,16,128]{2,1,0:T(8,128)(2,1)S(1)}, u32[]{:S(2)}, u32[]{:S(2)}) collective-permute-start(bf16[22,16,128]{2,1,0:T(8,128)(2,1)S(1)} %get-tuple-element.248), channel_id=1, source_target_pairs={{0,4},{1,5},{2,6},{3,7},{4,0},{5,1},{6,2},{7,3},{8,12},{9,13},{10,... | collective-permute-start | bytes 270344 | tf_op jit(solution)/shard_map/ppermute | solution.py:1018
  226.3 4.2 %collective-permute-done.49.refs_4_ = bf16[4,27,16,128]{3,2,1,0:T(8,128)(2,1)S(1)} collective-permute-done((bf16[4,27,16,128]{3,2,1,0:T(8,128)(2,1)S(1)}, bf16[4,27,16,128]{3,2,1,0:T(8,128)(2,1)S(1)}, u32[]{:S(2)}, u32[]{:S(2)}) %collective-permute-start.49) | collective-permute-done | bytes 442400 | tf_op jit(solution)/shard_map/ppermute | solution.py:1018
  249.8 7.2 %shard_map.297 = (f32[1,1]{1,0:T(1,128)}, f32[1,1]{1,0:T(1,128)}, f32[1,1]{1,0:T(1,128)}, f32[96,7632]{1,0:T(8,128)}, f32[96,7632]{1,0:T(8,128)}, /*index=5*/f32...) custom-call(f32[8,128]{1,0:T(8,128)S(1)} %add.13.refs_0_, ...), custom_call_target="tpu_custom_call" | custom-call | flops 11500000256 | bytes 1024 | tf_op jit(solution)/shard_map/pallas_call | solution.py:90
  (221 shorter events, 104.9 us)
Async XLA Ops:
  2.7 11.7 %collective-permute-start.1 = (bf16[96,1920]{1,0:T(8,128)(2,1)}, bf16[96,1920]{1,0:T(8,128)(2,1)S(1)}, u32[]{:S(2)}, u32[]{:S(2)}) collective-permute-start(bf16[96,1920]{1,0:T(8,128)(2,1)} %shard_map.271.refs_2_), channel_id=1, source_target_pairs={{0,16},{8,24},{16,0},{24,8},{1,17},{9,25},{17,1},{25,9},{2,18},{10... | collective-permute-start | bytes 1105928 | tf_op jit(solution)/shard_map/ppermute | solution.py:1018
  15.1 13.9 %collective-permute-start.4 = (bf16[128,1536]{1,0:T(8,128)(2,1)}, bf16[128,1536]{1,0:T(8,128)(2,1)}, u32[]{:S(2)}, u32[]{:S(2)}) collective-permute-start(bf16[128,1536]{1,0:T(8,128)(2,1)} %shard_map.272.refs_2_), channel_id=1, source_target_pairs={{0,16},{8,24},{16,0},{24,8},{1,17},{9,25},{17,1},{25,9},{2,18},{10... | collective-permute-start | bytes 1179656 | tf_op jit(solution)/shard_map/ppermute | solution.py:1018
  32.3 34.4 %collective-permute-start.17 = (bf16[96,4608]{1,0:T(8,128)(2,1)}, bf16[96,4608]{1,0:T(8,128)(2,1)S(1)}, u32[]{:S(2)}, u32[]{:S(2)}) collective-permute-start(bf16[96,4608]{1,0:T(8,128)(2,1)} %shard_map.274.refs_11_), channel_id=1, source_target_pairs={{0,16},{8,24},{16,0},{24,8},{1,17},{9,25},{17,1},{25,9},{2,18},{10... | collective-permute-start | bytes 2654216 | tf_op jit(solution)/shard_map/ppermute | solution.py:1018
  39.1 14.6 %collective-permute-start.6 = (bf16[1168,128]{1,0:T(8,128)(2,1)S(1)}, bf16[1168,128]{1,0:T(8,128)(2,1)S(1)}, u32[]{:S(2)}, u32[]{:S(2)}) collective-permute-start(bf16[1168,128]{1,0:T(8,128)(2,1)S(1)} %get-tuple-element.150), channel_id=1, source_target_pairs={{0,2},{1,3},{2,0},{3,1},{4,6},{5,7},{6,4},{7,5},{8,10},{9,11},{10,... | collective-permute-start | bytes 897032 | tf_op jit(solution)/shard_map/ppermute | solution.py:1018
  40.7 23.7 %collective-permute-start.7 = (bf16[1168,128]{1,0:T(8,128)(2,1)S(1)}, bf16[1168,128]{1,0:T(8,128)(2,1)S(1)}, u32[]{:S(2)}, u32[]{:S(2)}) collective-permute-start(bf16[1168,128]{1,0:T(8,128)(2,1)S(1)} %get-tuple-element.151), channel_id=1, source_target_pairs={{0,4},{1,5},{2,6},{3,7},{4,0},{5,1},{6,2},{7,3},{8,12},{9,13},{10,... | collective-permute-start | bytes 897032 | tf_op jit(solution)/shard_map/ppermute | solution.py:1018
  43.3 22.7 %collective-permute-start.8 = (bf16[1168,128]{1,0:T(8,128)(2,1)S(1)}, bf16[1168,128]{1,0:T(8,128)(2,1)S(1)}, u32[]{:S(2)}, u32[]{:S(2)}) collective-permute-start(bf16[1168,128]{1,0:T(8,128)(2,1)S(1)} %get-tuple-element.152), channel_id=1, source_target_pairs={{0,6},{1,7},{2,4},{3,5},{4,2},{5,3},{6,0},{7,1},{8,14},{9,15},{10,... | collective-permute-start | bytes 897032 | tf_op jit(solution)/shard_map/ppermute | solution.py:1018
  43.6 23.2 %collective-permute-start.9 = (bf16[784,128]{1,0:T(8,128)(2,1)S(1)}, bf16[784,128]{1,0:T(8,128)(2,1)S(1)}, u32[]{:S(2)}, u32[]{:S(2)}) collective-permute-start(bf16[784,128]{1,0:T(8,128)(2,1)S(1)} %slice.12), channel_id=1, source_target_pairs={{0,1},{1,0},{2,3},{3,2},{4,5},{5,4},{6,7},{7,6},{8,9},{9,8},{10,11... | collective-permute-start | bytes 602120 | tf_op jit(solution)/shard_map/ppermute | solution.py:1018
  53.7 13.5 %collective-permute-start.10 = (bf16[784,128]{1,0:T(8,128)(2,1)S(1)}, bf16[784,128]{1,0:T(8,128)(2,1)S(1)}, u32[]{:S(2)}, u32[]{:S(2)}) collective-permute-start(bf16[784,128]{1,0:T(8,128)(2,1)S(1)} %slice.16), channel_id=1, source_target_pairs={{0,1},{1,0},{2,3},{3,2},{4,5},{5,4},{6,7},{7,6},{8,9},{9,8},{10,11... | collective-permute-start | bytes 602120 | tf_op jit(solution)/shard_map/ppermute | solution.py:1018
  66.7 20.7 %collective-permute-start.16 = (bf16[96,4608]{1,0:T(8,128)(2,1)S(1)}, bf16[96,4608]{1,0:T(8,128)(2,1)S(1)}, u32[]{:S(2)}, u32[]{:S(2)}) collective-permute-start(bf16[96,4608]{1,0:T(8,128)(2,1)S(1)} %copy-done.2), channel_id=1, source_target_pairs={{0,8},{8,0},{16,24},{24,16},{1,9},{9,1},{17,25},{25,17},{2,10},{10... | collective-permute-start | bytes 2654216 | tf_op jit(solution)/shard_map/ppermute | solution.py:1018
  66.7 26.4 %collective-permute-start.18 = (bf16[96,4608]{1,0:T(8,128)(2,1)S(1)}, bf16[96,4608]{1,0:T(8,128)(2,1)S(1)}, u32[]{:S(2)}, u32[]{:S(2)}) collective-permute-start(bf16[96,4608]{1,0:T(8,128)(2,1)S(1)} %collective-permute-done.17.refs_13_), channel_id=1, source_target_pairs={{0,8},{8,0},{16,24},{24,16},{1,9},{9,1},{17,25},{25,17},{2,10},{10... | collective-permute-start | bytes 2654216 | tf_op jit(solution)/shard_map/ppermute | solution.py:1018
  119.8 10.8 %collective-permute-start.21 = (bf16[3,128,128]{2,1,0:T(8,128)(2,1)S(1)}, bf16[3,128,128]{2,1,0:T(8,128)(2,1)S(1)}, u32[]{:S(2)}, u32[]{:S(2)}) collective-permute-start(bf16[3,128,128]{2,1,0:T(8,128)(2,1)S(1)} %get-tuple-element.174), channel_id=1, source_target_pairs={{0,4},{1,5},{2,6},{3,7},{4,0},{5,1},{6,2},{7,3},{8,12},{9,13},{10,... | collective-permute-start | bytes 294920 | tf_op jit(solution)/shard_map/ppermute | solution.py:1018
  143.6 14.5 %collective-permute-start.23 = (bf16[1,4,256,128]{3,2,1,0:T(8,128)(2,1)S(1)}, bf16[1,4,256,128]{3,2,1,0:T(8,128)(2,1)S(1)}, u32[]{:S(2)}, u32[]{:S(2)}) collective-permute-start(bf16[1,4,256,128]{3,2,1,0:T(8,128)(2,1)S(1)} %get-tuple-element.182), channel_id=1, source_target_pairs={{0,1},{1,0},{2,3},{3,2},{4,5},{5,4},{6,7},{7,6},{8,9},{9,8},{10,11... | collective-permute-start | bytes 786440 | tf_op jit(solution)/shard_map/ppermute | solution.py:1018
  144.1 22.6 %collective-permute-start.25 = (bf16[216,16,128]{2,1,0:T(8,128)(2,1)S(1)}, bf16[216,16,128]{2,1,0:T(8,128)(2,1)S(1)}, u32[]{:S(2)}, u32[]{:S(2)}) collective-permute-start(bf16[216,16,128]{2,1,0:T(8,128)(2,1)S(1)} %get-tuple-element.185), channel_id=1, source_target_pairs={{0,16},{8,24},{16,0},{24,8},{1,17},{9,25},{17,1},{25,9},{2,18},{10... | collective-permute-start | bytes 2654216 | tf_op jit(solution)/shard_map/ppermute | solution.py:1018
  159.8 10.5 %collective-permute-start.30 = (bf16[384,128]{1,0:T(8,128)(2,1)S(1)}, bf16[384,128]{1,0:T(8,128)(2,1)S(1)}, u32[]{:S(2)}, u32[]{:S(2)}) collective-permute-start(bf16[384,128]{1,0:T(8,128)(2,1)S(1)} %get-tuple-element.198), channel_id=1, source_target_pairs={{0,4},{1,5},{2,6},{3,7},{4,0},{5,1},{6,2},{7,3},{8,12},{9,13},{10,... | collective-permute-start | bytes 294920 | tf_op jit(solution)/shard_map/ppermute | solution.py:1018
  160.7 10.7 %collective-permute-start.31 = (bf16[384,128]{1,0:T(8,128)(2,1)S(1)}, bf16[384,128]{1,0:T(8,128)(2,1)S(1)}, u32[]{:S(2)}, u32[]{:S(2)}) collective-permute-start(bf16[384,128]{1,0:T(8,128)(2,1)S(1)} %get-tuple-element.199), channel_id=1, source_target_pairs={{0,6},{1,7},{2,4},{3,5},{4,2},{5,3},{6,0},{7,1},{8,14},{9,15},{10,... | collective-permute-start | bytes 294920 | tf_op jit(solution)/shard_map/ppermute | solution.py:1018
  165.6 11.8 %collective-permute-start.34 = (bf16[384,128]{1,0:T(8,128)(2,1)S(1)}, bf16[384,128]{1,0:T(8,128)(2,1)S(1)}, u32[]{:S(2)}, u32[]{:S(2)}) collective-permute-start(bf16[384,128]{1,0:T(8,128)(2,1)S(1)} %get-tuple-element.207), channel_id=1, source_target_pairs={{0,4},{1,5},{2,6},{3,7},{4,0},{5,1},{6,2},{7,3},{8,12},{9,13},{10,... | collective-permute-start | bytes 294920 | tf_op jit(solution)/shard_map/ppermute | solution.py:1018
  166.7 10.7 %collective-permute-start.35 = (bf16[384,128]{1,0:T(8,128)(2,1)S(1)}, bf16[384,128]{1,0:T(8,128)(2,1)S(1)}, u32[]{:S(2)}, u32[]{:S(2)}) collective-permute-start(bf16[384,128]{1,0:T(8,128)(2,1)S(1)} %get-tuple-element.208), channel_id=1, source_target_pairs={{0,6},{1,7},{2,4},{3,5},{4,2},{5,3},{6,0},{7,1},{8,14},{9,15},{10,... | collective-permute-start | bytes 294920 | tf_op jit(solution)/shard_map/ppermute | solution.py:1018
  170.3 11.3 %collective-permute-start.36 = (bf16[108,16,128]{2,1,0:T(8,128)(2,1)S(1)}, bf16[108,16,128]{2,1,0:T(8,128)(2,1)S(1)}, u32[]{:S(2)}, u32[]{:S(2)}) collective-permute-start(bf16[108,16,128]{2,1,0:T(8,128)(2,1)S(1)} %get-tuple-element.211), channel_id=1, source_target_pairs={{0,1},{1,0},{2,3},{3,2},{4,5},{5,4},{6,7},{7,6},{8,9},{9,8},{10,11... | collective-permute-start | bytes 1327112 | tf_op jit(solution)/shard_map/ppermute | solution.py:1018
  181.8 13.7 %collective-permute-start.37 = (bf16[27,16,128]{2,1,0:T(8,128)(2,1)S(1)}, bf16[27,16,128]{2,1,0:T(8,128)(2,1)S(1)}, u32[]{:S(2)}, u32[]{:S(2)}) collective-permute-start(bf16[27,16,128]{2,1,0:T(8,128)(2,1)S(1)} %get-tuple-element.222), channel_id=1, source_target_pairs={{0,2},{1,3},{2,0},{3,1},{4,6},{5,7},{6,4},{7,5},{8,10},{9,11},{10,... | collective-permute-start | bytes 331784 | tf_op jit(solution)/shard_map/ppermute | solution.py:1018
  183.5 12.1 %collective-permute-start.38 = (bf16[27,16,128]{2,1,0:T(8,128)(2,1)S(1)}, bf16[27,16,128]{2,1,0:T(8,128)(2,1)S(1)}, u32[]{:S(2)}, u32[]{:S(2)}) collective-permute-start(bf16[27,16,128]{2,1,0:T(8,128)(2,1)S(1)} %get-tuple-element.223), channel_id=1, source_target_pairs={{0,4},{1,5},{2,6},{3,7},{4,0},{5,1},{6,2},{7,3},{8,12},{9,13},{10,... | collective-permute-start | bytes 331784 | tf_op jit(solution)/shard_map/ppermute | solution.py:1018
  184.6 11.0 %collective-permute-start.39 = (bf16[27,16,128]{2,1,0:T(8,128)(2,1)S(1)}, bf16[27,16,128]{2,1,0:T(8,128)(2,1)S(1)}, u32[]{:S(2)}, u32[]{:S(2)}) collective-permute-start(bf16[27,16,128]{2,1,0:T(8,128)(2,1)S(1)} %get-tuple-element.224), channel_id=1, source_target_pairs={{0,6},{1,7},{2,4},{3,5},{4,2},{5,3},{6,0},{7,1},{8,14},{9,15},{10,... | collective-permute-start | bytes 331784 | tf_op jit(solution)/shard_map/ppermute | solution.py:1018
  199.6 13.4 %collective-permute-start.45 = (bf16[88,16,128]{2,1,0:T(8,128)(2,1)S(1)}, bf16[88,16,128]{2,1,0:T(8,128)(2,1)S(1)}, u32[]{:S(2)}, u32[]{:S(2)}) collective-permute-start(bf16[88,16,128]{2,1,0:T(8,128)(2,1)S(1)} %get-tuple-element.232), channel_id=1, source_target_pairs={{0,16},{8,24},{16,0},{24,8},{1,17},{9,25},{17,1},{25,9},{2,18},{10... | collective-permute-start | bytes 1081352 | tf_op jit(solution)/shard_map/ppermute | solution.py:1018
  200.4 12.6 %collective-permute-start.46 = (bf16[88,16,128]{2,1,0:T(8,128)(2,1)S(1)}, bf16[88,16,128]{2,1,0:T(8,128)(2,1)S(1)}, u32[]{:S(2)}, u32[]{:S(2)}) collective-permute-start(bf16[88,16,128]{2,1,0:T(8,128)(2,1)S(1)} %get-tuple-element.234), channel_id=1, source_target_pairs={{0,1},{1,0},{2,3},{3,2},{4,5},{5,4},{6,7},{7,6},{8,9},{9,8},{10,11... | collective-permute-start | bytes 1081352 | tf_op jit(solution)/shard_map/ppermute | solution.py:1018
  220.2 10.3 %collective-permute-start.49 = (bf16[4,27,16,128]{3,2,1,0:T(8,128)(2,1)S(1)}, bf16[4,27,16,128]{3,2,1,0:T(8,128)(2,1)S(1)}, u32[]{:S(2)}, u32[]{:S(2)}) collective-permute-start(bf16[4,27,16,128]{3,2,1,0:T(8,128)(2,1)S(1)} %shard_map.291.refs_3_), channel_id=1, source_target_pairs={{0,1},{1,0},{2,3},{3,2},{4,5},{5,4},{6,7},{7,6},{8,9},{9,8},{10,11... | collective-permute-start | bytes 1327112 | tf_op jit(solution)/shard_map/ppermute | solution.py:1018
  (80 other events, 792.6 us)

commit v4 on v3

--- a/solution.py
+++ b/solution.py
@@ -1241,7 +1241,7 @@
             pltpu.VMEM((D, tokens), F32),
         ],
         us=10,
-        limit=34,
+        limit=62,
     )(fields, mask, *first)
     second = gather_blocks(
         second_own,

time: 259 us -> 257 us (level)
  local copies, waits for them, and re-layouts: 6.02 us -> 2.44 us
    unnamed x89 -> x85, local copies, waits for them, and re-layouts: 5.29 us -> 1.71 us
  transfers between devices with their start and end apart: 60 -> 60, of which waited for: 25 -> 25; matrix products, arithmetic and copies ran while one was open for 0% -> 0% of each run, Pallas kernels for 21% -> 22%
where the time goes in v4:
time: 257 us; the launch traced here: 255 us
  Pallas kernels  96.6 us (38%)
  waiting for transfers between devices  80.3 us (31%)
  starting transfers between devices  73.9 us (29%)
    pallas_call x27, Pallas kernels, run(): pl.pallas_call(kernel, out_shape=outs, grid=grid, in_specs=list(in_specs)...  96.6 us
    ppermute x60, waiting for transfers between devices, shift(): return lax.ppermute(value, axis, [(i, i ^ bit) for i in range(size)])  80.3 us
    ppermute x60, starting transfers between devices, shift(): return lax.ppermute(value, axis, [(i, i ^ bit) for i in range(size)])  73.9 us
  transfers between devices with their start and end apart: 60, of which 25 were waited for; matrix products, arithmetic and copies ran while one was open for 0% of the time, Pallas kernels for 22%

profile of v4, /device:TPU:0, one launch (start us, length us, event | category | flops | bytes accessed | tf_op | source)
XLA Modules:
  0.0 254.7 jit_solution(5515592819905918911)
XLA Ops:
  2.7 2.9 %collective-permute-start.1 = (bf16[96,1920]{1,0:T(8,128)(2,1)}, bf16[96,1920]{1,0:T(8,128)(2,1)S(1)}, u32[]{:S(2)}, u32[]{:S(2)}) collective-permute-start(bf16[96,1920]{1,0:T(8,128)(2,1)} %shard_map.271.refs_2_), channel_id=1, source_target_pairs={{0,16},{8,24},{16,0},{24,8},{1,17},{9,25},{17,1},{25,9},{2,18},{10... | collective-permute-start | bytes 1105928 | tf_op jit(solution)/shard_map/ppermute | solution.py:1018
  9.1 5.3 %collective-permute-done.1.refs_4_ = bf16[96,1920]{1,0:T(8,128)(2,1)S(1)} collective-permute-done((bf16[96,1920]{1,0:T(8,128)(2,1)}, bf16[96,1920]{1,0:T(8,128)(2,1)S(1)}, u32[]{:S(2)}, u32[]{:S(2)}) %collective-permute-start.1) | collective-permute-done | bytes 368672 | tf_op jit(solution)/shard_map/ppermute | solution.py:1018
  17.0 11.1 %shard_map.273 = (f32[2,480,256]{2,1,0:T(8,128)}, bf16[6,2,1104,256]{3,2,1,0:T(8,128)(2,1)}, bf16[512,384]{1,0:T(8,128)(2,1)}, bf16[384,768]{1,0:T(8,128)(2,1)},...) custom-call(bf16[2,1104,256]{2,1,0:T(8,128)(2,1)} %bitcast.26, ...), custom_call_target="tpu_custom_call" | custom-call | flops 11500000256 | bytes 1024 | tf_op jit(solution)/shard_map/pallas_call | solution.py:90
  33.0 4.1 %shard_map.275 = (f32[512,384]{1,0:T(8,128)}, bf16[512,384]{1,0:T(8,128)(2,1)}, bf16[384,1536]{1,0:T(8,128)(2,1)}, f32[8,2304]{1,0:T(8,128)}, bf16[1168,128]{1,0...) custom-call(s32[2]{0:T(128)S(1)} %copy-done.12, ...), custom_call_target="tpu_custom_call" | custom-call | flops 4600000000 | bytes 1024 | tf_op jit(solution)/shard_map/pallas_call | solution.py:90
  43.2 8.5 %collective-permute-done.6.refs_1_ = bf16[1168,128]{1,0:T(8,128)(2,1)S(1)} collective-permute-done((bf16[1168,128]{1,0:T(8,128)(2,1)S(1)}, bf16[1168,128]{1,0:T(8,128)(2,1)S(1)}, u32[]{:S(2)}, u32[]{:S(2)}) %collective-permute-start.6) | collective-permute-done | bytes 299040 | tf_op jit(solution)/shard_map/ppermute | solution.py:1018
  53.3 9.2 %collective-permute-done.7.refs_2_ = bf16[1168,128]{1,0:T(8,128)(2,1)S(1)} collective-permute-done((bf16[1168,128]{1,0:T(8,128)(2,1)S(1)}, bf16[1168,128]{1,0:T(8,128)(2,1)S(1)}, u32[]{:S(2)}, u32[]{:S(2)}) %collective-permute-start.7) | collective-permute-done | bytes 299040 | tf_op jit(solution)/shard_map/ppermute | solution.py:1018
  65.3 3.0 %collective-permute-done.11.refs_6_ = bf16[784,128]{1,0:T(8,128)(2,1)S(1)} collective-permute-done((bf16[784,128]{1,0:T(8,128)(2,1)S(1)}, bf16[784,128]{1,0:T(8,128)(2,1)S(1)}, u32[]{:S(2)}, u32[]{:S(2)}) %collective-permute-start.11) | collective-permute-done | bytes 200736 | tf_op jit(solution)/shard_map/ppermute | solution.py:1018
  70.5 9.0 %shard_map.276 = (bf16[3,128,128]{2,1,0:T(8,128)(2,1)S(1)}, bf16[3,128,128]{2,1,0:T(8,128)(2,1)S(1)}, bf16[3,128,128]{2,1,0:T(8,128)(2,1)S(1)}, bf16[3,128,128]{...) custom-call(bf16[1168,128]{1,0:T(8,128)(2,1)S(1)} %get-tuple-element.200.refs_0_, ...), custom_call_target="tpu_custom_call" | custom-call | flops 10350000128 | bytes 1024 | tf_op jit(solution)/shard_map/pallas_call | solution.py:90
  79.5 3.5 %collective-permute-start.13 = (bf16[3,128,128]{2,1,0:T(8,128)(2,1)S(1)}, bf16[3,128,128]{2,1,0:T(8,128)(2,1)S(1)}, u32[]{:S(2)}, u32[]{:S(2)}) collective-permute-start(bf16[3,128,128]{2,1,0:T(8,128)(2,1)S(1)} %get-tuple-element.156), channel_id=1, source_target_pairs={{0,2},{1,3},{2,0},{3,1},{4,6},{5,7},{6,4},{7,5},{8,10},{9,11},{10,... | collective-permute-start | bytes 294920 | tf_op jit(solution)/shard_map/ppermute | solution.py:1018
  85.8 5.4 %collective-permute-done.14.refs_9_ = bf16[3,128,128]{2,1,0:T(8,128)(2,1)S(1)} collective-permute-done((bf16[3,128,128]{2,1,0:T(8,128)(2,1)S(1)}, bf16[3,128,128]{2,1,0:T(8,128)(2,1)S(1)}, u32[]{:S(2)}, u32[]{:S(2)}) %collective-permute-start.14) | collective-permute-done | bytes 98336 | tf_op jit(solution)/shard_map/ppermute | solution.py:1018
  91.9 21.5 %shard_map.277 = (f32[512,384]{1,0:T(8,128)}, f32[2,8,384]{2,1,0:T(8,128)}, f32[8,128]{1,0:T(8,128)}, bf16[3,128,128]{2,1,0:T(8,128)(2,1)S(1)}, bf16[3,128,128]{...) custom-call(s32[2]{0:T(128)S(1)} %copy-done.12, ...), custom_call_target="tpu_custom_call" | custom-call | flops 12650000384 | bytes 1024 | tf_op jit(solution)/shard_map/pallas_call | solution.py:90
  121.4 7.2 %collective-permute-done.21.refs_10_ = bf16[3,128,128]{2,1,0:T(8,128)(2,1)S(1)} collective-permute-done((bf16[3,128,128]{2,1,0:T(8,128)(2,1)S(1)}, bf16[3,128,128]{2,1,0:T(8,128)(2,1)S(1)}, u32[]{:S(2)}, u32[]{:S(2)}) %collective-permute-start.21) | collective-permute-done | bytes 98336 | tf_op jit(solution)/shard_map/ppermute | solution.py:1018
  128.7 5.5 %shard_map.280 = (bf16[1,4,128,128]{3,2,1,0:T(8,128)(2,1)S(1)}, bf16[1,4,256,128]{3,2,1,0:T(8,128)(2,1)S(1)}, bf16[1,4,256,128]{3,2,1,0:T(8,128)(2,1)S(1)}) custom-call(bf16[1168,128]{1,0:T(8,128)(2,1)S(1)} %get-tuple-element.200.refs_0_, bf16[1168,128]{1,0:T(8,128)(2,1)S(1)} %collective-permute-done.6.refs_1_, ...), custom_call_target="tpu_custom_call" | custom-call | flops 6899999744 | bytes 1024 | tf_op jit(solution)/shard_map/pallas_call | solution.py:90
  135.7 5.9 %shard_map.281 = (bf16[1,4,128,128]{3,2,1,0:T(8,128)(2,1)S(1)}, bf16[1,4,256,128]{3,2,1,0:T(8,128)(2,1)S(1)}, bf16[1,4,256,128]{3,2,1,0:T(8,128)(2,1)S(1)}) custom-call(bf16[1168,128]{1,0:T(8,128)(2,1)S(1)} %get-tuple-element.200.refs_0_, bf16[1168,128]{1,0:T(8,128)(2,1)S(1)} %collective-permute-done.6.refs_1_, ...), custom_call_target="tpu_custom_call" | custom-call | flops 6899999744 | bytes 1024 | tf_op jit(solution)/shard_map/pallas_call | solution.py:90
  147.3 5.5 %shard_map.285 = (bf16[1,4,128,128]{3,2,1,0:T(8,128)(2,1)S(1)}, bf16[1,4,256,128]{3,2,1,0:T(8,128)(2,1)S(1)}, bf16[1,4,256,128]{3,2,1,0:T(8,128)(2,1)S(1)}) custom-call(bf16[1168,128]{1,0:T(8,128)(2,1)S(1)} %get-tuple-element.200.refs_0_, bf16[1168,128]{1,0:T(8,128)(2,1)S(1)} %collective-permute-done.6.refs_1_, ...), custom_call_target="tpu_custom_call" | custom-call | flops 6899999744 | bytes 1024 | tf_op jit(solution)/shard_map/pallas_call | solution.py:90
  168.7 6.0 %collective-permute-done.34.refs_18_ = bf16[384,128]{1,0:T(8,128)(2,1)S(1)} collective-permute-done((bf16[384,128]{1,0:T(8,128)(2,1)S(1)}, bf16[384,128]{1,0:T(8,128)(2,1)S(1)}, u32[]{:S(2)}, u32[]{:S(2)}) %collective-permute-start.34) | collective-permute-done | bytes 98336 | tf_op jit(solution)/shard_map/ppermute | solution.py:1018
  174.8 4.0 %shard_map.287 = (bf16[2,384,256]{2,1,0:T(8,128)(2,1)S(1)}, bf16[2,96,1664]{2,1,0:T(8,128)(2,1)S(1)}, bf16[2,96,1664]{2,1,0:T(8,128)(2,1)S(1)}) custom-call(s32[2]{0:T(128)S(1)} %copy-done.12, f32[512,384]{1,0:T(8,128)S(1)} %copy-done.19, bf16[512,384]{1,0:T(8,128)(2,1)S(1)} %copy-done.23, f32[512,384]{1,0:T(8,128)S(1)} %copy-done.20, ...), custom_call_target="tpu_custom_call" | custom-call | flops 4600000000 | bytes 1024 | tf_op jit(solution)/shard_map/pallas_call | solution.py:90
  183.7 9.3 %shard_map.289 = (bf16[2,96,1920]{2,1,0:T(8,128)(2,1)S(1)}, bf16[2,96,1920]{2,1,0:T(8,128)(2,1)S(1)}) custom-call(bf16[2,384,256]{2,1,0:T(8,128)(2,1)S(1)} %get-tuple-element.213.refs_0_, f32[2,480,256]{2,1,0:T(8,128)S(1)} %copy-done.24, bf16[6,2,1104,256]{3,2,1,0:T(8,128)(2,1)S(1)} %bitcast.35, bf16[2,1104,256]{2,1,0:T(8,128)(2,1)S(1)} %bitcast.27, ...), custom_call_target="tpu_custom_call" | custom-call | flops 14949999616 | bytes 1024 | tf_op jit(solution)/shard_map/pallas_call | solution.py:90
  203.4 3.4 %collective-permute-done.42.refs_3_ = bf16[27,16,128]{2,1,0:T(8,128)(2,1)S(1)} collective-permute-done((bf16[27,16,128]{2,1,0:T(8,128)(2,1)S(1)}, bf16[27,16,128]{2,1,0:T(8,128)(2,1)S(1)}, u32[]{:S(2)}, u32[]{:S(2)}) %collective-permute-start.42) | collective-permute-done | bytes 110624 | tf_op jit(solution)/shard_map/ppermute | solution.py:1018
  206.8 4.2 %collective-permute-done.41.refs_2_ = bf16[27,16,128]{2,1,0:T(8,128)(2,1)S(1)} collective-permute-done((bf16[27,16,128]{2,1,0:T(8,128)(2,1)S(1)}, bf16[27,16,128]{2,1,0:T(8,128)(2,1)S(1)}, u32[]{:S(2)}, u32[]{:S(2)}) %collective-permute-start.41) | collective-permute-done | bytes 110624 | tf_op jit(solution)/shard_map/ppermute | solution.py:1018
  213.6 3.7 %collective-permute-done.48.refs_3_ = bf16[44,16,128]{2,1,0:T(8,128)(2,1)S(1)} collective-permute-done((bf16[44,16,128]{2,1,0:T(8,128)(2,1)S(1)}, bf16[44,16,128]{2,1,0:T(8,128)(2,1)S(1)}, u32[]{:S(2)}, u32[]{:S(2)}) %collective-permute-start.48) | collective-permute-done | bytes 180256 | tf_op jit(solution)/shard_map/ppermute | solution.py:1018
  219.4 3.0 %collective-permute-start.51 = (bf16[22,16,128]{2,1,0:T(8,128)(2,1)S(1)}, bf16[22,16,128]{2,1,0:T(8,128)(2,1)S(1)}, u32[]{:S(2)}, u32[]{:S(2)}) collective-permute-start(bf16[22,16,128]{2,1,0:T(8,128)(2,1)S(1)} %get-tuple-element.248), channel_id=1, source_target_pairs={{0,4},{1,5},{2,6},{3,7},{4,0},{5,1},{6,2},{7,3},{8,12},{9,13},{10,... | collective-permute-start | bytes 270344 | tf_op jit(solution)/shard_map/ppermute | solution.py:1018
  223.7 4.1 %collective-permute-done.49.refs_4_ = bf16[4,27,16,128]{3,2,1,0:T(8,128)(2,1)S(1)} collective-permute-done((bf16[4,27,16,128]{3,2,1,0:T(8,128)(2,1)S(1)}, bf16[4,27,16,128]{3,2,1,0:T(8,128)(2,1)S(1)}, u32[]{:S(2)}, u32[]{:S(2)}) %collective-permute-start.49) | collective-permute-done | bytes 442400 | tf_op jit(solution)/shard_map/ppermute | solution.py:1018
  247.2 7.3 %shard_map.297 = (f32[1,1]{1,0:T(1,128)}, f32[1,1]{1,0:T(1,128)}, f32[1,1]{1,0:T(1,128)}, f32[96,7632]{1,0:T(8,128)}, f32[96,7632]{1,0:T(8,128)}, /*index=5*/f32...) custom-call(f32[8,128]{1,0:T(8,128)S(1)} %add.13.refs_0_, ...), custom_call_target="tpu_custom_call" | custom-call | flops 11500000256 | bytes 1024 | tf_op jit(solution)/shard_map/pallas_call | solution.py:90
  (217 shorter events, 100.5 us)
Async XLA Ops:
  2.7 11.7 %collective-permute-start.1 = (bf16[96,1920]{1,0:T(8,128)(2,1)}, bf16[96,1920]{1,0:T(8,128)(2,1)S(1)}, u32[]{:S(2)}, u32[]{:S(2)}) collective-permute-start(bf16[96,1920]{1,0:T(8,128)(2,1)} %shard_map.271.refs_2_), channel_id=1, source_target_pairs={{0,16},{8,24},{16,0},{24,8},{1,17},{9,25},{17,1},{25,9},{2,18},{10... | collective-permute-start | bytes 1105928 | tf_op jit(solution)/shard_map/ppermute | solution.py:1018
  14.4 13.8 %collective-permute-start.4 = (bf16[128,1536]{1,0:T(8,128)(2,1)}, bf16[128,1536]{1,0:T(8,128)(2,1)S(1)}, u32[]{:S(2)}, u32[]{:S(2)}) collective-permute-start(bf16[128,1536]{1,0:T(8,128)(2,1)} %shard_map.272.refs_2_), channel_id=1, source_target_pairs={{0,16},{8,24},{16,0},{24,8},{1,17},{9,25},{17,1},{25,9},{2,18},{10... | collective-permute-start | bytes 1179656 | tf_op jit(solution)/shard_map/ppermute | solution.py:1018
  31.4 33.4 %collective-permute-start.17 = (bf16[96,4608]{1,0:T(8,128)(2,1)}, bf16[96,4608]{1,0:T(8,128)(2,1)S(1)}, u32[]{:S(2)}, u32[]{:S(2)}) collective-permute-start(bf16[96,4608]{1,0:T(8,128)(2,1)} %shard_map.274.refs_11_), channel_id=1, source_target_pairs={{0,16},{8,24},{16,0},{24,8},{1,17},{9,25},{17,1},{25,9},{2,18},{10... | collective-permute-start | bytes 2654216 | tf_op jit(solution)/shard_map/ppermute | solution.py:1018
  37.1 14.6 %collective-permute-start.6 = (bf16[1168,128]{1,0:T(8,128)(2,1)S(1)}, bf16[1168,128]{1,0:T(8,128)(2,1)S(1)}, u32[]{:S(2)}, u32[]{:S(2)}) collective-permute-start(bf16[1168,128]{1,0:T(8,128)(2,1)S(1)} %get-tuple-element.150), channel_id=1, source_target_pairs={{0,2},{1,3},{2,0},{3,1},{4,6},{5,7},{6,4},{7,5},{8,10},{9,11},{10,... | collective-permute-start | bytes 897032 | tf_op jit(solution)/shard_map/ppermute | solution.py:1018
  38.8 23.7 %collective-permute-start.7 = (bf16[1168,128]{1,0:T(8,128)(2,1)S(1)}, bf16[1168,128]{1,0:T(8,128)(2,1)S(1)}, u32[]{:S(2)}, u32[]{:S(2)}) collective-permute-start(bf16[1168,128]{1,0:T(8,128)(2,1)S(1)} %get-tuple-element.151), channel_id=1, source_target_pairs={{0,4},{1,5},{2,6},{3,7},{4,0},{5,1},{6,2},{7,3},{8,12},{9,13},{10,... | collective-permute-start | bytes 897032 | tf_op jit(solution)/shard_map/ppermute | solution.py:1018
  41.4 22.7 %collective-permute-start.8 = (bf16[1168,128]{1,0:T(8,128)(2,1)S(1)}, bf16[1168,128]{1,0:T(8,128)(2,1)S(1)}, u32[]{:S(2)}, u32[]{:S(2)}) collective-permute-start(bf16[1168,128]{1,0:T(8,128)(2,1)S(1)} %get-tuple-element.152), channel_id=1, source_target_pairs={{0,6},{1,7},{2,4},{3,5},{4,2},{5,3},{6,0},{7,1},{8,14},{9,15},{10,... | collective-permute-start | bytes 897032 | tf_op jit(solution)/shard_map/ppermute | solution.py:1018
  41.6 23.2 %collective-permute-start.9 = (bf16[784,128]{1,0:T(8,128)(2,1)S(1)}, bf16[784,128]{1,0:T(8,128)(2,1)S(1)}, u32[]{:S(2)}, u32[]{:S(2)}) collective-permute-start(bf16[784,128]{1,0:T(8,128)(2,1)S(1)} %slice.12), channel_id=1, source_target_pairs={{0,1},{1,0},{2,3},{3,2},{4,5},{5,4},{6,7},{7,6},{8,9},{9,8},{10,11... | collective-permute-start | bytes 602120 | tf_op jit(solution)/shard_map/ppermute | solution.py:1018
  51.8 13.6 %collective-permute-start.10 = (bf16[784,128]{1,0:T(8,128)(2,1)S(1)}, bf16[784,128]{1,0:T(8,128)(2,1)S(1)}, u32[]{:S(2)}, u32[]{:S(2)}) collective-permute-start(bf16[784,128]{1,0:T(8,128)(2,1)S(1)} %slice.16), channel_id=1, source_target_pairs={{0,1},{1,0},{2,3},{3,2},{4,5},{5,4},{6,7},{7,6},{8,9},{9,8},{10,11... | collective-permute-start | bytes 602120 | tf_op jit(solution)/shard_map/ppermute | solution.py:1018
  64.8 20.7 %collective-permute-start.16 = (bf16[96,4608]{1,0:T(8,128)(2,1)S(1)}, bf16[96,4608]{1,0:T(8,128)(2,1)S(1)}, u32[]{:S(2)}, u32[]{:S(2)}) collective-permute-start(bf16[96,4608]{1,0:T(8,128)(2,1)S(1)} %copy-done.2), channel_id=1, source_target_pairs={{0,8},{8,0},{16,24},{24,16},{1,9},{9,1},{17,25},{25,17},{2,10},{10... | collective-permute-start | bytes 2654216 | tf_op jit(solution)/shard_map/ppermute | solution.py:1018
  64.8 26.4 %collective-permute-start.18 = (bf16[96,4608]{1,0:T(8,128)(2,1)S(1)}, bf16[96,4608]{1,0:T(8,128)(2,1)S(1)}, u32[]{:S(2)}, u32[]{:S(2)}) collective-permute-start(bf16[96,4608]{1,0:T(8,128)(2,1)S(1)} %collective-permute-done.17.refs_13_), channel_id=1, source_target_pairs={{0,8},{8,0},{16,24},{24,16},{1,9},{9,1},{17,25},{25,17},{2,10},{10... | collective-permute-start | bytes 2654216 | tf_op jit(solution)/shard_map/ppermute | solution.py:1018
  117.9 10.8 %collective-permute-start.21 = (bf16[3,128,128]{2,1,0:T(8,128)(2,1)S(1)}, bf16[3,128,128]{2,1,0:T(8,128)(2,1)S(1)}, u32[]{:S(2)}, u32[]{:S(2)}) collective-permute-start(bf16[3,128,128]{2,1,0:T(8,128)(2,1)S(1)} %get-tuple-element.174), channel_id=1, source_target_pairs={{0,4},{1,5},{2,6},{3,7},{4,0},{5,1},{6,2},{7,3},{8,12},{9,13},{10,... | collective-permute-start | bytes 294920 | tf_op jit(solution)/shard_map/ppermute | solution.py:1018
  141.6 13.8 %collective-permute-start.23 = (bf16[1,4,256,128]{3,2,1,0:T(8,128)(2,1)S(1)}, bf16[1,4,256,128]{3,2,1,0:T(8,128)(2,1)S(1)}, u32[]{:S(2)}, u32[]{:S(2)}) collective-permute-start(bf16[1,4,256,128]{3,2,1,0:T(8,128)(2,1)S(1)} %get-tuple-element.182), channel_id=1, source_target_pairs={{0,1},{1,0},{2,3},{3,2},{4,5},{5,4},{6,7},{7,6},{8,9},{9,8},{10,11... | collective-permute-start | bytes 786440 | tf_op jit(solution)/shard_map/ppermute | solution.py:1018
  142.2 21.8 %collective-permute-start.25 = (bf16[216,16,128]{2,1,0:T(8,128)(2,1)S(1)}, bf16[216,16,128]{2,1,0:T(8,128)(2,1)S(1)}, u32[]{:S(2)}, u32[]{:S(2)}) collective-permute-start(bf16[216,16,128]{2,1,0:T(8,128)(2,1)S(1)} %get-tuple-element.185), channel_id=1, source_target_pairs={{0,16},{8,24},{16,0},{24,8},{1,17},{9,25},{17,1},{25,9},{2,18},{10... | collective-permute-start | bytes 2654216 | tf_op jit(solution)/shard_map/ppermute | solution.py:1018
  157.2 10.5 %collective-permute-start.30 = (bf16[384,128]{1,0:T(8,128)(2,1)S(1)}, bf16[384,128]{1,0:T(8,128)(2,1)S(1)}, u32[]{:S(2)}, u32[]{:S(2)}) collective-permute-start(bf16[384,128]{1,0:T(8,128)(2,1)S(1)} %get-tuple-element.198), channel_id=1, source_target_pairs={{0,4},{1,5},{2,6},{3,7},{4,0},{5,1},{6,2},{7,3},{8,12},{9,13},{10,... | collective-permute-start | bytes 294920 | tf_op jit(solution)/shard_map/ppermute | solution.py:1018
  158.1 10.7 %collective-permute-start.31 = (bf16[384,128]{1,0:T(8,128)(2,1)S(1)}, bf16[384,128]{1,0:T(8,128)(2,1)S(1)}, u32[]{:S(2)}, u32[]{:S(2)}) collective-permute-start(bf16[384,128]{1,0:T(8,128)(2,1)S(1)} %get-tuple-element.199), channel_id=1, source_target_pairs={{0,6},{1,7},{2,4},{3,5},{4,2},{5,3},{6,0},{7,1},{8,14},{9,15},{10,... | collective-permute-start | bytes 294920 | tf_op jit(solution)/shard_map/ppermute | solution.py:1018
  162.9 11.8 %collective-permute-start.34 = (bf16[384,128]{1,0:T(8,128)(2,1)S(1)}, bf16[384,128]{1,0:T(8,128)(2,1)S(1)}, u32[]{:S(2)}, u32[]{:S(2)}) collective-permute-start(bf16[384,128]{1,0:T(8,128)(2,1)S(1)} %get-tuple-element.207), channel_id=1, source_target_pairs={{0,4},{1,5},{2,6},{3,7},{4,0},{5,1},{6,2},{7,3},{8,12},{9,13},{10,... | collective-permute-start | bytes 294920 | tf_op jit(solution)/shard_map/ppermute | solution.py:1018
  164.1 10.7 %collective-permute-start.35 = (bf16[384,128]{1,0:T(8,128)(2,1)S(1)}, bf16[384,128]{1,0:T(8,128)(2,1)S(1)}, u32[]{:S(2)}, u32[]{:S(2)}) collective-permute-start(bf16[384,128]{1,0:T(8,128)(2,1)S(1)} %get-tuple-element.208), channel_id=1, source_target_pairs={{0,6},{1,7},{2,4},{3,5},{4,2},{5,3},{6,0},{7,1},{8,14},{9,15},{10,... | collective-permute-start | bytes 294920 | tf_op jit(solution)/shard_map/ppermute | solution.py:1018
  167.6 11.3 %collective-permute-start.36 = (bf16[108,16,128]{2,1,0:T(8,128)(2,1)S(1)}, bf16[108,16,128]{2,1,0:T(8,128)(2,1)S(1)}, u32[]{:S(2)}, u32[]{:S(2)}) collective-permute-start(bf16[108,16,128]{2,1,0:T(8,128)(2,1)S(1)} %get-tuple-element.211), channel_id=1, source_target_pairs={{0,1},{1,0},{2,3},{3,2},{4,5},{5,4},{6,7},{7,6},{8,9},{9,8},{10,11... | collective-permute-start | bytes 1327112 | tf_op jit(solution)/shard_map/ppermute | solution.py:1018
  179.1 13.9 %collective-permute-start.37 = (bf16[27,16,128]{2,1,0:T(8,128)(2,1)S(1)}, bf16[27,16,128]{2,1,0:T(8,128)(2,1)S(1)}, u32[]{:S(2)}, u32[]{:S(2)}) collective-permute-start(bf16[27,16,128]{2,1,0:T(8,128)(2,1)S(1)} %get-tuple-element.222), channel_id=1, source_target_pairs={{0,2},{1,3},{2,0},{3,1},{4,6},{5,7},{6,4},{7,5},{8,10},{9,11},{10,... | collective-permute-start | bytes 331784 | tf_op jit(solution)/shard_map/ppermute | solution.py:1018
  180.8 12.2 %collective-permute-start.38 = (bf16[27,16,128]{2,1,0:T(8,128)(2,1)S(1)}, bf16[27,16,128]{2,1,0:T(8,128)(2,1)S(1)}, u32[]{:S(2)}, u32[]{:S(2)}) collective-permute-start(bf16[27,16,128]{2,1,0:T(8,128)(2,1)S(1)} %get-tuple-element.223), channel_id=1, source_target_pairs={{0,4},{1,5},{2,6},{3,7},{4,0},{5,1},{6,2},{7,3},{8,12},{9,13},{10,... | collective-permute-start | bytes 331784 | tf_op jit(solution)/shard_map/ppermute | solution.py:1018
  181.9 11.1 %collective-permute-start.39 = (bf16[27,16,128]{2,1,0:T(8,128)(2,1)S(1)}, bf16[27,16,128]{2,1,0:T(8,128)(2,1)S(1)}, u32[]{:S(2)}, u32[]{:S(2)}) collective-permute-start(bf16[27,16,128]{2,1,0:T(8,128)(2,1)S(1)} %get-tuple-element.224), channel_id=1, source_target_pairs={{0,6},{1,7},{2,4},{3,5},{4,2},{5,3},{6,0},{7,1},{8,14},{9,15},{10,... | collective-permute-start | bytes 331784 | tf_op jit(solution)/shard_map/ppermute | solution.py:1018
  197.0 14.1 %collective-permute-start.45 = (bf16[88,16,128]{2,1,0:T(8,128)(2,1)S(1)}, bf16[88,16,128]{2,1,0:T(8,128)(2,1)S(1)}, u32[]{:S(2)}, u32[]{:S(2)}) collective-permute-start(bf16[88,16,128]{2,1,0:T(8,128)(2,1)S(1)} %get-tuple-element.232), channel_id=1, source_target_pairs={{0,16},{8,24},{16,0},{24,8},{1,17},{9,25},{17,1},{25,9},{2,18},{10... | collective-permute-start | bytes 1081352 | tf_op jit(solution)/shard_map/ppermute | solution.py:1018
  198.5 12.6 %collective-permute-start.46 = (bf16[88,16,128]{2,1,0:T(8,128)(2,1)S(1)}, bf16[88,16,128]{2,1,0:T(8,128)(2,1)S(1)}, u32[]{:S(2)}, u32[]{:S(2)}) collective-permute-start(bf16[88,16,128]{2,1,0:T(8,128)(2,1)S(1)} %get-tuple-element.234), channel_id=1, source_target_pairs={{0,1},{1,0},{2,3},{3,2},{4,5},{5,4},{6,7},{7,6},{8,9},{9,8},{10,11... | collective-permute-start | bytes 1081352 | tf_op jit(solution)/shard_map/ppermute | solution.py:1018
  217.6 10.3 %collective-permute-start.49 = (bf16[4,27,16,128]{3,2,1,0:T(8,128)(2,1)S(1)}, bf16[4,27,16,128]{3,2,1,0:T(8,128)(2,1)S(1)}, u32[]{:S(2)}, u32[]{:S(2)}) collective-permute-start(bf16[4,27,16,128]{3,2,1,0:T(8,128)(2,1)S(1)} %shard_map.291.refs_3_), channel_id=1, source_target_pairs={{0,1},{1,0},{2,3},{3,2},{4,5},{5,4},{6,7},{7,6},{8,9},{9,8},{10,11... | collective-permute-start | bytes 1327112 | tf_op jit(solution)/shard_map/ppermute | solution.py:1018
  (78 other events, 800.8 us)

commit v5 on v4

--- a/solution.py
+++ b/solution.py
@@ -81,7 +81,7 @@
 
 
 def call(
-    kernel, outs, grid=(), in_specs=None, out_specs=None, scratch=(), us=1, limit=34, after=()
+    kernel, outs, grid=(), in_specs=None, out_specs=None, scratch=(), us=1, limit=16, after=()
 ):
     def run(*args):
         if after:

time: 257 us -> 257 us (level)
  no operation moved by 1% of the time
where the time goes in v5:
time: 257 us; the launch traced here: 255 us
  Pallas kernels  96.6 us (38%)
  waiting for transfers between devices  80.2 us (31%)
  starting transfers between devices  73.9 us (29%)
    pallas_call x27, Pallas kernels, run(): pl.pallas_call(kernel, out_shape=outs, grid=grid, in_specs=list(in_specs)...  96.6 us
    ppermute x60, waiting for transfers between devices, shift(): return lax.ppermute(value, axis, [(i, i ^ bit) for i in range(size)])  80.2 us
    ppermute x60, starting transfers between devices, shift(): return lax.ppermute(value, axis, [(i, i ^ bit) for i in range(size)])  73.9 us
  transfers between devices with their start and end apart: 60, of which 25 were waited for; matrix products, arithmetic and copies ran while one was open for 0% of the time, Pallas kernels for 22%

profile of v5, /device:TPU:0, one launch (start us, length us, event | category | flops | bytes accessed | tf_op | source)
XLA Modules:
  0.0 254.7 jit_solution(10162810631899902638)
XLA Ops:
  2.7 2.9 %collective-permute-start.1 = (bf16[96,1920]{1,0:T(8,128)(2,1)}, bf16[96,1920]{1,0:T(8,128)(2,1)S(1)}, u32[]{:S(2)}, u32[]{:S(2)}) collective-permute-start(bf16[96,1920]{1,0:T(8,128)(2,1)} %shard_map.271.refs_2_), channel_id=1, source_target_pairs={{0,16},{8,24},{16,0},{24,8},{1,17},{9,25},{17,1},{25,9},{2,18},{10... | collective-permute-start | bytes 1105928 | tf_op jit(solution)/shard_map/ppermute | solution.py:1018
  9.1 5.3 %collective-permute-done.1.refs_4_ = bf16[96,1920]{1,0:T(8,128)(2,1)S(1)} collective-permute-done((bf16[96,1920]{1,0:T(8,128)(2,1)}, bf16[96,1920]{1,0:T(8,128)(2,1)S(1)}, u32[]{:S(2)}, u32[]{:S(2)}) %collective-permute-start.1) | collective-permute-done | bytes 368672 | tf_op jit(solution)/shard_map/ppermute | solution.py:1018
  17.0 11.1 %shard_map.273 = (f32[2,480,256]{2,1,0:T(8,128)}, bf16[6,2,1104,256]{3,2,1,0:T(8,128)(2,1)}, bf16[512,384]{1,0:T(8,128)(2,1)}, bf16[384,768]{1,0:T(8,128)(2,1)},...) custom-call(bf16[2,1104,256]{2,1,0:T(8,128)(2,1)} %bitcast.26, ...), custom_call_target="tpu_custom_call" | custom-call | flops 11500000256 | bytes 1024 | tf_op jit(solution)/shard_map/pallas_call | solution.py:90
  33.0 4.1 %shard_map.275 = (f32[512,384]{1,0:T(8,128)}, bf16[512,384]{1,0:T(8,128)(2,1)}, bf16[384,1536]{1,0:T(8,128)(2,1)}, f32[8,2304]{1,0:T(8,128)}, bf16[1168,128]{1,0...) custom-call(s32[2]{0:T(128)S(1)} %copy-done.12, ...), custom_call_target="tpu_custom_call" | custom-call | flops 4600000000 | bytes 1024 | tf_op jit(solution)/shard_map/pallas_call | solution.py:90
  43.2 8.5 %collective-permute-done.6.refs_1_ = bf16[1168,128]{1,0:T(8,128)(2,1)S(1)} collective-permute-done((bf16[1168,128]{1,0:T(8,128)(2,1)S(1)}, bf16[1168,128]{1,0:T(8,128)(2,1)S(1)}, u32[]{:S(2)}, u32[]{:S(2)}) %collective-permute-start.6) | collective-permute-done | bytes 299040 | tf_op jit(solution)/shard_map/ppermute | solution.py:1018
  53.3 9.2 %collective-permute-done.7.refs_2_ = bf16[1168,128]{1,0:T(8,128)(2,1)S(1)} collective-permute-done((bf16[1168,128]{1,0:T(8,128)(2,1)S(1)}, bf16[1168,128]{1,0:T(8,128)(2,1)S(1)}, u32[]{:S(2)}, u32[]{:S(2)}) %collective-permute-start.7) | collective-permute-done | bytes 299040 | tf_op jit(solution)/shard_map/ppermute | solution.py:1018
  65.3 3.0 %collective-permute-done.11.refs_6_ = bf16[784,128]{1,0:T(8,128)(2,1)S(1)} collective-permute-done((bf16[784,128]{1,0:T(8,128)(2,1)S(1)}, bf16[784,128]{1,0:T(8,128)(2,1)S(1)}, u32[]{:S(2)}, u32[]{:S(2)}) %collective-permute-start.11) | collective-permute-done | bytes 200736 | tf_op jit(solution)/shard_map/ppermute | solution.py:1018
  70.5 9.0 %shard_map.276 = (bf16[3,128,128]{2,1,0:T(8,128)(2,1)S(1)}, bf16[3,128,128]{2,1,0:T(8,128)(2,1)S(1)}, bf16[3,128,128]{2,1,0:T(8,128)(2,1)S(1)}, bf16[3,128,128]{...) custom-call(bf16[1168,128]{1,0:T(8,128)(2,1)S(1)} %get-tuple-element.200.refs_0_, ...), custom_call_target="tpu_custom_call" | custom-call | flops 10350000128 | bytes 1024 | tf_op jit(solution)/shard_map/pallas_call | solution.py:90
  79.5 3.5 %collective-permute-start.13 = (bf16[3,128,128]{2,1,0:T(8,128)(2,1)S(1)}, bf16[3,128,128]{2,1,0:T(8,128)(2,1)S(1)}, u32[]{:S(2)}, u32[]{:S(2)}) collective-permute-start(bf16[3,128,128]{2,1,0:T(8,128)(2,1)S(1)} %get-tuple-element.156), channel_id=1, source_target_pairs={{0,2},{1,3},{2,0},{3,1},{4,6},{5,7},{6,4},{7,5},{8,10},{9,11},{10,... | collective-permute-start | bytes 294920 | tf_op jit(solution)/shard_map/ppermute | solution.py:1018
  85.8 5.4 %collective-permute-done.14.refs_9_ = bf16[3,128,128]{2,1,0:T(8,128)(2,1)S(1)} collective-permute-done((bf16[3,128,128]{2,1,0:T(8,128)(2,1)S(1)}, bf16[3,128,128]{2,1,0:T(8,128)(2,1)S(1)}, u32[]{:S(2)}, u32[]{:S(2)}) %collective-permute-start.14) | collective-permute-done | bytes 98336 | tf_op jit(solution)/shard_map/ppermute | solution.py:1018
  91.9 21.5 %shard_map.277 = (f32[512,384]{1,0:T(8,128)}, f32[2,8,384]{2,1,0:T(8,128)}, f32[8,128]{1,0:T(8,128)}, bf16[3,128,128]{2,1,0:T(8,128)(2,1)S(1)}, bf16[3,128,128]{...) custom-call(s32[2]{0:T(128)S(1)} %copy-done.12, ...), custom_call_target="tpu_custom_call" | custom-call | flops 12650000384 | bytes 1024 | tf_op jit(solution)/shard_map/pallas_call | solution.py:90
  121.4 7.2 %collective-permute-done.21.refs_10_ = bf16[3,128,128]{2,1,0:T(8,128)(2,1)S(1)} collective-permute-done((bf16[3,128,128]{2,1,0:T(8,128)(2,1)S(1)}, bf16[3,128,128]{2,1,0:T(8,128)(2,1)S(1)}, u32[]{:S(2)}, u32[]{:S(2)}) %collective-permute-start.21) | collective-permute-done | bytes 98336 | tf_op jit(solution)/shard_map/ppermute | solution.py:1018
  128.7 5.5 %shard_map.280 = (bf16[1,4,128,128]{3,2,1,0:T(8,128)(2,1)S(1)}, bf16[1,4,256,128]{3,2,1,0:T(8,128)(2,1)S(1)}, bf16[1,4,256,128]{3,2,1,0:T(8,128)(2,1)S(1)}) custom-call(bf16[1168,128]{1,0:T(8,128)(2,1)S(1)} %get-tuple-element.200.refs_0_, bf16[1168,128]{1,0:T(8,128)(2,1)S(1)} %collective-permute-done.6.refs_1_, ...), custom_call_target="tpu_custom_call" | custom-call | flops 6899999744 | bytes 1024 | tf_op jit(solution)/shard_map/pallas_call | solution.py:90
  135.7 5.9 %shard_map.281 = (bf16[1,4,128,128]{3,2,1,0:T(8,128)(2,1)S(1)}, bf16[1,4,256,128]{3,2,1,0:T(8,128)(2,1)S(1)}, bf16[1,4,256,128]{3,2,1,0:T(8,128)(2,1)S(1)}) custom-call(bf16[1168,128]{1,0:T(8,128)(2,1)S(1)} %get-tuple-element.200.refs_0_, bf16[1168,128]{1,0:T(8,128)(2,1)S(1)} %collective-permute-done.6.refs_1_, ...), custom_call_target="tpu_custom_call" | custom-call | flops 6899999744 | bytes 1024 | tf_op jit(solution)/shard_map/pallas_call | solution.py:90
  147.3 5.5 %shard_map.285 = (bf16[1,4,128,128]{3,2,1,0:T(8,128)(2,1)S(1)}, bf16[1,4,256,128]{3,2,1,0:T(8,128)(2,1)S(1)}, bf16[1,4,256,128]{3,2,1,0:T(8,128)(2,1)S(1)}) custom-call(bf16[1168,128]{1,0:T(8,128)(2,1)S(1)} %get-tuple-element.200.refs_0_, bf16[1168,128]{1,0:T(8,128)(2,1)S(1)} %collective-permute-done.6.refs_1_, ...), custom_call_target="tpu_custom_call" | custom-call | flops 6899999744 | bytes 1024 | tf_op jit(solution)/shard_map/pallas_call | solution.py:90
  168.7 6.0 %collective-permute-done.34.refs_18_ = bf16[384,128]{1,0:T(8,128)(2,1)S(1)} collective-permute-done((bf16[384,128]{1,0:T(8,128)(2,1)S(1)}, bf16[384,128]{1,0:T(8,128)(2,1)S(1)}, u32[]{:S(2)}, u32[]{:S(2)}) %collective-permute-start.34) | collective-permute-done | bytes 98336 | tf_op jit(solution)/shard_map/ppermute | solution.py:1018
  174.8 4.0 %shard_map.287 = (bf16[2,384,256]{2,1,0:T(8,128)(2,1)S(1)}, bf16[2,96,1664]{2,1,0:T(8,128)(2,1)S(1)}, bf16[2,96,1664]{2,1,0:T(8,128)(2,1)S(1)}) custom-call(s32[2]{0:T(128)S(1)} %copy-done.12, f32[512,384]{1,0:T(8,128)S(1)} %copy-done.19, bf16[512,384]{1,0:T(8,128)(2,1)S(1)} %copy-done.23, f32[512,384]{1,0:T(8,128)S(1)} %copy-done.20, ...), custom_call_target="tpu_custom_call" | custom-call | flops 4600000000 | bytes 1024 | tf_op jit(solution)/shard_map/pallas_call | solution.py:90
  183.7 9.3 %shard_map.289 = (bf16[2,96,1920]{2,1,0:T(8,128)(2,1)S(1)}, bf16[2,96,1920]{2,1,0:T(8,128)(2,1)S(1)}) custom-call(bf16[2,384,256]{2,1,0:T(8,128)(2,1)S(1)} %get-tuple-element.213.refs_0_, f32[2,480,256]{2,1,0:T(8,128)S(1)} %copy-done.24, bf16[6,2,1104,256]{3,2,1,0:T(8,128)(2,1)S(1)} %bitcast.35, bf16[2,1104,256]{2,1,0:T(8,128)(2,1)S(1)} %bitcast.27, ...), custom_call_target="tpu_custom_call" | custom-call | flops 14949999616 | bytes 1024 | tf_op jit(solution)/shard_map/pallas_call | solution.py:90
  203.4 3.4 %collective-permute-done.42.refs_3_ = bf16[27,16,128]{2,1,0:T(8,128)(2,1)S(1)} collective-permute-done((bf16[27,16,128]{2,1,0:T(8,128)(2,1)S(1)}, bf16[27,16,128]{2,1,0:T(8,128)(2,1)S(1)}, u32[]{:S(2)}, u32[]{:S(2)}) %collective-permute-start.42) | collective-permute-done | bytes 110624 | tf_op jit(solution)/shard_map/ppermute | solution.py:1018
  206.8 4.2 %collective-permute-done.41.refs_2_ = bf16[27,16,128]{2,1,0:T(8,128)(2,1)S(1)} collective-permute-done((bf16[27,16,128]{2,1,0:T(8,128)(2,1)S(1)}, bf16[27,16,128]{2,1,0:T(8,128)(2,1)S(1)}, u32[]{:S(2)}, u32[]{:S(2)}) %collective-permute-start.41) | collective-permute-done | bytes 110624 | tf_op jit(solution)/shard_map/ppermute | solution.py:1018
  213.6 3.7 %collective-permute-done.48.refs_3_ = bf16[44,16,128]{2,1,0:T(8,128)(2,1)S(1)} collective-permute-done((bf16[44,16,128]{2,1,0:T(8,128)(2,1)S(1)}, bf16[44,16,128]{2,1,0:T(8,128)(2,1)S(1)}, u32[]{:S(2)}, u32[]{:S(2)}) %collective-permute-start.48) | collective-permute-done | bytes 180256 | tf_op jit(solution)/shard_map/ppermute | solution.py:1018
  219.4 3.0 %collective-permute-start.51 = (bf16[22,16,128]{2,1,0:T(8,128)(2,1)S(1)}, bf16[22,16,128]{2,1,0:T(8,128)(2,1)S(1)}, u32[]{:S(2)}, u32[]{:S(2)}) collective-permute-start(bf16[22,16,128]{2,1,0:T(8,128)(2,1)S(1)} %get-tuple-element.248), channel_id=1, source_target_pairs={{0,4},{1,5},{2,6},{3,7},{4,0},{5,1},{6,2},{7,3},{8,12},{9,13},{10,... | collective-permute-start | bytes 270344 | tf_op jit(solution)/shard_map/ppermute | solution.py:1018
  223.7 4.1 %collective-permute-done.49.refs_4_ = bf16[4,27,16,128]{3,2,1,0:T(8,128)(2,1)S(1)} collective-permute-done((bf16[4,27,16,128]{3,2,1,0:T(8,128)(2,1)S(1)}, bf16[4,27,16,128]{3,2,1,0:T(8,128)(2,1)S(1)}, u32[]{:S(2)}, u32[]{:S(2)}) %collective-permute-start.49) | collective-permute-done | bytes 442400 | tf_op jit(solution)/shard_map/ppermute | solution.py:1018
  247.2 7.2 %shard_map.297 = (f32[1,1]{1,0:T(1,128)}, f32[1,1]{1,0:T(1,128)}, f32[1,1]{1,0:T(1,128)}, f32[96,7632]{1,0:T(8,128)}, f32[96,7632]{1,0:T(8,128)}, /*index=5*/f32...) custom-call(f32[8,128]{1,0:T(8,128)S(1)} %add.13.refs_0_, ...), custom_call_target="tpu_custom_call" | custom-call | flops 11500000256 | bytes 1024 | tf_op jit(solution)/shard_map/pallas_call | solution.py:90
  (217 shorter events, 100.5 us)
Async XLA Ops:
  2.7 11.7 %collective-permute-start.1 = (bf16[96,1920]{1,0:T(8,128)(2,1)}, bf16[96,1920]{1,0:T(8,128)(2,1)S(1)}, u32[]{:S(2)}, u32[]{:S(2)}) collective-permute-start(bf16[96,1920]{1,0:T(8,128)(2,1)} %shard_map.271.refs_2_), channel_id=1, source_target_pairs={{0,16},{8,24},{16,0},{24,8},{1,17},{9,25},{17,1},{25,9},{2,18},{10... | collective-permute-start | bytes 1105928 | tf_op jit(solution)/shard_map/ppermute | solution.py:1018
  14.4 13.8 %collective-permute-start.4 = (bf16[128,1536]{1,0:T(8,128)(2,1)}, bf16[128,1536]{1,0:T(8,128)(2,1)S(1)}, u32[]{:S(2)}, u32[]{:S(2)}) collective-permute-start(bf16[128,1536]{1,0:T(8,128)(2,1)} %shard_map.272.refs_2_), channel_id=1, source_target_pairs={{0,16},{8,24},{16,0},{24,8},{1,17},{9,25},{17,1},{25,9},{2,18},{10... | collective-permute-start | bytes 1179656 | tf_op jit(solution)/shard_map/ppermute | solution.py:1018
  31.4 33.4 %collective-permute-start.17 = (bf16[96,4608]{1,0:T(8,128)(2,1)}, bf16[96,4608]{1,0:T(8,128)(2,1)S(1)}, u32[]{:S(2)}, u32[]{:S(2)}) collective-permute-start(bf16[96,4608]{1,0:T(8,128)(2,1)} %shard_map.274.refs_11_), channel_id=1, source_target_pairs={{0,16},{8,24},{16,0},{24,8},{1,17},{9,25},{17,1},{25,9},{2,18},{10... | collective-permute-start | bytes 2654216 | tf_op jit(solution)/shard_map/ppermute | solution.py:1018
  37.1 14.6 %collective-permute-start.6 = (bf16[1168,128]{1,0:T(8,128)(2,1)S(1)}, bf16[1168,128]{1,0:T(8,128)(2,1)S(1)}, u32[]{:S(2)}, u32[]{:S(2)}) collective-permute-start(bf16[1168,128]{1,0:T(8,128)(2,1)S(1)} %get-tuple-element.150), channel_id=1, source_target_pairs={{0,2},{1,3},{2,0},{3,1},{4,6},{5,7},{6,4},{7,5},{8,10},{9,11},{10,... | collective-permute-start | bytes 897032 | tf_op jit(solution)/shard_map/ppermute | solution.py:1018
  38.8 23.7 %collective-permute-start.7 = (bf16[1168,128]{1,0:T(8,128)(2,1)S(1)}, bf16[1168,128]{1,0:T(8,128)(2,1)S(1)}, u32[]{:S(2)}, u32[]{:S(2)}) collective-permute-start(bf16[1168,128]{1,0:T(8,128)(2,1)S(1)} %get-tuple-element.151), channel_id=1, source_target_pairs={{0,4},{1,5},{2,6},{3,7},{4,0},{5,1},{6,2},{7,3},{8,12},{9,13},{10,... | collective-permute-start | bytes 897032 | tf_op jit(solution)/shard_map/ppermute | solution.py:1018
  41.4 22.7 %collective-permute-start.8 = (bf16[1168,128]{1,0:T(8,128)(2,1)S(1)}, bf16[1168,128]{1,0:T(8,128)(2,1)S(1)}, u32[]{:S(2)}, u32[]{:S(2)}) collective-permute-start(bf16[1168,128]{1,0:T(8,128)(2,1)S(1)} %get-tuple-element.152), channel_id=1, source_target_pairs={{0,6},{1,7},{2,4},{3,5},{4,2},{5,3},{6,0},{7,1},{8,14},{9,15},{10,... | collective-permute-start | bytes 897032 | tf_op jit(solution)/shard_map/ppermute | solution.py:1018
  41.6 23.2 %collective-permute-start.9 = (bf16[784,128]{1,0:T(8,128)(2,1)S(1)}, bf16[784,128]{1,0:T(8,128)(2,1)S(1)}, u32[]{:S(2)}, u32[]{:S(2)}) collective-permute-start(bf16[784,128]{1,0:T(8,128)(2,1)S(1)} %slice.12), channel_id=1, source_target_pairs={{0,1},{1,0},{2,3},{3,2},{4,5},{5,4},{6,7},{7,6},{8,9},{9,8},{10,11... | collective-permute-start | bytes 602120 | tf_op jit(solution)/shard_map/ppermute | solution.py:1018
  51.8 13.6 %collective-permute-start.10 = (bf16[784,128]{1,0:T(8,128)(2,1)S(1)}, bf16[784,128]{1,0:T(8,128)(2,1)S(1)}, u32[]{:S(2)}, u32[]{:S(2)}) collective-permute-start(bf16[784,128]{1,0:T(8,128)(2,1)S(1)} %slice.16), channel_id=1, source_target_pairs={{0,1},{1,0},{2,3},{3,2},{4,5},{5,4},{6,7},{7,6},{8,9},{9,8},{10,11... | collective-permute-start | bytes 602120 | tf_op jit(solution)/shard_map/ppermute | solution.py:1018
  64.8 20.7 %collective-permute-start.16 = (bf16[96,4608]{1,0:T(8,128)(2,1)S(1)}, bf16[96,4608]{1,0:T(8,128)(2,1)S(1)}, u32[]{:S(2)}, u32[]{:S(2)}) collective-permute-start(bf16[96,4608]{1,0:T(8,128)(2,1)S(1)} %copy-done.2), channel_id=1, source_target_pairs={{0,8},{8,0},{16,24},{24,16},{1,9},{9,1},{17,25},{25,17},{2,10},{10... | collective-permute-start | bytes 2654216 | tf_op jit(solution)/shard_map/ppermute | solution.py:1018
  64.8 26.4 %collective-permute-start.18 = (bf16[96,4608]{1,0:T(8,128)(2,1)S(1)}, bf16[96,4608]{1,0:T(8,128)(2,1)S(1)}, u32[]{:S(2)}, u32[]{:S(2)}) collective-permute-start(bf16[96,4608]{1,0:T(8,128)(2,1)S(1)} %collective-permute-done.17.refs_13_), channel_id=1, source_target_pairs={{0,8},{8,0},{16,24},{24,16},{1,9},{9,1},{17,25},{25,17},{2,10},{10... | collective-permute-start | bytes 2654216 | tf_op jit(solution)/shard_map/ppermute | solution.py:1018
  117.9 10.8 %collective-permute-start.21 = (bf16[3,128,128]{2,1,0:T(8,128)(2,1)S(1)}, bf16[3,128,128]{2,1,0:T(8,128)(2,1)S(1)}, u32[]{:S(2)}, u32[]{:S(2)}) collective-permute-start(bf16[3,128,128]{2,1,0:T(8,128)(2,1)S(1)} %get-tuple-element.174), channel_id=1, source_target_pairs={{0,4},{1,5},{2,6},{3,7},{4,0},{5,1},{6,2},{7,3},{8,12},{9,13},{10,... | collective-permute-start | bytes 294920 | tf_op jit(solution)/shard_map/ppermute | solution.py:1018
  141.6 13.8 %collective-permute-start.23 = (bf16[1,4,256,128]{3,2,1,0:T(8,128)(2,1)S(1)}, bf16[1,4,256,128]{3,2,1,0:T(8,128)(2,1)S(1)}, u32[]{:S(2)}, u32[]{:S(2)}) collective-permute-start(bf16[1,4,256,128]{3,2,1,0:T(8,128)(2,1)S(1)} %get-tuple-element.182), channel_id=1, source_target_pairs={{0,1},{1,0},{2,3},{3,2},{4,5},{5,4},{6,7},{7,6},{8,9},{9,8},{10,11... | collective-permute-start | bytes 786440 | tf_op jit(solution)/shard_map/ppermute | solution.py:1018
  142.2 21.8 %collective-permute-start.25 = (bf16[216,16,128]{2,1,0:T(8,128)(2,1)S(1)}, bf16[216,16,128]{2,1,0:T(8,128)(2,1)S(1)}, u32[]{:S(2)}, u32[]{:S(2)}) collective-permute-start(bf16[216,16,128]{2,1,0:T(8,128)(2,1)S(1)} %get-tuple-element.185), channel_id=1, source_target_pairs={{0,16},{8,24},{16,0},{24,8},{1,17},{9,25},{17,1},{25,9},{2,18},{10... | collective-permute-start | bytes 2654216 | tf_op jit(solution)/shard_map/ppermute | solution.py:1018
  157.2 10.5 %collective-permute-start.30 = (bf16[384,128]{1,0:T(8,128)(2,1)S(1)}, bf16[384,128]{1,0:T(8,128)(2,1)S(1)}, u32[]{:S(2)}, u32[]{:S(2)}) collective-permute-start(bf16[384,128]{1,0:T(8,128)(2,1)S(1)} %get-tuple-element.198), channel_id=1, source_target_pairs={{0,4},{1,5},{2,6},{3,7},{4,0},{5,1},{6,2},{7,3},{8,12},{9,13},{10,... | collective-permute-start | bytes 294920 | tf_op jit(solution)/shard_map/ppermute | solution.py:1018
  158.1 10.7 %collective-permute-start.31 = (bf16[384,128]{1,0:T(8,128)(2,1)S(1)}, bf16[384,128]{1,0:T(8,128)(2,1)S(1)}, u32[]{:S(2)}, u32[]{:S(2)}) collective-permute-start(bf16[384,128]{1,0:T(8,128)(2,1)S(1)} %get-tuple-element.199), channel_id=1, source_target_pairs={{0,6},{1,7},{2,4},{3,5},{4,2},{5,3},{6,0},{7,1},{8,14},{9,15},{10,... | collective-permute-start | bytes 294920 | tf_op jit(solution)/shard_map/ppermute | solution.py:1018
  162.9 11.8 %collective-permute-start.34 = (bf16[384,128]{1,0:T(8,128)(2,1)S(1)}, bf16[384,128]{1,0:T(8,128)(2,1)S(1)}, u32[]{:S(2)}, u32[]{:S(2)}) collective-permute-start(bf16[384,128]{1,0:T(8,128)(2,1)S(1)} %get-tuple-element.207), channel_id=1, source_target_pairs={{0,4},{1,5},{2,6},{3,7},{4,0},{5,1},{6,2},{7,3},{8,12},{9,13},{10,... | collective-permute-start | bytes 294920 | tf_op jit(solution)/shard_map/ppermute | solution.py:1018
  164.1 10.7 %collective-permute-start.35 = (bf16[384,128]{1,0:T(8,128)(2,1)S(1)}, bf16[384,128]{1,0:T(8,128)(2,1)S(1)}, u32[]{:S(2)}, u32[]{:S(2)}) collective-permute-start(bf16[384,128]{1,0:T(8,128)(2,1)S(1)} %get-tuple-element.208), channel_id=1, source_target_pairs={{0,6},{1,7},{2,4},{3,5},{4,2},{5,3},{6,0},{7,1},{8,14},{9,15},{10,... | collective-permute-start | bytes 294920 | tf_op jit(solution)/shard_map/ppermute | solution.py:1018
  167.6 11.3 %collective-permute-start.36 = (bf16[108,16,128]{2,1,0:T(8,128)(2,1)S(1)}, bf16[108,16,128]{2,1,0:T(8,128)(2,1)S(1)}, u32[]{:S(2)}, u32[]{:S(2)}) collective-permute-start(bf16[108,16,128]{2,1,0:T(8,128)(2,1)S(1)} %get-tuple-element.211), channel_id=1, source_target_pairs={{0,1},{1,0},{2,3},{3,2},{4,5},{5,4},{6,7},{7,6},{8,9},{9,8},{10,11... | collective-permute-start | bytes 1327112 | tf_op jit(solution)/shard_map/ppermute | solution.py:1018
  179.1 13.9 %collective-permute-start.37 = (bf16[27,16,128]{2,1,0:T(8,128)(2,1)S(1)}, bf16[27,16,128]{2,1,0:T(8,128)(2,1)S(1)}, u32[]{:S(2)}, u32[]{:S(2)}) collective-permute-start(bf16[27,16,128]{2,1,0:T(8,128)(2,1)S(1)} %get-tuple-element.222), channel_id=1, source_target_pairs={{0,2},{1,3},{2,0},{3,1},{4,6},{5,7},{6,4},{7,5},{8,10},{9,11},{10,... | collective-permute-start | bytes 331784 | tf_op jit(solution)/shard_map/ppermute | solution.py:1018
  180.8 12.2 %collective-permute-start.38 = (bf16[27,16,128]{2,1,0:T(8,128)(2,1)S(1)}, bf16[27,16,128]{2,1,0:T(8,128)(2,1)S(1)}, u32[]{:S(2)}, u32[]{:S(2)}) collective-permute-start(bf16[27,16,128]{2,1,0:T(8,128)(2,1)S(1)} %get-tuple-element.223), channel_id=1, source_target_pairs={{0,4},{1,5},{2,6},{3,7},{4,0},{5,1},{6,2},{7,3},{8,12},{9,13},{10,... | collective-permute-start | bytes 331784 | tf_op jit(solution)/shard_map/ppermute | solution.py:1018
  181.9 11.1 %collective-permute-start.39 = (bf16[27,16,128]{2,1,0:T(8,128)(2,1)S(1)}, bf16[27,16,128]{2,1,0:T(8,128)(2,1)S(1)}, u32[]{:S(2)}, u32[]{:S(2)}) collective-permute-start(bf16[27,16,128]{2,1,0:T(8,128)(2,1)S(1)} %get-tuple-element.224), channel_id=1, source_target_pairs={{0,6},{1,7},{2,4},{3,5},{4,2},{5,3},{6,0},{7,1},{8,14},{9,15},{10,... | collective-permute-start | bytes 331784 | tf_op jit(solution)/shard_map/ppermute | solution.py:1018
  197.0 14.1 %collective-permute-start.45 = (bf16[88,16,128]{2,1,0:T(8,128)(2,1)S(1)}, bf16[88,16,128]{2,1,0:T(8,128)(2,1)S(1)}, u32[]{:S(2)}, u32[]{:S(2)}) collective-permute-start(bf16[88,16,128]{2,1,0:T(8,128)(2,1)S(1)} %get-tuple-element.232), channel_id=1, source_target_pairs={{0,16},{8,24},{16,0},{24,8},{1,17},{9,25},{17,1},{25,9},{2,18},{10... | collective-permute-start | bytes 1081352 | tf_op jit(solution)/shard_map/ppermute | solution.py:1018
  198.5 12.6 %collective-permute-start.46 = (bf16[88,16,128]{2,1,0:T(8,128)(2,1)S(1)}, bf16[88,16,128]{2,1,0:T(8,128)(2,1)S(1)}, u32[]{:S(2)}, u32[]{:S(2)}) collective-permute-start(bf16[88,16,128]{2,1,0:T(8,128)(2,1)S(1)} %get-tuple-element.234), channel_id=1, source_target_pairs={{0,1},{1,0},{2,3},{3,2},{4,5},{5,4},{6,7},{7,6},{8,9},{9,8},{10,11... | collective-permute-start | bytes 1081352 | tf_op jit(solution)/shard_map/ppermute | solution.py:1018
  217.6 10.3 %collective-permute-start.49 = (bf16[4,27,16,128]{3,2,1,0:T(8,128)(2,1)S(1)}, bf16[4,27,16,128]{3,2,1,0:T(8,128)(2,1)S(1)}, u32[]{:S(2)}, u32[]{:S(2)}) collective-permute-start(bf16[4,27,16,128]{3,2,1,0:T(8,128)(2,1)S(1)} %shard_map.291.refs_3_), channel_id=1, source_target_pairs={{0,1},{1,0},{2,3},{3,2},{4,5},{5,4},{6,7},{7,6},{8,9},{9,8},{10,11... | collective-permute-start | bytes 1327112 | tf_op jit(solution)/shard_map/ppermute | solution.py:1018
  (78 other events, 800.8 us)
